TPU v7x, 256 devices: a whole 4x4x8 slice. The times are simulated.
256 devices in a mesh: grp: 16 (over y, z_lo), head: 4 (over x), tile: 4 (over z_hi, core).
Axes of the slice: x: 4, y: 4, z: 8 (z_hi: 2, z_lo: 4; z = z_hi * 4 + z_lo), core: 2. Of those that a mesh axis runs over, the one named last changes fastest.
Arguments:
- query_states: bfloat16 [16, 4, 8, 24, 4096], P('grp', None, 'tile', 'head'), may hold values from -8 to 8
- key_states: bfloat16 [16, 4, 8, 24, 4096], P('grp', None, 'tile', 'head'), may hold values from -8 to 8
- value_states: bfloat16 [16, 4, 8, 24, 4096], P('grp', None, 'tile', 'head'), may hold values from -6 to 6
- noisy_latent: float32 [16, 4, 8, 24, 64], P('grp', None, 'tile', 'head'), may hold values from -6 to 6
- noise_level: float32 [16], P('grp'), may hold values from 0.5 to 1
- head_weight: bfloat16 [4096, 64], replicated, may hold values from -0.25 to 0.25
- inlet_weight: bfloat16 [3, 3, 3, 16, 384], replicated, may hold values from -0.3125 to 0.3125
- inlet_bias: float32 [384], replicated, may hold values from -3 to 3
- temporal_weight: bfloat16 [3, 384, 768], replicated, may hold values from -0.1875 to 0.1875
- temporal_bias: float32 [768], replicated, may hold values from -3 to 3
- spatial_weight: bfloat16 [3, 3, 384, 192], replicated, may hold values from -0.109375 to 0.109375
- spatial_bias: float32 [192], replicated, may hold values from -3 to 3
Outputs:
- clean_latent: float32 [16, 4, 8, 24, 64], P('grp', None, 'tile', 'head')
- decoded_frames: bfloat16 [16, 8, 32, 96, 192], P('grp', None, 'tile', 'head')
All inputs are finite; a program needn't handle non-finite values.
Results may differ from a plain program's by a relative error of at most 0.015.
Values may be sent and summed in bfloat16 or wider, within the bound.
No kernel may reach another device: no remote copies, remote signals or barrier semaphores. Data moves between devices by JAX's collectives and lax.ppermute only.
A program may use at most 64 MiB of HBM per device.

v0:
```python
import math

import jax
import jax.numpy as jnp
from jax import lax
from jax.sharding import PartitionSpec as P

HD = 128
ZC = 16


def shifted(block, axis, distance):
    devices = range(lax.axis_size(axis))
    route = [(i - distance, i) for i in devices if i - distance in devices]
    return lax.ppermute(block, axis, route)


def with_halo(cells, sides, width):
    for axis, dim in sides:
        count = lax.axis_size(axis)
        ends = count - 1
        head = lax.slice_in_dim(cells, 0, width, axis=dim)
        tail = lax.slice_in_dim(cells, cells.shape[dim] - width, cells.shape[dim], axis=dim)
        cells = jnp.concatenate(
            [
                lax.ppermute(tail, axis, [(i, (i + 1) % count) for i in range(ends)]),
                cells,
                lax.ppermute(head, axis, [((i + 1) % count, i) for i in range(ends)]),
            ],
            axis=dim,
        )
    return cells


def attend(query_heads, key_heads, value_heads, has_prior):
    span_tokens = query_heads.shape[0]
    head_size = query_heads.shape[2]
    block_rows = math.gcd(span_tokens, 512)
    score_scale = 1.0 / math.sqrt(head_size)
    column = jnp.arange(key_heads.shape[0])
    allowed = jnp.logical_or(column >= span_tokens, has_prior)
    penalty = jnp.where(allowed, 0.0, -1e30).astype(jnp.float32)
    blocks = query_heads.reshape((span_tokens // block_rows, block_rows) + query_heads.shape[1:])

    def one_block(query_block):
        scores = (
            jnp.einsum("qhd,khd->hqk", query_block, key_heads, preferred_element_type=jnp.float32)
            * score_scale
        )
        scores = scores + penalty[None, None, :]
        row_max = jnp.max(scores, axis=-1, keepdims=True)
        weights = jnp.exp(scores - row_max)
        row_total = jnp.sum(weights, axis=-1)
        mixture = jnp.einsum(
            "hqk,khd->qhd",
            weights.astype(jnp.bfloat16),
            value_heads,
            preferred_element_type=jnp.float32,
        )
        return (mixture / jnp.transpose(row_total)[:, :, None]).astype(jnp.bfloat16)

    return lax.map(one_block, blocks).reshape(query_heads.shape)


def inlet_filter(padded, filter_weight, filter_bias, frames_out):
    out_rows = padded.shape[1] - 2
    out_cols = padded.shape[2] - 2
    pieces = []
    for frame_shift in range(3):
        for row_shift in range(3):
            for column_shift in range(3):
                pieces.append(
                    padded[
                        frame_shift : frame_shift + frames_out,
                        row_shift : row_shift + out_rows,
                        column_shift : column_shift + out_cols,
                        :,
                    ]
                )
    stacked = jnp.concatenate(pieces, axis=-1)
    channels = filter_weight.shape[-1]
    flat = jnp.dot(
        stacked.reshape(-1, stacked.shape[-1]),
        filter_weight.reshape(-1, channels),
        preferred_element_type=jnp.float32,
    )
    return flat.reshape(frames_out, out_rows, out_cols, channels) + filter_bias


def temporal_filter(features, filter_weight, filter_bias, frames_out):
    stacked = jnp.concatenate(
        [features[offset : offset + frames_out] for offset in range(3)], axis=-1
    )
    channels = features.shape[-1]
    flat = jnp.dot(
        stacked.reshape(-1, 3 * channels),
        filter_weight.reshape(3 * channels, 2 * channels),
        preferred_element_type=jnp.float32,
    )
    flat = (flat + filter_bias).astype(jnp.bfloat16)
    grid_rows = features.shape[1]
    grid_cols = features.shape[2]
    split = flat.reshape(frames_out, grid_rows, grid_cols, 2, channels).transpose(0, 3, 1, 2, 4)
    return split.reshape(2 * frames_out, grid_rows, grid_cols, channels)


def spatial_filter(bordered, filter_weight, filter_bias):
    frames = bordered.shape[0]
    grid_rows = bordered.shape[1]
    grid_cols = bordered.shape[2]
    channels = bordered.shape[3]
    widened = jnp.broadcast_to(
        bordered[:, :, None, :, None, :], (frames, grid_rows, 2, grid_cols, 2, channels)
    )
    widened = widened.reshape(frames, 2 * grid_rows, 2 * grid_cols, channels)[:, 1:-1, 1:-1, :]
    out_rows = 2 * grid_rows - 4
    out_cols = 2 * grid_cols - 4
    outputs = filter_weight.shape[-1]
    accum = jnp.zeros((frames * out_rows * out_cols, outputs), jnp.float32)
    for row_shift in range(3):
        for column_shift in range(3):
            window = widened[
                :, row_shift : row_shift + out_rows, column_shift : column_shift + out_cols, :
            ]
            accum = accum + jnp.dot(
                window.reshape(-1, channels),
                filter_weight[row_shift, column_shift],
                preferred_element_type=jnp.float32,
            )
    return (accum + filter_bias).astype(jnp.bfloat16).reshape(frames, out_rows, out_cols, outputs)


def shards(
    query_states,
    key_states,
    value_states,
    noisy_latent,
    noise_level,
    head_weight,
    inlet_weight,
    inlet_bias,
    temporal_weight,
    temporal_bias,
    spatial_weight,
    spatial_bias,
):
    frames_span = query_states.shape[1]
    patch_rows = query_states.shape[2]
    patch_cols = query_states.shape[3]
    model_width = query_states.shape[4]
    query_flat = query_states.reshape(-1, model_width)
    key_flat = key_states.reshape(-1, model_width)
    value_flat = value_states.reshape(-1, model_width)
    has_prior = lax.axis_index("grp") > 0
    prior_pair = shifted(jnp.stack([key_flat, value_flat]), "grp", 1)
    spread = lax.all_to_all(
        jnp.stack([query_flat, key_flat, value_flat, prior_pair[0], prior_pair[1]]),
        ("head", "tile"),
        split_axis=2,
        concat_axis=1,
        tiled=True,
    )
    query_heads = spread[0]
    key_window = jnp.concatenate([spread[3], spread[1]], axis=0)
    value_window = jnp.concatenate([spread[4], spread[2]], axis=0)
    local_width = query_heads.shape[1]
    head_count = local_width // HD
    attention = attend(
        query_heads.reshape(-1, head_count, HD),
        key_window.reshape(-1, head_count, HD),
        value_window.reshape(-1, head_count, HD),
        has_prior,
    )
    attention = attention.reshape(-1, local_width)
    regrouped = lax.all_to_all(attention, ("head", "tile"), split_axis=0, concat_axis=1, tiled=True)
    velocity = jnp.dot(regrouped, head_weight, preferred_element_type=jnp.float32)
    noisy_flat = noisy_latent.reshape(-1, noisy_latent.shape[-1])
    clean_flat = noisy_flat - noise_level[0] * velocity
    clean_latent = clean_flat.reshape(noisy_latent.shape)
    latent_tile = clean_flat.reshape(frames_span, patch_rows, patch_cols, 2, 2, ZC).transpose(
        0, 1, 3, 2, 4, 5
    )
    latent_tile = latent_tile.reshape(frames_span, 2 * patch_rows, 2 * patch_cols, ZC).astype(
        jnp.bfloat16
    )
    prior_tile = shifted(latent_tile, "grp", 1)
    stacked = jnp.concatenate([prior_tile, latent_tile], axis=0)
    tile_rows = 2 * patch_rows
    tile_cols = 2 * patch_cols
    prior_keep = jnp.where(jnp.arange(frames_span + 2) >= 2, 1.0, has_prior.astype(jnp.float32))
    padded = with_halo(stacked, (("head", 2), ("tile", 1)), 2)
    features = inlet_filter(padded, inlet_weight, inlet_bias, frames_span + 2)
    row_global = lax.axis_index("tile") * tile_rows + jnp.arange(tile_rows + 2) - 1
    column_global = lax.axis_index("head") * tile_cols + jnp.arange(tile_cols + 2) - 1
    row_inside = jnp.logical_and(row_global >= 0, row_global < tile_rows * lax.axis_size("tile"))
    column_inside = jnp.logical_and(
        column_global >= 0, column_global < tile_cols * lax.axis_size("head")
    )
    inside = jnp.logical_and(row_inside[:, None], column_inside[None, :]).astype(jnp.float32)
    features = (features * prior_keep[:, None, None, None] * inside[None, :, :, None]).astype(
        jnp.bfloat16
    )
    doubled = temporal_filter(features, temporal_weight, temporal_bias, frames_span)
    bordered = doubled * inside[None, :, :, None].astype(jnp.bfloat16)
    decoded = spatial_filter(bordered, spatial_weight, spatial_bias)
    return (clean_latent, decoded[None])


def solution(mesh):
    return jax.shard_map(
        shards,
        mesh=mesh,
        in_specs=(
            P("grp", None, "tile", "head", None),
            P("grp", None, "tile", "head", None),
            P("grp", None, "tile", "head", None),
            P("grp", None, "tile", "head", None),
            P("grp"),
            P(),
            P(),
            P(),
            P(),
            P(),
            P(),
            P(),
        ),
        out_specs=(P("grp", None, "tile", "head", None), P("grp", None, "tile", "head", None)),
        check_vma=False,
    )
```

profile of v0, /device:TPU:25, one launch (start us, length us, event | category | flops | bytes accessed | tf_op | source)
XLA Modules:
  0.0 230.6 jit_solution(17378221345705428746)
XLA Ops:
  0.7 1.4 copy.61
  2.6 0.9 pad_maximum_fusion.2
  3.5 3.5 %collective-permute-start = (bf16[2,48,4096]{2,1,0:T(8,128)(2,1)}, bf16[2,48,4096]{2,1,0:T(8,128)(2,1)}, u32[]{:S(2)}, u32[]{:S(2)}) collective-permute-start(bf16[2,48,4096]{2,1,0:T(8,128)(2,1)} %pad_maximum_fusion.2), channel_id=1, source_target_pairs={{0,16},{16,32},{32,48},{48,64},{64,80},{80,96},{96,112},{112,128},... | collective-permute-start | bytes 2359304 | tf_op jit(solution)/shard_map/ppermute | solution.py:15
  7.5 20.1 %collective-permute-done = bf16[2,48,4096]{2,1,0:T(8,128)(2,1)} collective-permute-done((bf16[2,48,4096]{2,1,0:T(8,128)(2,1)}, bf16[2,48,4096]{2,1,0:T(8,128)(2,1)}, u32[]{:S(2)}, u32[]{:S(2)}) %collective-permute-start) | collective-permute-done | bytes 786464 | tf_op jit(solution)/shard_map/ppermute | solution.py:15
  27.5 2.7 %pad_maximum_fusion = bf16[5,48,4096]{2,1,0:T(8,128)(2,1)} fusion(bf16[2,48,4096]{2,1,0:T(8,128)(2,1)} %collective-permute-done, bf16[1,48,4096]{2,1,0:T(8,128)(2,1)S(1)} %stack_reshape.13, bf16[1,48,4096]{2,1,0:T(8,128)(2,1)S(1)} %stack_reshape.12, bf16[1,48,4096]{2,1,0:T(8,128)(2,1)S(1)} %stack_reshape.11), kind=kLoop, calls=%fused_computation.28 | loop fusion | flops 2949120 | bytes 3932160 | tf_op jit(solution)/shard_map/stack | solution.py:157
  30.2 9.6 %copy.63 = bf16[5,48,4096]{1,0,2:T(8,128)(2,1)} copy(bf16[5,48,4096]{2,1,0:T(8,128)(2,1)} %pad_maximum_fusion) | data formatting | bytes 3932160 | tf_op jit(solution)/shard_map/stack | solution.py:157
  39.8 11.1 %reshape.201 = bf16[16,2,30720]{2,1,0:T(2,128)(2,1)} reshape(bf16[4096,5,48]{2,1,0:T(8,128)(2,1)} %bitcast.118) | data formatting | bytes 3932160
  50.9 11.8 %all-to-all-start = ((bf16[16,2,30720]{2,1,0:T(2,128)(2,1)}), bf16[16,2,30720]{2,1,0:T(2,128)(2,1)}, u32[]{:S(2)}, u32[]{:S(2)}) async-start(bf16[16,2,30720]{2,1,0:T(2,128)(2,1)} %reshape.201), calls=%async_computation | async-start | bytes 3932160 | tf_op jit(solution)/shard_map/all_to_all | solution.py:156
  62.7 47.3 %all-to-all-done = bf16[16,2,30720]{2,1,0:T(2,128)(2,1)} async-done(((bf16[16,2,30720]{2,1,0:T(2,128)(2,1)}), bf16[16,2,30720]{2,1,0:T(2,128)(2,1)}, u32[]{:S(2)}, u32[]{:S(2)}) %all-to-all-start) | async-done | bytes 1966112 | tf_op jit(solution)/shard_map/all_to_all | solution.py:156
  110.1 10.8 %reshape.202 = bf16[4096,5,48]{2,1,0:T(8,128)(2,1)} reshape(bf16[16,2,30720]{2,1,0:T(2,128)(2,1)} %all-to-all-done) | data formatting | bytes 3932160
  120.9 8.7 %copy.64 = bf16[5,48,16,256]{3,1,2,0:T(8,128)(2,1)} copy(bf16[5,48,16,256]{1,0,3,2:T(8,128)(2,1)} %bitcast.119) | data formatting | bytes 3932160 | tf_op jit(solution)/shard_map/all_to_all | solution.py:156
  129.5 2.5 %fusion.51 = (bf16[1,16,48,256]{3,2,1,0:T(8,128)(2,1)S(1)}, bf16[1,16,48,256]{3,2,1,0:T(8,128)(2,1)}, bf16[1,16,48,256]{3,2,1,0:T(8,128)(2,1)}, bf16[1,16,48,256...) fusion(bf16[5,16,48,256]{3,2,1,0:T(8,128)(2,1)} %bitcast.120), kind=kLoop, calls=%fused_computation.75 | loop fusion | bytes 3932160 | tf_op jit(solution)/shard_map/slice | solution.py:165
  132.2 1.1 concatenate.57
  133.3 7.0 %pad_maximum_fusion.4 = bf16[1536,2,128]{2,1,0:T(2,128)(2,1)S(1)} fusion(bf16[768,2,128]{2,1,0:T(2,128)(2,1)S(1)} %concatenate.57, bf16[768,2,128]{2,1,0:T(2,128)(2,1)S(1)} %concatenate.56), kind=kLoop, calls=%fused_computation.40 | loop fusion | flops 393216 | bytes 1572864 | tf_op jit(solution)/shard_map/concatenate | solution.py:165
  140.3 1.0 copy.67
  141.5 7.0 %pad_maximum_fusion.3 = bf16[1536,2,128]{2,1,0:T(2,128)(2,1)S(1)} fusion(bf16[768,2,128]{2,1,0:T(2,128)(2,1)S(1)} %concatenate.54, bf16[768,2,128]{2,1,0:T(2,128)(2,1)S(1)} %concatenate.53), kind=kLoop, calls=%fused_computation.39 | loop fusion | flops 393216 | bytes 1572864 | tf_op jit(solution)/shard_map/concatenate | solution.py:164
  148.7 10.3 %while.11 = (s32[]{:T(128)}, bf16[3,256,2,128]{3,2,1,0:T(2,128)(2,1)}, bf16[3,256,2,128]{3,2,1,0:T(2,128)(2,1)S(1)}, bf16[1536,2,128]{2,0,1:T(8,128)(2,1)S(1)}, ...) while((s32[]{:T(128)}, bf16[3,256,2,128]{3,2,1,0:T(2,128)(2,1)}, ...), condition=%wide.region_3.4_spmd.clone, body=%wide.region_0.3_spmd.clone.sunk | while | flops 408292864 | bytes 14964858 | solution.py:62
  148.8 0.7 fusion.87
  150.6 0.7 fusion.89
  151.3 0.8 copy_dynamic-update-slice_fusion.2
  152.2 0.7 fusion.87
  154.0 0.7 fusion.89
  154.8 0.8 copy_dynamic-update-slice_fusion.2
  155.7 0.7 fusion.87
  157.5 0.7 fusion.89
  158.2 0.8 copy_dynamic-update-slice_fusion.2
  159.0 2.0 all_to_all.28
  161.0 7.1 %all-to-all-start.1 = ((bf16[16,48,256]{2,1,0:T(8,128)(2,1)}), bf16[16,48,256]{2,1,0:T(8,128)(2,1)S(1)}, u32[]{:S(2)}, u32[]{:S(2)}) async-start(bf16[16,48,256]{2,1,0:T(8,128)(2,1)} %all_to_all.28), calls=%async_computation.1 | async-start | bytes 786432 | tf_op jit(solution)/shard_map/all_to_all | solution.py:175
  168.8 11.6 %all-to-all-done.1 = bf16[16,48,256]{2,1,0:T(8,128)(2,1)S(1)} async-done(((bf16[16,48,256]{2,1,0:T(8,128)(2,1)}), bf16[16,48,256]{2,1,0:T(8,128)(2,1)S(1)}, u32[]{:S(2)}, u32[]{:S(2)}) %all-to-all-start.1) | async-done | bytes 393248 | tf_op jit(solution)/shard_map/all_to_all | solution.py:175
  180.9 4.9 %collective-permute-start.1 = (bf16[4,4,12,16]{3,2,1,0:T(8,128)(2,1)S(1)}, bf16[4,4,12,16]{3,2,1,0:T(8,128)(2,1)S(1)}, u32[]{:S(2)}, u32[]{:S(2)}) collective-permute-start(bf16[4,4,12,16]{3,2,1,0:T(8,128)(2,1)S(1)} %copy.71), channel_id=1, source_target_pairs={{0,16},{16,32},{32,48},{48,64},{64,80},{80,96},{96,112},{112,128},... | collective-permute-start | bytes 18440 | tf_op jit(solution)/shard_map/ppermute | solution.py:15
  185.9 2.8 %collective-permute-done.1 = bf16[4,4,12,16]{3,2,1,0:T(8,128)(2,1)S(1)} collective-permute-done((bf16[4,4,12,16]{3,2,1,0:T(8,128)(2,1)S(1)}, bf16[4,4,12,16]{3,2,1,0:T(8,128)(2,1)S(1)}, u32[]{:S(2)}, u32[]{:S(2)}) %collective-permute-start.1) | collective-permute-done | bytes 6176 | tf_op jit(solution)/shard_map/ppermute | solution.py:15
  188.7 1.9 collective-permute-start.2
  190.6 1.3 collective-permute-start.3
  192.0 3.1 %collective-permute-done.3 = bf16[8,4,2,16]{3,2,1,0:T(2,128)(2,1)S(1)} collective-permute-done((bf16[8,4,2,16]{3,2,1,0:T(2,128)(2,1)S(1)}, bf16[8,4,2,16]{3,2,1,0:T(2,128)(2,1)S(1)}, u32[]{:S(2)}, u32[]{:S(2)}) %collective-permute-start.3) | collective-permute-done | bytes 2080 | tf_op jit(solution)/shard_map/ppermute | solution.py:28
  195.2 4.8 %collective-permute-start.5 = (bf16[8,2,16,16]{3,2,1,0:T(8,128)(2,1)S(1)}, bf16[8,2,16,16]{3,2,1,0:T(8,128)(2,1)S(1)}, u32[]{:S(2)}, u32[]{:S(2)}) collective-permute-start(bf16[8,2,16,16]{3,2,1,0:T(8,128)(2,1)S(1)} %get-tuple-element.136), channel_id=1, source_target_pairs={{1,0},{2,1},{3,2},{5,4},{6,5},{7,6},{9,8},{10,9},{11,10},{13,12},{... | collective-permute-start | bytes 24584 | tf_op jit(solution)/shard_map/ppermute | solution.py:28
  200.0 4.7 %collective-permute-start.4 = (bf16[8,2,16,16]{3,2,1,0:T(8,128)(2,1)S(1)}, bf16[8,2,16,16]{3,2,1,0:T(8,128)(2,1)S(1)}, u32[]{:S(2)}, u32[]{:S(2)}) collective-permute-start(bf16[8,2,16,16]{3,2,1,0:T(8,128)(2,1)S(1)} %get-tuple-element.137), channel_id=1, source_target_pairs={{0,1},{1,2},{2,3},{4,5},{5,6},{6,7},{8,9},{9,10},{10,11},{12,13},{... | collective-permute-start | bytes 24584 | tf_op jit(solution)/shard_map/ppermute | solution.py:26
  204.7 0.6 copy.84
  205.3 0.7 collective-permute-done.4
  206.1 0.8 fusion.53
  207.0 1.5 fusion.54
  208.5 4.7 %concatenate.64 = bf16[6,6,14,432]{3,2,1,0:T(8,128)(2,1)S(1)} concatenate(bf16[6,6,14,16]{3,2,1,0:T(8,128)(2,1)} %get-tuple-element.144, bf16[6,6,14,16]{3,2,1,0:T(8,128)(2,1)} %get-tuple-element.145, bf16[6,6,14,16]{3,2,1,0:T(8,128)(2,1)} %get-tuple-element.146, bf16[6,6,14,16]{3,2,1,0:T(8,128)(2,1)} %get-tuple-element.115, bf16[6,6,14,16]{3,2,1,0:T(8,128)(2,1)S(1)} %get-tuple-element.114, ...), dimensions={3} | concatenate | bytes 870912 | tf_op jit(solution)/shard_map/concatenate | solution.py:80
  213.3 1.4 fusion.27
  215.6 1.6 fusion.26
  217.2 1.2 reshape.188
  219.3 2.0 fusion.50
  223.0 1.1 copy-done.2
  225.8 0.6 convolution_add_fusion.5
  229.4 1.2 copy.83
  (90 shorter events, 14.1 us)
Async XLA Ops:
  0.6 214.5 %copy-start = (bf16[3,384,768]{2,1,0:T(8,128)(2,1)S(1)}, bf16[3,384,768]{2,1,0:T(8,128)(2,1)}, u32[]{:S(2)}) copy-start(bf16[3,384,768]{2,1,0:T(8,128)(2,1)} %param.22) | copy-start | bytes 5308420
  0.6 1.5 copy-start.5
  2.4 4.7 %copy-start.6 = (bf16[1,4,2,6,4096]{4,2,3,1,0:T(2,128)(2,1)S(1)}, bf16[1,4,2,6,4096]{4,2,3,1,0:T(2,128)(2,1)}, u32[]{:S(2)}) copy-start(bf16[1,4,2,6,4096]{4,2,3,1,0:T(2,128)(2,1)} %param.14) | copy-start | bytes 1179652
  3.5 24.0 %collective-permute-start = (bf16[2,48,4096]{2,1,0:T(8,128)(2,1)}, bf16[2,48,4096]{2,1,0:T(8,128)(2,1)}, u32[]{:S(2)}, u32[]{:S(2)}) collective-permute-start(bf16[2,48,4096]{2,1,0:T(8,128)(2,1)} %pad_maximum_fusion.2), channel_id=1, source_target_pairs={{0,16},{16,32},{32,48},{48,64},{64,80},{80,96},{96,112},{112,128},... | collective-permute-start | bytes 2359304 | tf_op jit(solution)/shard_map/ppermute | solution.py:15
  50.9 59.1 %all-to-all-start = ((bf16[16,2,30720]{2,1,0:T(2,128)(2,1)}), bf16[16,2,30720]{2,1,0:T(2,128)(2,1)}, u32[]{:S(2)}, u32[]{:S(2)}) async-start(bf16[16,2,30720]{2,1,0:T(2,128)(2,1)} %reshape.201), calls=%async_computation | async-start | bytes 3932160 | tf_op jit(solution)/shard_map/all_to_all | solution.py:156
  140.3 1.0 copy-start.1
  149.5 1.1 copy-start.3
  152.9 1.1 copy-start.3
  156.3 1.1 copy-start.3
  159.0 9.8 %copy-start.7 = (f32[1,4,2,6,64]{4,2,3,1,0:T(2,128)S(1)}, f32[1,4,2,6,64]{4,2,3,1,0:T(2,128)}, u32[]{:S(2)}) copy-start(f32[1,4,2,6,64]{4,2,3,1,0:T(2,128)} %param.17) | copy-start | bytes 36868
  159.0 21.5 %copy-start.4 = (bf16[4096,64]{0,1:T(8,128)(2,1)S(1)}, bf16[4096,64]{0,1:T(8,128)(2,1)}, u32[]{:S(2)}) copy-start(bf16[4096,64]{0,1:T(8,128)(2,1)} %param.19) | copy-start | bytes 1572868
  161.0 19.4 %all-to-all-start.1 = ((bf16[16,48,256]{2,1,0:T(8,128)(2,1)}), bf16[16,48,256]{2,1,0:T(8,128)(2,1)S(1)}, u32[]{:S(2)}, u32[]{:S(2)}) async-start(bf16[16,48,256]{2,1,0:T(8,128)(2,1)} %all_to_all.28), calls=%async_computation.1 | async-start | bytes 786432 | tf_op jit(solution)/shard_map/all_to_all | solution.py:175
  180.9 7.7 %collective-permute-start.1 = (bf16[4,4,12,16]{3,2,1,0:T(8,128)(2,1)S(1)}, bf16[4,4,12,16]{3,2,1,0:T(8,128)(2,1)S(1)}, u32[]{:S(2)}, u32[]{:S(2)}) collective-permute-start(bf16[4,4,12,16]{3,2,1,0:T(8,128)(2,1)S(1)} %copy.71), channel_id=1, source_target_pairs={{0,16},{16,32},{32,48},{48,64},{64,80},{80,96},{96,112},{112,128},... | collective-permute-start | bytes 18440 | tf_op jit(solution)/shard_map/ppermute | solution.py:15
  188.7 3.2 %collective-permute-start.2 = (bf16[8,4,2,16]{3,2,1,0:T(2,128)(2,1)S(1)}, bf16[8,4,2,16]{3,2,1,0:T(2,128)(2,1)S(1)}, u32[]{:S(2)}, u32[]{:S(2)}) collective-permute-start(bf16[8,4,2,16]{3,2,1,0:T(2,128)(2,1)S(1)} %get-tuple-element.138), channel_id=1, source_target_pairs={{0,4},{4,8},{8,12},{1,5},{5,9},{9,13},{2,6},{6,10},{10,14},{3,7},{... | collective-permute-start | bytes 6152 | tf_op jit(solution)/shard_map/ppermute | solution.py:26
  190.6 4.5 %collective-permute-start.3 = (bf16[8,4,2,16]{3,2,1,0:T(2,128)(2,1)S(1)}, bf16[8,4,2,16]{3,2,1,0:T(2,128)(2,1)S(1)}, u32[]{:S(2)}, u32[]{:S(2)}) collective-permute-start(bf16[8,4,2,16]{3,2,1,0:T(2,128)(2,1)S(1)} %get-tuple-element.139), channel_id=1, source_target_pairs={{4,0},{8,4},{12,8},{5,1},{9,5},{13,9},{6,2},{10,6},{14,10},{7,3},{... | collective-permute-start | bytes 6152 | tf_op jit(solution)/shard_map/ppermute | solution.py:28
  195.2 10.1 %collective-permute-start.5 = (bf16[8,2,16,16]{3,2,1,0:T(8,128)(2,1)S(1)}, bf16[8,2,16,16]{3,2,1,0:T(8,128)(2,1)S(1)}, u32[]{:S(2)}, u32[]{:S(2)}) collective-permute-start(bf16[8,2,16,16]{3,2,1,0:T(8,128)(2,1)S(1)} %get-tuple-element.136), channel_id=1, source_target_pairs={{1,0},{2,1},{3,2},{5,4},{6,5},{7,6},{9,8},{10,9},{11,10},{13,12},{... | collective-permute-start | bytes 24584 | tf_op jit(solution)/shard_map/ppermute | solution.py:28
  200.0 6.0 %collective-permute-start.4 = (bf16[8,2,16,16]{3,2,1,0:T(8,128)(2,1)S(1)}, bf16[8,2,16,16]{3,2,1,0:T(8,128)(2,1)S(1)}, u32[]{:S(2)}, u32[]{:S(2)}) collective-permute-start(bf16[8,2,16,16]{3,2,1,0:T(8,128)(2,1)S(1)} %get-tuple-element.137), channel_id=1, source_target_pairs={{0,1},{1,2},{2,3},{4,5},{5,6},{6,7},{8,9},{9,10},{10,11},{12,13},{... | collective-permute-start | bytes 24584 | tf_op jit(solution)/shard_map/ppermute | solution.py:26
  208.5 4.8 %copy-start.10 = (f32[384]{0:T(512)S(1)}, f32[384]{0:T(512)}, u32[]{:S(2)}) copy-start(f32[384]{0:T(512)} %param.21) | copy-start | bytes 4612
  214.9 0.7 copy-start.9
  222.8 1.3 copy-start.2
  228.2 0.7 copy-start.8
where the time goes:
time: 233 us; the launch traced here: 231 us
  waiting for transfers between devices  85.6 us (37%)
  local copies, waits for them, and re-layouts  70.4 us (30%)
  starting transfers between devices  39.9 us (17%)
  other arithmetic  20.1 us (9%)
  matrix products  12.6 us (5%)
    all_to_all x1, waiting for transfers between devices, shards(): lax.all_to_all(jnp.stack([query_flat, key_flat, value_flat, prior_pair[0]...  47.3 us
    unnamed x30, local copies, waits for them, and re-layouts  27.1 us
    ppermute x2, waiting for transfers between devices, shifted(): return lax.ppermute(block, axis, route)  22.9 us
    all_to_all x1, starting transfers between devices, shards(): lax.all_to_all(jnp.stack([query_flat, key_flat, value_flat, prior_pair[0]...  11.8 us
    all_to_all x1, waiting for transfers between devices, shards(): lax.all_to_all(attention, ('head', 'tile'), split_axis=0, concat_axis=1,...  11.6 us
    another operation x4, local copies, waits for them, and re-layouts, shards(): jnp.stack([query_flat, key_flat, value_flat, prior_pair[0], prior_pair[1]])  10 us
    all_to_all x1, local copies, waits for them, and re-layouts, shards(): lax.all_to_all(jnp.stack([query_flat, key_flat, value_flat, prior_pair[0]...  8.68 us
    ppermute x2, starting transfers between devices, shifted(): return lax.ppermute(block, axis, route)  8.42 us
  transfers between devices with their start and end apart: 8, of which 6 were waited for; matrix products, arithmetic and copies ran while one was open for 0% of the time, Pallas kernels for 0%

commit v1 on v0

--- a/solution.py
+++ b/solution.py
@@ -3,10 +3,185 @@
 import jax
 import jax.numpy as jnp
 from jax import lax
+from jax.experimental import pallas as pl
+from jax.experimental.pallas import tpu as pltpu
 from jax.sharding import PartitionSpec as P
 
 HD = 128
 ZC = 16
+HEADS = 32
+OWN = 48
+LAT = 64
+ROWS = 2 * OWN + OWN // 2
+AXES = ("grp", "head", "tile")
+VMEM_BYTES = 48 * 1024 * 1024
+
+
+def device_id(y, pair, low, x, high, core):
+    return ((y * 4 + 2 * pair + low) * 4 + x) * 4 + 2 * high + core
+
+
+def pair_groups():
+    groups = []
+    for y in range(4):
+        for pair in range(2):
+            members = []
+            for a in range(2):
+                for x in range(4):
+                    for b in range(2):
+                        for core in range(2):
+                            low = a if pair == 0 else 1 - a
+                            high = b if pair == 0 or a == 1 else 1 - b
+                            members.append(device_id(y, pair, low, x, high, core))
+            groups.append(members)
+    return groups
+
+
+def prior_route(groups):
+    return [(groups[g][k], groups[g + 1][k]) for g in range(len(groups) - 1) for k in range(HEADS)]
+
+
+def prep_kernel(query_ref, key_ref, value_ref, weight_ref, out_ref):
+    for h in range(HEADS):
+        lanes = slice(h * HD, (h + 1) * HD)
+        out_ref[h, 0:OWN, :] = query_ref[:, lanes]
+        out_ref[h, OWN : 2 * OWN, :] = key_ref[:, lanes]
+        folded = jnp.dot(value_ref[:, lanes], weight_ref[lanes, :], preferred_element_type=jnp.float32)
+        packed = jnp.concatenate([folded[: OWN // 2], folded[OWN // 2 :]], axis=1)
+        out_ref[h, 2 * OWN : ROWS, :] = packed.astype(jnp.bfloat16)
+
+
+def prep(query, key, value, weight):
+    return pl.pallas_call(
+        prep_kernel,
+        out_shape=jax.ShapeDtypeStruct((HEADS, ROWS, HD), jnp.bfloat16),
+        in_specs=[pl.BlockSpec(memory_space=pltpu.VMEM)] * 4,
+        out_specs=pl.BlockSpec(memory_space=pltpu.VMEM),
+        compiler_params=pltpu.CompilerParams(vmem_limit_bytes=VMEM_BYTES),
+    )(query, key, value, weight)
+
+
+def spread_values(packed, target):
+    lower = packed[:, :, :LAT].astype(jnp.float32)
+    upper = packed[:, :, LAT:].astype(jnp.float32)
+    both = jnp.concatenate([lower, upper], axis=1).reshape(16 * OWN, LAT)
+    ones = jnp.ones((16 * OWN, HD - LAT), jnp.float32)
+    target[...] = jnp.concatenate([both, ones], axis=1).astype(jnp.bfloat16)
+
+
+def fold_scale():
+    return (1.0 / math.sqrt(HD)) * math.log2(math.e)
+
+
+def scores_of(query, keys):
+    dims = (((1,), (1,)), ((), ()))
+    return lax.dot_general(query, keys, dims, preferred_element_type=jnp.float32)
+
+
+def pack_result(mixed, out_ref, start, blocks):
+    velocity = mixed[:, :LAT] / mixed[:, LAT : 2 * LAT]
+    velocity = velocity.reshape(blocks, OWN, LAT)
+    packed = jnp.concatenate([velocity[:, : OWN // 2], velocity[:, OWN // 2 :]], axis=2)
+    out_ref[pl.ds(start, blocks)] = packed.astype(out_ref.dtype)
+
+
+QB = 4
+
+
+def attend_here_kernel(place_ref, recv_ref, out_ref, max_ref, mix_ref, early_v, late_v):
+    early = place_ref[0]
+    late = 16 - early
+    spread_values(recv_ref[pl.ds(early, 16), 2 * OWN :, :], early_v)
+    spread_values(recv_ref[pl.ds(late, 16), 2 * OWN :, :], late_v)
+    early_k = recv_ref[pl.ds(early, 16), OWN : 2 * OWN, :].reshape(16 * OWN, HD)
+    late_k = recv_ref[pl.ds(late, 16), OWN : 2 * OWN, :].reshape(16 * OWN, HD)
+    scale = fold_scale()
+
+    def late_block(i, carry):
+        query = recv_ref[pl.ds(late + i * QB, QB), :OWN, :].reshape(QB * OWN, HD)
+        here = scores_of(query, late_k) * scale
+        before = scores_of(query, early_k) * scale
+        top = jnp.maximum(
+            jnp.max(here, axis=1, keepdims=True), jnp.max(before, axis=1, keepdims=True)
+        )
+        here = jnp.exp2(here - top).astype(jnp.bfloat16)
+        before = jnp.exp2(before - top).astype(jnp.bfloat16)
+        mixed = jnp.dot(here, late_v[...], preferred_element_type=jnp.float32)
+        mixed += jnp.dot(before, early_v[...], preferred_element_type=jnp.float32)
+        pack_result(mixed, out_ref, i * QB, QB)
+        return carry
+
+    lax.fori_loop(0, 16 // QB, late_block, 0)
+
+    def early_block(i, carry):
+        query = recv_ref[pl.ds(early + i * QB, QB), :OWN, :].reshape(QB * OWN, HD)
+        here = scores_of(query, early_k) * scale
+        top = jnp.max(here, axis=1, keepdims=True)
+        here = jnp.exp2(here - top).astype(jnp.bfloat16)
+        mix_ref[pl.ds(i * QB * OWN, QB * OWN), :] = jnp.dot(
+            here, early_v[...], preferred_element_type=jnp.float32
+        )
+        max_ref[pl.ds(i * QB * OWN, QB * OWN), :] = jnp.broadcast_to(top, (QB * OWN, HD))
+        return carry
+
+    lax.fori_loop(0, 16 // QB, early_block, 0)
+
+
+def attend_here(place, recv):
+    vmem = pl.BlockSpec(memory_space=pltpu.VMEM)
+    tokens = 16 * OWN
+    return pl.pallas_call(
+        attend_here_kernel,
+        out_shape=(
+            jax.ShapeDtypeStruct((16, OWN // 2, HD), jnp.bfloat16),
+            jax.ShapeDtypeStruct((tokens, HD), jnp.float32),
+            jax.ShapeDtypeStruct((tokens, HD), jnp.float32),
+        ),
+        in_specs=[pl.BlockSpec(memory_space=pltpu.SMEM), vmem],
+        out_specs=(vmem, vmem, vmem),
+        scratch_shapes=[pltpu.VMEM((tokens, HD), jnp.bfloat16)] * 2,
+        compiler_params=pltpu.CompilerParams(vmem_limit_bytes=VMEM_BYTES),
+        cost_estimate=pl.CostEstimate(
+            flops=4 * 3 * tokens * tokens * HD, bytes_accessed=4 << 20, transcendentals=3 * tokens * tokens
+        ),
+    )(place, recv)
+
+
+def attend_prior_kernel(place_ref, recv_ref, prior_ref, late_ref, max_ref, mix_ref, out_ref, prior_v):
+    early = place_ref[0]
+    late = 16 - early
+    penalty = jnp.where(place_ref[1] > 0, 0.0, -1e30).astype(jnp.float32)
+    spread_values(prior_ref[:, OWN:, :], prior_v)
+    prior_k = prior_ref[:, :OWN, :].reshape(16 * OWN, HD)
+    scale = fold_scale()
+    out_ref[pl.ds(late, 16)] = late_ref[...]
+
+    def block(i, carry):
+        rows = pl.ds(i * QB * OWN, QB * OWN)
+        query = recv_ref[pl.ds(early + i * QB, QB), :OWN, :].reshape(QB * OWN, HD)
+        before = scores_of(query, prior_k) * scale + penalty
+        old = max_ref[rows, :]
+        top = jnp.maximum(old[:, :1], jnp.max(before, axis=1, keepdims=True))
+        before = jnp.exp2(before - top).astype(jnp.bfloat16)
+        mixed = jnp.dot(before, prior_v[...], preferred_element_type=jnp.float32)
+        mixed += mix_ref[rows, :] * jnp.exp2(old - top)
+        pack_result(mixed, out_ref, early + i * QB, QB)
+        return carry
+
+    lax.fori_loop(0, 16 // QB, block, 0)
+
+
+def attend_prior(place, recv, prior, late, top, mix):
+    vmem = pl.BlockSpec(memory_space=pltpu.VMEM)
+    tokens = 16 * OWN
+    return pl.pallas_call(
+        attend_prior_kernel,
+        out_shape=jax.ShapeDtypeStruct((HEADS, OWN // 2, HD), jnp.bfloat16),
+        in_specs=[pl.BlockSpec(memory_space=pltpu.SMEM)] + [vmem] * 5,
+        out_specs=vmem,
+        scratch_shapes=[pltpu.VMEM((tokens, HD), jnp.bfloat16)],
+        compiler_params=pltpu.CompilerParams(vmem_limit_bytes=VMEM_BYTES),
+    )(place, recv, prior, late, top, mix)
 
 
 def shifted(block, axis, distance):
@@ -30,36 +205,6 @@
             axis=dim,
         )
     return cells
-
-
-def attend(query_heads, key_heads, value_heads, has_prior):
-    span_tokens = query_heads.shape[0]
-    head_size = query_heads.shape[2]
-    block_rows = math.gcd(span_tokens, 512)
-    score_scale = 1.0 / math.sqrt(head_size)
-    column = jnp.arange(key_heads.shape[0])
-    allowed = jnp.logical_or(column >= span_tokens, has_prior)
-    penalty = jnp.where(allowed, 0.0, -1e30).astype(jnp.float32)
-    blocks = query_heads.reshape((span_tokens // block_rows, block_rows) + query_heads.shape[1:])
-
-    def one_block(query_block):
-        scores = (
-            jnp.einsum("qhd,khd->hqk", query_block, key_heads, preferred_element_type=jnp.float32)
-            * score_scale
-        )
-        scores = scores + penalty[None, None, :]
-        row_max = jnp.max(scores, axis=-1, keepdims=True)
-        weights = jnp.exp(scores - row_max)
-        row_total = jnp.sum(weights, axis=-1)
-        mixture = jnp.einsum(
-            "hqk,khd->qhd",
-            weights.astype(jnp.bfloat16),
-            value_heads,
-            preferred_element_type=jnp.float32,
-        )
-        return (mixture / jnp.transpose(row_total)[:, :, None]).astype(jnp.bfloat16)
-
-    return lax.map(one_block, blocks).reshape(query_heads.shape)
 
 
 def inlet_filter(padded, filter_weight, filter_bias, frames_out):
@@ -148,32 +293,27 @@
     patch_rows = query_states.shape[2]
     patch_cols = query_states.shape[3]
     model_width = query_states.shape[4]
-    query_flat = query_states.reshape(-1, model_width)
-    key_flat = key_states.reshape(-1, model_width)
-    value_flat = value_states.reshape(-1, model_width)
-    has_prior = lax.axis_index("grp") > 0
-    prior_pair = shifted(jnp.stack([key_flat, value_flat]), "grp", 1)
-    spread = lax.all_to_all(
-        jnp.stack([query_flat, key_flat, value_flat, prior_pair[0], prior_pair[1]]),
-        ("head", "tile"),
-        split_axis=2,
-        concat_axis=1,
-        tiled=True,
-    )
-    query_heads = spread[0]
-    key_window = jnp.concatenate([spread[3], spread[1]], axis=0)
-    value_window = jnp.concatenate([spread[4], spread[2]], axis=0)
-    local_width = query_heads.shape[1]
-    head_count = local_width // HD
-    attention = attend(
-        query_heads.reshape(-1, head_count, HD),
-        key_window.reshape(-1, head_count, HD),
-        value_window.reshape(-1, head_count, HD),
-        has_prior,
-    )
-    attention = attention.reshape(-1, local_width)
-    regrouped = lax.all_to_all(attention, ("head", "tile"), split_axis=0, concat_axis=1, tiled=True)
-    velocity = jnp.dot(regrouped, head_weight, preferred_element_type=jnp.float32)
+    groups = pair_groups()
+    grp = lax.axis_index("grp")
+    pair = (grp // 2) % 2
+    has_prior = grp > 0
+    early = 16 * pair
+    pair_has_prior = (grp // 2 > 0).astype(jnp.int32)
+    place = jnp.stack([early.astype(jnp.int32), pair_has_prior])
+    sent = prep(
+        query_states.reshape(-1, model_width),
+        key_states.reshape(-1, model_width),
+        value_states.reshape(-1, model_width),
+        head_weight,
+    )
+    recv = lax.all_to_all(sent, AXES, 0, 0, tiled=True, axis_index_groups=groups)
+    late_kv = lax.dynamic_slice(recv, (16 - early, OWN, 0), (16, ROWS - OWN, HD))
+    prior = lax.ppermute(late_kv, AXES, prior_route(groups))
+    late, top, mix = attend_here(place, recv)
+    partial = attend_prior(place, recv, prior, late, top, mix)
+    back = lax.all_to_all(partial, AXES, 0, 0, tiled=True, axis_index_groups=groups)
+    packed = jnp.sum(back.astype(jnp.float32), axis=0)
+    velocity = jnp.concatenate([packed[:, :LAT], packed[:, LAT:]], axis=0)
     noisy_flat = noisy_latent.reshape(-1, noisy_latent.shape[-1])
     clean_flat = noisy_flat - noise_level[0] * velocity
     clean_latent = clean_flat.reshape(noisy_latent.shape)

time: 233 us -> 133 us (0.57)
  the two profiles are of different devices: /device:TPU:25 before, /device:TPU:17 now
where the time goes in v1:
time: 133 us; the launch traced here: 132 us
  waiting for transfers between devices  52.8 us (40%)
  starting transfers between devices  33.7 us (25%)
  local copies, waits for them, and re-layouts  23.9 us (18%)
  Pallas kernels  11.4 us (9%)
  matrix products  7.42 us (6%)
  between operations  1.88 us (1%)
    all_to_all x1, waiting for transfers between devices, shards(): lax.all_to_all(sent, AXES, 0, 0, tiled=True, axis_index_groups=groups)  28.9 us
    all_to_all x1, starting transfers between devices, shards(): lax.all_to_all(sent, AXES, 0, 0, tiled=True, axis_index_groups=groups)  11.8 us
    all_to_all x1, waiting for transfers between devices, shards(): lax.all_to_all(partial, AXES, 0, 0, tiled=True, axis_index_groups=groups)  10.8 us
    unnamed x28, local copies, waits for them, and re-layouts  8.63 us
    ppermute x2, starting transfers between devices, with_halo(): lax.ppermute(head, axis, [((i + 1) % count, i) for i in range(ends)])  6.53 us
    ppermute x2, starting transfers between devices, with_halo(): lax.ppermute(tail, axis, [(i, (i + 1) % count) for i in range(ends)])  6.53 us
    pallas_call x1, Pallas kernels, attend_here(): pl.pallas_call(attend_here_kernel, out_shape=(jax.ShapeDtypeStruct((16, O...  6.11 us
    ppermute x1, waiting for transfers between devices, shifted(): return lax.ppermute(block, axis, route)  5.7 us
  transfers between devices with their start and end apart: 8, of which 6 were waited for; matrix products, arithmetic and copies ran while one was open for 1% of the time, Pallas kernels for 5%

profile of v1, /device:TPU:17, one launch (start us, length us, event | category | flops | bytes accessed | tf_op | source)
XLA Modules:
  0.0 131.9 jit_solution(12930749131490780623)
XLA Ops:
  0.7 1.4 %copy.32 = bf16[1,4,2,6,4096]{4,3,2,1,0:T(8,128)(2,1)S(1)} copy(bf16[1,4,2,6,4096]{4,2,3,1,0:T(2,128)(2,1)} %param.12) | data formatting | bytes 786432 | tf_op args[0]
  2.2 0.2 copy.33
  2.4 0.9 reshape.179.key_ref
  3.3 0.2 copy.34
  3.5 0.9 reshape.180.value_ref
  4.4 1.5 %copy.35.weight_ref = bf16[4096,64]{1,0:T(8,128)(2,1)S(1)} copy(bf16[4096,64]{0,1:T(8,128)(2,1)} %param.17) | data formatting | bytes 1048576 | tf_op args[5]
  6.0 1.0 copy-done.2
  7.0 1.0 copy-done.3
  8.0 0.6 shard_map.131
  8.6 1.0 copy-done.1
  9.5 11.8 %all-to-all-start = ((bf16[32,120,128]{2,1,0:T(8,128)(2,1)}), bf16[32,120,128]{2,1,0:T(8,128)(2,1)S(1)}, u32[]{:S(2)}, u32[]{:S(2)}) async-start(bf16[32,120,128]{2,1,0:T(8,128)(2,1)} %copy-done.1), calls=%async_computation | async-start | bytes 1966080 | tf_op jit(solution)/shard_map/all_to_all | solution.py:309
  21.3 28.9 %all-to-all-done.recv_ref = bf16[32,120,128]{2,1,0:T(8,128)(2,1)S(1)} async-done(((bf16[32,120,128]{2,1,0:T(8,128)(2,1)}), bf16[32,120,128]{2,1,0:T(8,128)(2,1)S(1)}, u32[]{:S(2)}, u32[]{:S(2)}) %all-to-all-start) | async-done | bytes 983072 | tf_op jit(solution)/shard_map/all_to_all | solution.py:309
  50.2 1.9 %collective-permute-start = (bf16[16,72,128]{2,1,0:T(8,128)(2,1)S(1)}, bf16[16,72,128]{2,1,0:T(8,128)(2,1)S(1)}, u32[]{:S(2)}, u32[]{:S(2)}) collective-permute-start(bf16[16,72,128]{2,1,0:T(8,128)(2,1)S(1)} %constant_dynamic-slice_fusion), channel_id=1, source_target_pairs={{0,50},{1,51},{2,48},{3,49},{4,54},{5,55},{6,52},{7,53},{8,58},{9,... | collective-permute-start | bytes 884744 | tf_op jit(solution)/shard_map/ppermute | solution.py:311
  52.2 6.1 %shard_map.132 = (bf16[16,24,128]{2,1,0:T(8,128)(2,1)S(1)}, f32[768,128]{1,0:T(8,128)S(1)}, f32[768,128]{1,0:T(8,128)S(1)}) custom-call(s32[2]{0:T(128)S(1)} %pad_add_fusion.place_ref, bf16[32,120,128]{2,1,0:T(8,128)(2,1)S(1)} %all-to-all-done.recv_ref), custom_call_target="tpu_custom_call" | custom-call | flops 905969664 | bytes 4194304 | tf_op jit(solution)/shard_map/pallas_call | solution.py:133
  58.3 3.8 %collective-permute-done.prior_ref = bf16[16,72,128]{2,1,0:T(8,128)(2,1)S(1)} collective-permute-done((bf16[16,72,128]{2,1,0:T(8,128)(2,1)S(1)}, bf16[16,72,128]{2,1,0:T(8,128)(2,1)S(1)}, u32[]{:S(2)}, u32[]{:S(2)}) %collective-permute-start) | collective-permute-done | bytes 294944 | tf_op jit(solution)/shard_map/ppermute | solution.py:311
  62.2 4.7 %shard_map.133 = bf16[32,24,128]{2,1,0:T(8,128)(2,1)} custom-call(s32[2]{0:T(128)S(1)} %pad_add_fusion.place_ref, bf16[32,120,128]{2,1,0:T(8,128)(2,1)S(1)} %all-to-all-done.recv_ref, bf16[16,72,128]{2,1,0:T(8,128)(2,1)S(1)} %collective-permute-done.prior_ref, bf16[16,24,128]{2,1,0:T(8,128)(2,1)S(1)} %get-tuple-element.5.late_ref, ...), custom_call_target="tpu_custom_call" | custom-call | tf_op jit(solution)/shard_map/pallas_call | solution.py:177
  66.8 5.0 %all-to-all-start.1 = ((bf16[32,24,128]{2,1,0:T(8,128)(2,1)}), bf16[32,24,128]{2,1,0:T(8,128)(2,1)S(1)}, u32[]{:S(2)}, u32[]{:S(2)}) async-start(bf16[32,24,128]{2,1,0:T(8,128)(2,1)} %shard_map.133), calls=%async_computation.1 | async-start | bytes 393216 | tf_op jit(solution)/shard_map/all_to_all | solution.py:314
  72.7 10.8 %all-to-all-done.1 = bf16[32,24,128]{2,1,0:T(8,128)(2,1)S(1)} async-done(((bf16[32,24,128]{2,1,0:T(8,128)(2,1)}), bf16[32,24,128]{2,1,0:T(8,128)(2,1)S(1)}, u32[]{:S(2)}, u32[]{:S(2)}) %all-to-all-start.1) | async-done | bytes 196640 | tf_op jit(solution)/shard_map/all_to_all | solution.py:314
  83.9 1.9 %collective-permute-start.1 = (bf16[4,4,12,16]{3,2,1,0:T(8,128)(2,1)S(1)}, bf16[4,4,12,16]{3,2,1,0:T(8,128)(2,1)S(1)}, u32[]{:S(2)}, u32[]{:S(2)}) collective-permute-start(bf16[4,4,12,16]{3,2,1,0:T(8,128)(2,1)S(1)} %copy.39), channel_id=1, source_target_pairs={{0,16},{16,32},{32,48},{48,64},{64,80},{80,96},{96,112},{112,128},... | collective-permute-start | bytes 18440 | tf_op jit(solution)/shard_map/ppermute | solution.py:190
  85.9 5.7 %collective-permute-done.1 = bf16[4,4,12,16]{3,2,1,0:T(8,128)(2,1)S(1)} collective-permute-done((bf16[4,4,12,16]{3,2,1,0:T(8,128)(2,1)S(1)}, bf16[4,4,12,16]{3,2,1,0:T(8,128)(2,1)S(1)}, u32[]{:S(2)}, u32[]{:S(2)}) %collective-permute-start.1) | collective-permute-done | bytes 6176 | tf_op jit(solution)/shard_map/ppermute | solution.py:190
  91.6 2.1 %collective-permute-start.2 = (bf16[8,4,2,16]{3,2,1,0:T(2,128)(2,1)S(1)}, bf16[8,4,2,16]{3,2,1,0:T(2,128)(2,1)S(1)}, u32[]{:S(2)}, u32[]{:S(2)}) collective-permute-start(bf16[8,4,2,16]{3,2,1,0:T(2,128)(2,1)S(1)} %get-tuple-element.57), channel_id=1, source_target_pairs={{0,4},{4,8},{8,12},{1,5},{5,9},{9,13},{2,6},{6,10},{10,14},{3,7},{... | collective-permute-start | bytes 6152 | tf_op jit(solution)/shard_map/ppermute | solution.py:201
  93.8 1.3 collective-permute-start.3
  95.1 3.1 %collective-permute-done.3 = bf16[8,4,2,16]{3,2,1,0:T(2,128)(2,1)S(1)} collective-permute-done((bf16[8,4,2,16]{3,2,1,0:T(2,128)(2,1)S(1)}, bf16[8,4,2,16]{3,2,1,0:T(2,128)(2,1)S(1)}, u32[]{:S(2)}, u32[]{:S(2)}) %collective-permute-start.3) | collective-permute-done | bytes 2080 | tf_op jit(solution)/shard_map/ppermute | solution.py:203
  98.4 5.2 %collective-permute-start.5 = (bf16[8,2,16,16]{3,2,1,0:T(8,128)(2,1)S(1)}, bf16[8,2,16,16]{3,2,1,0:T(8,128)(2,1)S(1)}, u32[]{:S(2)}, u32[]{:S(2)}) collective-permute-start(bf16[8,2,16,16]{3,2,1,0:T(8,128)(2,1)S(1)} %get-tuple-element.55), channel_id=1, source_target_pairs={{1,0},{2,1},{3,2},{5,4},{6,5},{7,6},{9,8},{10,9},{11,10},{13,12},{... | collective-permute-start | bytes 24584 | tf_op jit(solution)/shard_map/ppermute | solution.py:203
  103.6 4.4 %collective-permute-start.4 = (bf16[8,2,16,16]{3,2,1,0:T(8,128)(2,1)S(1)}, bf16[8,2,16,16]{3,2,1,0:T(8,128)(2,1)S(1)}, u32[]{:S(2)}, u32[]{:S(2)}) collective-permute-start(bf16[8,2,16,16]{3,2,1,0:T(8,128)(2,1)S(1)} %get-tuple-element.56), channel_id=1, source_target_pairs={{0,1},{1,2},{2,3},{4,5},{5,6},{6,7},{8,9},{9,10},{10,11},{12,13},{... | collective-permute-start | bytes 24584 | tf_op jit(solution)/shard_map/ppermute | solution.py:201
  108.0 0.6 copy.52
  108.7 0.5 collective-permute-done.4
  109.3 0.8 fusion.30
  110.2 1.5 %fusion.31 = (bf16[6,6,14,16]{3,2,1,0:T(8,128)(2,1)}, bf16[6,6,14,16]{3,2,1,0:T(8,128)(2,1)}, bf16[6,6,14,16]{3,2,1,0:T(8,128)(2,1)}, bf16[6,6,14,16]{3,2,1,0:T(...) fusion(bf16[8,6,16,16]{3,2,1,0:T(8,128)(2,1)S(1)} %get-tuple-el, ...), kind=kLoop, calls=%fused_computation.60 | loop fusion | bytes 580608 | tf_op jit(solution)/shard_map/slice | solution.py:218
  111.7 4.7 %concatenate.46 = bf16[6,6,14,432]{3,2,1,0:T(8,128)(2,1)S(1)} concatenate(bf16[6,6,14,16]{3,2,1,0:T(8,128)(2,1)} %get-tuple-element.63, bf16[6,6,14,16]{3,2,1,0:T(8,128)(2,1)} %get-tuple-element.64, bf16[6,6,14,16]{3,2,1,0:T(8,128)(2,1)} %get-tuple-element.65, bf16[6,6,14,16]{3,2,1,0:T(8,128)(2,1)} %get-tuple-element.34, bf16[6,6,14,16]{3,2,1,0:T(8,128)(2,1)S(1)} %get-tuple-element.33, ...), dimensions={3} | concatenate | bytes 870912 | tf_op jit(solution)/shard_map/concatenate | solution.py:225
  116.5 1.4 %fusion.5 = bf16[6,6,14,384]{3,2,1,0:T(8,128)(2,1)S(1)} fusion(bf16[6,6,14,432]{3,2,1,0:T(8,128)(2,1)S(1)} %concatenate.46, bf16[432,384,1,1]{1,0,3,2:T(8,128)(2,1)} %bitcast.86, f32[6,14]{1,0:T(8,128)S(1)} %get-tuple-element.62, f32[6]{0:T(128)S(1)} %compare_select_fusion, f32[384]{0:T(512)S(1)} %copy-done.10), kind=kOutput, calls=%fused_computation.15 | convolution fusion | flops 167989248 | bytes 1156200 | tf_op jit(solution)/shard_map/dot_general | solution.py:227
  118.1 0.2 reshape.183
  118.3 0.4 copy-done.9
  118.8 0.8 fusion.4
  119.7 0.4 copy.62
  120.1 0.2 reshape.186
  120.7 2.0 %fusion.28 = (bf16[8,8,24,384]{3,0,2,1:T(8,128)(2,1)S(1)}, bf16[8,8,24,384]{3,0,2,1:T(8,128)(2,1)S(1)}, bf16[8,8,24,384]{3,0,2,1:T(8,128)(2,1)S(1)}, bf16[8,8,24...) fusion(bf16[8,12,28,384]{3,0,2,1:T(8,128)(2,1)S(1)} %bitcast.72), kind=kLoop, calls=%fused_computation.57 | loop fusion | bytes 21233664 | tf_op jit(solution)/shard_map/slice | solution.py:267
  124.3 1.1 copy-done.4
  125.5 0.6 fusion.14
  126.0 0.6 convolution_add_fusion.7
  126.6 0.6 convolution_add_fusion.6
  127.2 0.6 convolution_add_fusion.5
  127.8 0.6 convolution_add_fusion.4
  128.4 0.6 convolution_add_fusion.3
  129.0 0.6 convolution_add_fusion.2
  129.5 0.6 convolution_add_fusion.1
  130.2 0.6 fusion.1
  130.8 1.2 copy.51
  (57 shorter events, 3.6 us)
Async XLA Ops:
  0.6 117.7 %copy-start = (bf16[3,384,768]{2,1,0:T(8,128)(2,1)S(1)}, bf16[3,384,768]{2,1,0:T(8,128)(2,1)}, u32[]{:S(2)}) copy-start(bf16[3,384,768]{2,1,0:T(8,128)(2,1)} %param.20) | copy-start | bytes 5308420
  0.6 1.5 %copy-start.5 = (bf16[1,4,2,6,4096]{4,2,3,1,0:T(2,128)(2,1)S(1)}, bf16[1,4,2,6,4096]{4,2,3,1,0:T(2,128)(2,1)}, u32[]{:S(2)}) copy-start(bf16[1,4,2,6,4096]{4,2,3,1,0:T(2,128)(2,1)} %param.13) | copy-start | bytes 1179652
  2.0 1.3 copy-start.6
  6.0 1.0 copy-start.2
  7.0 1.0 copy-start.3
  8.5 1.0 copy-start.1
  9.5 40.7 %all-to-all-start = ((bf16[32,120,128]{2,1,0:T(8,128)(2,1)}), bf16[32,120,128]{2,1,0:T(8,128)(2,1)S(1)}, u32[]{:S(2)}, u32[]{:S(2)}) async-start(bf16[32,120,128]{2,1,0:T(8,128)(2,1)} %copy-done.1), calls=%async_computation | async-start | bytes 1966080 | tf_op jit(solution)/shard_map/all_to_all | solution.py:309
  50.2 11.9 %collective-permute-start = (bf16[16,72,128]{2,1,0:T(8,128)(2,1)S(1)}, bf16[16,72,128]{2,1,0:T(8,128)(2,1)S(1)}, u32[]{:S(2)}, u32[]{:S(2)}) collective-permute-start(bf16[16,72,128]{2,1,0:T(8,128)(2,1)S(1)} %constant_dynamic-slice_fusion), channel_id=1, source_target_pairs={{0,50},{1,51},{2,48},{3,49},{4,54},{5,55},{6,52},{7,53},{8,58},{9,... | collective-permute-start | bytes 884744 | tf_op jit(solution)/shard_map/ppermute | solution.py:311
  62.2 10.3 %copy-start.7 = (f32[1,4,2,6,64]{4,2,3,1,0:T(2,128)S(1)}, f32[1,4,2,6,64]{4,2,3,1,0:T(2,128)}, u32[]{:S(2)}) copy-start(f32[1,4,2,6,64]{4,2,3,1,0:T(2,128)} %param.15) | copy-start | bytes 36868
  66.8 16.6 %all-to-all-start.1 = ((bf16[32,24,128]{2,1,0:T(8,128)(2,1)}), bf16[32,24,128]{2,1,0:T(8,128)(2,1)S(1)}, u32[]{:S(2)}, u32[]{:S(2)}) async-start(bf16[32,24,128]{2,1,0:T(8,128)(2,1)} %shard_map.133), calls=%async_computation.1 | async-start | bytes 393216 | tf_op jit(solution)/shard_map/all_to_all | solution.py:314
  83.9 7.7 %collective-permute-start.1 = (bf16[4,4,12,16]{3,2,1,0:T(8,128)(2,1)S(1)}, bf16[4,4,12,16]{3,2,1,0:T(8,128)(2,1)S(1)}, u32[]{:S(2)}, u32[]{:S(2)}) collective-permute-start(bf16[4,4,12,16]{3,2,1,0:T(8,128)(2,1)S(1)} %copy.39), channel_id=1, source_target_pairs={{0,16},{16,32},{32,48},{48,64},{64,80},{80,96},{96,112},{112,128},... | collective-permute-start | bytes 18440 | tf_op jit(solution)/shard_map/ppermute | solution.py:190
  91.6 3.5 %collective-permute-start.2 = (bf16[8,4,2,16]{3,2,1,0:T(2,128)(2,1)S(1)}, bf16[8,4,2,16]{3,2,1,0:T(2,128)(2,1)S(1)}, u32[]{:S(2)}, u32[]{:S(2)}) collective-permute-start(bf16[8,4,2,16]{3,2,1,0:T(2,128)(2,1)S(1)} %get-tuple-element.57), channel_id=1, source_target_pairs={{0,4},{4,8},{8,12},{1,5},{5,9},{9,13},{2,6},{6,10},{10,14},{3,7},{... | collective-permute-start | bytes 6152 | tf_op jit(solution)/shard_map/ppermute | solution.py:201
  93.8 4.5 %collective-permute-start.3 = (bf16[8,4,2,16]{3,2,1,0:T(2,128)(2,1)S(1)}, bf16[8,4,2,16]{3,2,1,0:T(2,128)(2,1)S(1)}, u32[]{:S(2)}, u32[]{:S(2)}) collective-permute-start(bf16[8,4,2,16]{3,2,1,0:T(2,128)(2,1)S(1)} %get-tuple-element.58), channel_id=1, source_target_pairs={{4,0},{8,4},{12,8},{5,1},{9,5},{13,9},{6,2},{10,6},{14,10},{7,3},{... | collective-permute-start | bytes 6152 | tf_op jit(solution)/shard_map/ppermute | solution.py:203
  98.4 10.3 %collective-permute-start.5 = (bf16[8,2,16,16]{3,2,1,0:T(8,128)(2,1)S(1)}, bf16[8,2,16,16]{3,2,1,0:T(8,128)(2,1)S(1)}, u32[]{:S(2)}, u32[]{:S(2)}) collective-permute-start(bf16[8,2,16,16]{3,2,1,0:T(8,128)(2,1)S(1)} %get-tuple-element.55), channel_id=1, source_target_pairs={{1,0},{2,1},{3,2},{5,4},{6,5},{7,6},{9,8},{10,9},{11,10},{13,12},{... | collective-permute-start | bytes 24584 | tf_op jit(solution)/shard_map/ppermute | solution.py:203
  103.6 5.5 %collective-permute-start.4 = (bf16[8,2,16,16]{3,2,1,0:T(8,128)(2,1)S(1)}, bf16[8,2,16,16]{3,2,1,0:T(8,128)(2,1)S(1)}, u32[]{:S(2)}, u32[]{:S(2)}) collective-permute-start(bf16[8,2,16,16]{3,2,1,0:T(8,128)(2,1)S(1)} %get-tuple-element.56), channel_id=1, source_target_pairs={{0,1},{1,2},{2,3},{4,5},{5,6},{6,7},{8,9},{9,10},{10,11},{12,13},{... | collective-permute-start | bytes 24584 | tf_op jit(solution)/shard_map/ppermute | solution.py:201
  111.7 4.8 %copy-start.10 = (f32[384]{0:T(512)S(1)}, f32[384]{0:T(512)}, u32[]{:S(2)}) copy-start(f32[384]{0:T(512)} %param.19) | copy-start | bytes 4612
  118.1 0.7 copy-start.9
  124.1 1.3 %copy-start.4 = (bf16[3,3,384,192]{2,3,1,0:T(8,128)(2,1)S(1)}, bf16[3,3,384,192]{2,3,1,0:T(8,128)(2,1)}, u32[]{:S(2)}) copy-start(bf16[3,3,384,192]{2,3,1,0:T(8,128)(2,1)} %param.22) | copy-start | bytes 3981316
  129.5 0.7 copy-start.8

commit v2 on v1

v2 whole, which is shorter than its diff:
```python
import math

import jax
import jax.numpy as jnp
from jax import lax
from jax.experimental import pallas as pl
from jax.experimental.pallas import tpu as pltpu
from jax.sharding import PartitionSpec as P

HD = 128
ZC = 16
HEADS = 32
OWN = 48
LAT = 64
ROWS = 2 * OWN + OWN // 2
AXES = ("grp", "head", "tile")
VMEM_BYTES = 32 * 1024 * 1024


def device_id(y, pair, low, x, high, core):
    return ((y * 4 + 2 * pair + low) * 4 + x) * 4 + 2 * high + core


def pair_groups():
    groups = []
    for y in range(4):
        for pair in range(2):
            members = []
            for a in range(2):
                for x in range(4):
                    for b in range(2):
                        for core in range(2):
                            low = a if pair == 0 else 1 - a
                            high = b if pair == 0 or a == 1 else 1 - b
                            members.append(device_id(y, pair, low, x, high, core))
            groups.append(members)
    return groups


def half_groups(groups):
    return [[d for d in group if d // 2 % 2 == high] for group in groups for high in range(2)]


def prior_route(groups):
    return [(groups[g][k], groups[g + 1][k]) for g in range(len(groups) - 1) for k in range(HEADS)]


PREP_STEPS = 4
PREP_HEADS = HEADS // PREP_STEPS


def prep_kernel(query_ref, key_ref, value_ref, weight_ref, out_ref):
    dims = (((1,), (1,)), ((), ()))
    for h in range(PREP_HEADS):
        lanes = slice(h * HD, (h + 1) * HD)
        out_ref[h, 0:OWN, :] = query_ref[:, lanes]
        out_ref[h, OWN : 2 * OWN, :] = key_ref[:, lanes]
        folded = lax.dot_general(
            value_ref[:, lanes], weight_ref[:, lanes], dims, preferred_element_type=jnp.float32
        )
        packed = jnp.concatenate([folded[: OWN // 2], folded[OWN // 2 :]], axis=1)
        out_ref[h, 2 * OWN : ROWS, :] = packed.astype(jnp.bfloat16)


def token_rows(states):
    return states.transpose(0, 1, 3, 2, 4).reshape(OWN, states.shape[-1])


def prep(query, key, value, weight):
    width = PREP_HEADS * HD
    tile = pl.BlockSpec((OWN, width), lambda i: (0, i))
    return pl.pallas_call(
        prep_kernel,
        grid=(PREP_STEPS,),
        out_shape=jax.ShapeDtypeStruct((HEADS, ROWS, HD), jnp.bfloat16),
        in_specs=[tile, tile, tile, pl.BlockSpec((LAT, width), lambda i: (0, i))],
        out_specs=pl.BlockSpec((PREP_HEADS, ROWS, HD), lambda i: (i, 0, 0)),
        compiler_params=pltpu.CompilerParams(vmem_limit_bytes=16 * 1024 * 1024),
    )(token_rows(query), token_rows(key), token_rows(value), weight.T)


def spread_values(packed, target):
    lower = packed[:, :, :LAT].astype(jnp.float32)
    upper = packed[:, :, LAT:].astype(jnp.float32)
    both = jnp.concatenate([lower, upper], axis=1).reshape(16 * OWN, LAT)
    ones = jnp.ones((16 * OWN, HD - LAT), jnp.float32)
    target[...] = jnp.concatenate([both, ones], axis=1).astype(jnp.bfloat16)


def fold_scale():
    return (1.0 / math.sqrt(HD)) * math.log2(math.e)


def scores_of(query, keys):
    dims = (((1,), (1,)), ((), ()))
    return lax.dot_general(query, keys, dims, preferred_element_type=jnp.float32)


def pack_result(mixed, out_ref, start, blocks):
    velocity = mixed[:, :LAT] / mixed[:, LAT : 2 * LAT]
    velocity = velocity.reshape(blocks, OWN, LAT)
    packed = jnp.concatenate([velocity[:, : OWN // 2], velocity[:, OWN // 2 :]], axis=2)
    out_ref[pl.ds(start, blocks)] = packed.astype(out_ref.dtype)


QB = 16
PB = 8


def late_part_kernel(place_ref, recv_ref, *rest):
    rest[-1][...] = recv_ref[pl.ds(16 - place_ref[0], 16), OWN:, :]


def late_part(place, recv, ready):
    vmem = pl.BlockSpec(memory_space=pltpu.VMEM)
    return pl.pallas_call(
        late_part_kernel,
        out_shape=jax.ShapeDtypeStruct((16, ROWS - OWN, HD), jnp.bfloat16),
        in_specs=[pl.BlockSpec(memory_space=pltpu.SMEM), vmem]
        + [pl.BlockSpec(memory_space=pl.ANY)] * len(ready),
        out_specs=vmem,
        compiler_params=pltpu.CompilerParams(vmem_limit_bytes=4 * 1024 * 1024),
    )(place, recv, *ready)


def attend_here_kernel(place_ref, recv_ref, out_ref, max_ref, mix_ref, early_v, late_v):
    early = place_ref[0]
    late = 16 - early
    spread_values(recv_ref[pl.ds(early, 16), 2 * OWN :, :], early_v)
    spread_values(recv_ref[pl.ds(late, 16), 2 * OWN :, :], late_v)
    early_k = recv_ref[pl.ds(early, 16), OWN : 2 * OWN, :].reshape(16 * OWN, HD)
    late_k = recv_ref[pl.ds(late, 16), OWN : 2 * OWN, :].reshape(16 * OWN, HD)
    scale = fold_scale()

    def late_block(i, carry):
        query = recv_ref[pl.ds(late + i * QB, QB), :OWN, :].reshape(QB * OWN, HD)
        here = scores_of(query, late_k) * scale
        before = scores_of(query, early_k) * scale
        top = jnp.maximum(
            jnp.max(here, axis=1, keepdims=True), jnp.max(before, axis=1, keepdims=True)
        )
        here = jnp.exp2(here - top).astype(jnp.bfloat16)
        before = jnp.exp2(before - top).astype(jnp.bfloat16)
        mixed = jnp.dot(here, late_v[...], preferred_element_type=jnp.float32)
        mixed += jnp.dot(before, early_v[...], preferred_element_type=jnp.float32)
        pack_result(mixed, out_ref, i * QB, QB)
        return carry

    lax.fori_loop(0, 16 // QB, late_block, 0)

    def early_block(i, carry):
        query = recv_ref[pl.ds(early + i * QB, QB), :OWN, :].reshape(QB * OWN, HD)
        here = scores_of(query, early_k) * scale
        top = jnp.max(here, axis=1, keepdims=True)
        here = jnp.exp2(here - top).astype(jnp.bfloat16)
        mix_ref[pl.ds(i * QB * OWN, QB * OWN), :] = jnp.dot(
            here, early_v[...], preferred_element_type=jnp.float32
        )
        max_ref[pl.ds(i * QB * OWN, QB * OWN), :] = jnp.broadcast_to(top, (QB * OWN, HD))
        return carry

    lax.fori_loop(0, 16 // QB, early_block, 0)


def attend_here(place, recv):
    vmem = pl.BlockSpec(memory_space=pltpu.VMEM)
    tokens = 16 * OWN
    return pl.pallas_call(
        attend_here_kernel,
        out_shape=(
            jax.ShapeDtypeStruct((16, OWN // 2, HD), jnp.float32),
            jax.ShapeDtypeStruct((tokens, HD), jnp.float32),
            jax.ShapeDtypeStruct((tokens, HD), jnp.float32),
        ),
        in_specs=[pl.BlockSpec(memory_space=pltpu.SMEM), vmem],
        out_specs=(vmem, vmem, vmem),
        scratch_shapes=[pltpu.VMEM((tokens, HD), jnp.bfloat16)] * 2,
        compiler_params=pltpu.CompilerParams(vmem_limit_bytes=VMEM_BYTES),
        cost_estimate=pl.CostEstimate(
            flops=4 * 3 * tokens * tokens * HD, bytes_accessed=4 << 20, transcendentals=3 * tokens * tokens
        ),
    )(place, recv)


def attend_prior_kernel(
    place_ref, recv_ref, prior_ref, late_ref, max_ref, mix_ref, out_hbm, prior_v, packed_ref, grid_ref,
    out_ref, sem,
):
    early = place_ref[0]
    late = 16 - early
    penalty = jnp.where(place_ref[1] > 0, 0.0, -1e30).astype(jnp.float32)
    spread_values(prior_ref[:, OWN:, :], prior_v)
    prior_k = prior_ref[:, :OWN, :].reshape(16 * OWN, HD)
    scale = fold_scale()
    packed_ref[pl.ds(late, 16)] = late_ref[...]

    def block(i, carry):
        rows = pl.ds(i * PB * OWN, PB * OWN)
        query = recv_ref[pl.ds(early + i * PB, PB), :OWN, :].reshape(PB * OWN, HD)
        before = scores_of(query, prior_k) * scale + penalty
        old = max_ref[rows, :]
        top = jnp.maximum(old[:, :1], jnp.max(before, axis=1, keepdims=True))
        before = jnp.exp2(before - top).astype(jnp.bfloat16)
        mixed = jnp.dot(before, prior_v[...], preferred_element_type=jnp.float32)
        mixed += mix_ref[rows, :] * jnp.exp2(old - top)
        pack_result(mixed, packed_ref, early + i * PB, PB)
        return carry

    lax.fori_loop(0, 16 // PB, block, 0, unroll=True)
    scatter_halo(place_ref, packed_ref, grid_ref, out_ref)
    copy = pltpu.make_async_copy(out_ref, out_hbm, sem)
    copy.start()
    copy.wait()


def scatter_halo(place_ref, packed_ref, grid_ref, out_ref):
    flip = place_ref[2]
    high = place_ref[3]
    grid_ref[...] = jnp.zeros_like(grid_ref)
    for a in range(2):
        for b in range(2):
            tile_high = b if a == 1 else jnp.where(flip > 0, 1 - b, b)
            for core in range(2):
                row = 2 * (2 * tile_high + core) + 1
                for x in range(4):
                    block = a * 16 + x * 4 + b * 2 + core
                    for frame in range(2):
                        for sub in range(2):
                            line = packed_ref[block, pl.ds(frame * 12 + sub, 6, stride=2), :]
                            grid_ref[a, x, frame, row + sub, 1:7, :] = line
                            if x < 3:
                                grid_ref[a, x + 1, frame, row + sub, 0:1, :] = line[5:6]
                            if x > 0:
                                grid_ref[a, x - 1, frame, row + sub, 7:8, :] = line[0:1]
    for a in range(2):
        for x in range(4):
            for core in range(2):
                for part in range(2):
                    row = 2 * (2 * (high if part == 0 else 1 - high) + core)
                    tile = grid_ref[a, x, :, pl.ds(row, 4), :, :].reshape(64, HD)
                    out_ref[a * 8 + x * 2 + core, part * 64 : (part + 1) * 64, :] = tile.astype(
                        jnp.bfloat16
                    )


def attend_prior(place, recv, prior, late, top, mix):
    vmem = pl.BlockSpec(memory_space=pltpu.VMEM)
    tokens = 16 * OWN
    return pl.pallas_call(
        attend_prior_kernel,
        out_shape=pltpu.HBM((16, 128, HD), jnp.bfloat16),
        in_specs=[pl.BlockSpec(memory_space=pltpu.SMEM)] + [vmem] * 5,
        out_specs=pl.BlockSpec(memory_space=pltpu.HBM),
        scratch_shapes=[
            pltpu.VMEM((tokens, HD), jnp.bfloat16),
            pltpu.VMEM((HEADS, OWN // 2, HD), jnp.float32),
            pltpu.VMEM((2, 4, 2, 10, 8, HD), jnp.float32),
            pltpu.VMEM((16, 128, HD), jnp.bfloat16),
            pltpu.SemaphoreType.DMA,
        ],
        compiler_params=pltpu.CompilerParams(vmem_limit_bytes=VMEM_BYTES),
    )(place, recv, prior, late, top, mix)


def sum_kernel(back_ref, own_ref, other_ref):
    total = back_ref[0].astype(jnp.float32)
    for k in range(1, 16):
        total += back_ref[k].astype(jnp.float32)
    own_ref[...] = total[:64]
    other_ref[...] = total[64:].astype(jnp.bfloat16)


def sum_heads(back):
    vmem = pl.BlockSpec(memory_space=pltpu.VMEM)
    return pl.pallas_call(
        sum_kernel,
        out_shape=(
            jax.ShapeDtypeStruct((64, HD), jnp.float32),
            jax.ShapeDtypeStruct((64, HD), jnp.bfloat16),
        ),
        in_specs=[vmem],
        out_specs=(vmem, vmem),
        compiler_params=pltpu.CompilerParams(vmem_limit_bytes=4 * 1024 * 1024),
    )(back)


CH = 384
OC = 192
TAPS = {(0, 0): (0, 1), (0, 1): (2,), (1, 0): (0,), (1, 1): (1, 2)}


def spread_inlet(inlet_ref, wide_ref):
    wide_ref[...] = jnp.zeros_like(wide_ref)
    for frame in range(3):
        for b in range(3):
            for e in range(3):
                tap = inlet_ref[((frame * 3 + b) * 3 + e) * ZC : ((frame * 3 + b) * 3 + e + 1) * ZC, :]
                for down in range(2):
                    for right in range(2):
                        u, v = b + down, e + right
                        row = frame * 256 + (u // 2 * 2 + v // 2) * LAT + (u % 2 * 2 + v % 2) * ZC
                        sub = 2 * down + right
                        wide_ref[row : row + ZC, sub * CH : (sub + 1) * CH] = tap


def window_kernel(spatial_ref, window_ref):
    for wy in range(2):
        for wx in range(2):
            rows = slice((2 * wy + wx) * CH, (2 * wy + wx + 1) * CH)
            rest = []
            for oy in range(2):
                for ox in range(2):
                    total = None
                    for b in TAPS[oy, wy]:
                        for e in TAPS[ox, wx]:
                            tap = spatial_ref[b, e].astype(jnp.float32)
                            total = tap if total is None else total + tap
                    out = 2 * oy + ox
                    window_ref[rows, out * 128 : (out + 1) * 128] = total[:, :128].astype(jnp.bfloat16)
                    rest.append(total[:, 128:])
            for oy in range(2):
                both = jnp.concatenate([rest[2 * oy], rest[2 * oy + 1]], axis=1)
                window_ref[rows, (4 + oy) * 128 : (5 + oy) * 128] = both.astype(jnp.bfloat16)


def window_weights(spatial_weight):
    vmem = pl.BlockSpec(memory_space=pltpu.VMEM)
    return pl.pallas_call(
        window_kernel,
        out_shape=jax.ShapeDtypeStruct((4 * CH, 4 * OC), jnp.bfloat16),
        in_specs=[vmem],
        out_specs=vmem,
        compiler_params=pltpu.CompilerParams(vmem_limit_bytes=16 * 1024 * 1024),
        cost_estimate=pl.CostEstimate(flops=4 << 20, bytes_accessed=4 << 20, transcendentals=0),
    )(spatial_weight)


WIN = 24


def decode_kernel(
    place_ref, before_ref, now_ref, inlet_ref, inlet_bias_ref, time_hbm, time_bias_ref, window_hbm,
    space_bias_ref, out_ref, patch_ref, feature_ref, time_in_ref, double_ref, shift_ref, space_in_ref,
    low_ref, rest_ref, wide_ref, time_ref, window_ref, sems,
):
    time_copy = pltpu.make_async_copy(time_hbm, time_ref, sems.at[0])
    time_copy.start()
    window_copy = pltpu.make_async_copy(window_hbm, window_ref, sems.at[1])
    window_copy.start()
    has_prior, tile, head = place_ref[0], place_ref[1], place_ref[2]
    spread_inlet(inlet_ref, wide_ref)
    for half, ref in enumerate((before_ref, now_ref)):
        cells = ref[...].astype(jnp.float32)
        after = jnp.concatenate([cells[1:], cells[:1]], axis=0)
        for part in range(2):
            lanes = slice(part * LAT, (part + 1) * LAT)
            pairs = jnp.concatenate([cells[:, lanes], after[:, lanes]], axis=1)
            for frame in range(2):
                row = (half * 4 + part * 2 + frame) * WIN
                patch_ref[row : row + WIN, :128] = pairs[frame * 32 : frame * 32 + WIN]
                patch_ref[row : row + WIN, 128:] = pairs[frame * 32 + 8 : frame * 32 + 8 + WIN]
    taps = [patch_ref[a * WIN : (a + 6) * WIN, :].astype(jnp.bfloat16) for a in range(3)]
    features = jnp.dot(
        jnp.concatenate(taps, axis=1), wide_ref[...], preferred_element_type=jnp.float32
    )
    frame_row = lax.broadcasted_iota(jnp.int32, (6 * WIN, 1), 0)
    keep = jnp.logical_or(frame_row >= 2 * WIN, has_prior > 0)
    for sub in range(4):
        lanes = slice(sub * CH, (sub + 1) * CH)
        value = jnp.where(keep, features[:, lanes] + inlet_bias_ref[...], 0.0)
        feature_ref[:, lanes] = value
    for sub in range(4):
        for a in range(3):
            time_in_ref[sub * 96 : (sub + 1) * 96, a * CH : (a + 1) * CH] = feature_ref[
                a * WIN : a * WIN + 96, sub * CH : (sub + 1) * CH
            ].astype(jnp.bfloat16)
    time_copy.wait()
    doubled = jnp.dot(time_in_ref[...], time_ref[...], preferred_element_type=jnp.float32)
    place = lax.broadcasted_iota(jnp.int32, (96, 1), 0)
    window_row = lax.rem(place, WIN) // 8
    window_col = lax.rem(place, 8)
    for sub in range(4):
        row = 4 * tile + 2 * window_row - 1 + sub // 2
        col = 12 * head + 2 * window_col - 1 + sub % 2
        inside = jnp.logical_and(
            jnp.logical_and(row >= 0, row < 16), jnp.logical_and(col >= 0, col < 48)
        )
        value = jnp.where(inside, doubled[sub * 96 : (sub + 1) * 96] + time_bias_ref[...], 0.0)
        double_ref[sub, :96, :] = value
        double_ref[sub, 96:, :] = jnp.zeros((16, 2 * CH), jnp.float32)
        if sub % 2 == 0:
            shift_ref[sub // 2, :103, :] = double_ref[sub, 1:104, :]
            shift_ref[sub // 2, 103:, :] = jnp.zeros((9, 2 * CH), jnp.float32)
    for py in range(2):
        for px in range(2):
            for wy in range(2):
                for wx in range(2):
                    down, right = (py + wy) // 2, (px + wx) // 2
                    alpha, beta = (py + wy) % 2, (px + wx) % 2
                    for u in range(2):
                        lanes = slice(u * CH, (u + 1) * CH)
                        rows = slice(down * 8, down * 8 + 96)
                        if right:
                            value = shift_ref[alpha, rows, lanes]
                        else:
                            value = double_ref[2 * alpha + beta, rows, lanes]
                        start = ((2 * py + px) * 2 + u) * 96
                        piece = (2 * wy + wx) * CH
                        space_in_ref[start : start + 96, piece : piece + CH] = value.astype(
                            jnp.bfloat16
                        )
    window_copy.wait()
    for py in range(2):
        for px in range(2):
            start = (2 * py + px) * 192
            mixed = jnp.dot(
                space_in_ref[start : start + 192, :], window_ref[...], preferred_element_type=jnp.float32
            )
            for oy in range(2):
                for ox in range(2):
                    column = 8 - 1 + 2 * px + ox
                    out = 2 * oy + ox
                    for ri in range(3):
                        high = 4 * ri - 1 + 2 * py + oy
                        if not 0 <= high < 8:
                            continue
                        for u in range(2):
                            for t in range(4):
                                row = u * 96 + t * WIN + ri * 8
                                low = mixed[row : row + 8, out * 128 : (out + 1) * 128]
                                rest = mixed[row : row + 8, (4 + oy) * 128 : (5 + oy) * 128]
                                if ox:
                                    rest = pltpu.roll(rest, 64, 1)
                                spot = pl.ds(column, 8, stride=4)
                                low_ref[(2 * t + u) * 8 + high, spot, :] = low
                                rest_ref[(2 * t + u) * 8 + high, spot, :] = rest
    low_bias = space_bias_ref[:, :128]
    rest_bias = space_bias_ref[:, 128:]
    for frame in range(8):
        for high in range(8):
            line = frame * 8 + high
            out_ref[frame, high, :, :128] = (low_ref[line, 8:32, :] + low_bias).astype(jnp.bfloat16)
            out_ref[frame, high, :, 128:] = (rest_ref[line, 8:32, :LAT] + rest_bias).astype(
                jnp.bfloat16
            )


def decode(place, before, now, inlet, inlet_bias, time_weight, time_bias, window, space_bias):
    vmem = pl.BlockSpec(memory_space=pltpu.VMEM)
    hbm = pl.BlockSpec(memory_space=pltpu.HBM)
    f32, bf16 = jnp.float32, jnp.bfloat16
    time_weight = pltpu.with_memory_space_constraint(time_weight, pltpu.HBM)
    window = pltpu.with_memory_space_constraint(window, pltpu.HBM)
    return pl.pallas_call(
        decode_kernel,
        out_shape=jax.ShapeDtypeStruct((8, 8, 24, OC), bf16),
        in_specs=[pl.BlockSpec(memory_space=pltpu.SMEM)] + [vmem] * 4 + [hbm, vmem, hbm, vmem],
        out_specs=vmem,
        scratch_shapes=[
            pltpu.VMEM((8 * WIN, 256), f32),
            pltpu.VMEM((6 * WIN, 4 * CH), f32),
            pltpu.VMEM((384, 3 * CH), bf16),
            pltpu.VMEM((4, 112, 2 * CH), f32),
            pltpu.VMEM((2, 112, 2 * CH), f32),
            pltpu.VMEM((768, 4 * CH), bf16),
            pltpu.VMEM((64, 40, 128), f32),
            pltpu.VMEM((64, 40, 128), f32),
            pltpu.VMEM((768, 4 * CH), bf16),
            pltpu.VMEM((3 * CH, 2 * CH), bf16),
            pltpu.VMEM((4 * CH, 4 * OC), bf16),
            pltpu.SemaphoreType.DMA((2,)),
        ],
        compiler_params=pltpu.CompilerParams(vmem_limit_bytes=VMEM_BYTES),
    )(place, before, now, inlet, inlet_bias, time_weight, time_bias, window, space_bias)


def shifted(block, axis, distance):
    devices = range(lax.axis_size(axis))
    route = [(i - distance, i) for i in devices if i - distance in devices]
    return lax.ppermute(block, axis, route)


def with_halo(cells, sides, width):
    for axis, dim in sides:
        count = lax.axis_size(axis)
        ends = count - 1
        head = lax.slice_in_dim(cells, 0, width, axis=dim)
        tail = lax.slice_in_dim(cells, cells.shape[dim] - width, cells.shape[dim], axis=dim)
        cells = jnp.concatenate(
            [
                lax.ppermute(tail, axis, [(i, (i + 1) % count) for i in range(ends)]),
                cells,
                lax.ppermute(head, axis, [((i + 1) % count, i) for i in range(ends)]),
            ],
            axis=dim,
        )
    return cells


def shards(
    query_states,
    key_states,
    value_states,
    noisy_latent,
    noise_level,
    head_weight,
    inlet_weight,
    inlet_bias,
    temporal_weight,
    temporal_bias,
    spatial_weight,
    spatial_bias,
):
    groups = pair_groups()
    grp = lax.axis_index("grp")
    pair = (grp // 2) % 2
    has_prior = grp > 0
    early = 16 * pair
    pair_has_prior = (grp // 2 > 0).astype(jnp.int32)
    high = lax.axis_index("tile") // 2
    place = jnp.stack([early, pair_has_prior, pair, high]).astype(jnp.int32)
    sent = prep(query_states, key_states, value_states, head_weight)
    sent, spatial_weight, noisy_latent = lax.optimization_barrier(
        (sent, spatial_weight, noisy_latent)
    )
    window = window_weights(spatial_weight)
    halo_noisy = with_halo(noisy_latent[0], (("head", 2), ("tile", 1)), 1)
    halo_noisy = halo_noisy.reshape(2, 2, 4, 8, LAT).transpose(1, 2, 3, 0, 4).reshape(64, HD)
    recv = lax.all_to_all(sent, AXES, 0, 0, tiled=True, axis_index_groups=groups)
    late_kv = late_part(place, recv, (halo_noisy, window))
    prior = lax.ppermute(late_kv, AXES, prior_route(groups))
    late, top, mix = attend_here(place, recv)
    partial = attend_prior(place, recv, prior, late, top, mix)
    back = lax.all_to_all(partial, AXES, 0, 0, tiled=True, axis_index_groups=half_groups(groups))
    own, other = sum_heads(back)
    other = lax.ppermute(other, "tile", [(0, 2), (1, 3), (2, 0), (3, 1)])
    velocity = own + other.astype(jnp.float32)
    clean = halo_noisy - noise_level[0] * velocity
    latent = clean.astype(jnp.bfloat16)
    before = shifted(latent, "grp", 1)
    clean_latent = clean.reshape(2, 4, 8, 2, LAT)[:, 1:3, 1:7].transpose(3, 0, 1, 2, 4)
    clean_latent = clean_latent.reshape(noisy_latent.shape)
    where = jnp.stack([has_prior.astype(jnp.int32), lax.axis_index("tile"), lax.axis_index("head")])
    decoded = decode(
        where,
        before,
        latent,
        inlet_weight.reshape(27 * ZC, CH),
        inlet_bias[None],
        temporal_weight.reshape(3 * CH, 2 * CH),
        temporal_bias[None],
        window,
        spatial_bias[None],
    )
    return (clean_latent, decoded[None])


def solution(mesh):
    return jax.shard_map(
        shards,
        mesh=mesh,
        in_specs=(
            P("grp", None, "tile", "head", None),
            P("grp", None, "tile", "head", None),
            P("grp", None, "tile", "head", None),
            P("grp", None, "tile", "head", None),
            P("grp"),
            P(),
            P(),
            P(),
            P(),
            P(),
            P(),
            P(),
        ),
        out_specs=(P("grp", None, "tile", "head", None), P("grp", None, "tile", "head", None)),
        check_vma=False,
    )
```

time: 133 us -> 101 us (0.76)
  the two profiles are of different devices: /device:TPU:17 before, /device:TPU:16 now
where the time goes in v2:
time: 101 us; the launch traced here: 100 us
  waiting for transfers between devices  47.3 us (47%)
  starting transfers between devices  27.1 us (27%)
  Pallas kernels  16.7 us (17%)
  local copies, waits for them, and re-layouts  7.2 us (7%)
  between operations  1.62 us (2%)
    all_to_all x1, starting transfers between devices, shards(): lax.all_to_all(sent, AXES, 0, 0, tiled=True, axis_index_groups=groups)  11.4 us
    all_to_all x1, waiting for transfers between devices, shards(): lax.all_to_all(partial, AXES, 0, 0, tiled=True, axis_index_groups=half_gr...  10.8 us
    all_to_all x1, waiting for transfers between devices, shards(): lax.all_to_all(sent, AXES, 0, 0, tiled=True, axis_index_groups=groups)  9.8 us
    ppermute x1, waiting for transfers between devices, shards(): prior = lax.ppermute(late_kv, AXES, prior_route(groups))  7.97 us
    ppermute x1, waiting for transfers between devices, shards(): other = lax.ppermute(other, 'tile', [(0, 2), (1, 3), (2, 0), (3, 1)])  6.86 us
    ppermute x2, waiting for transfers between devices, with_halo(): lax.ppermute(head, axis, [((i + 1) % count, i) for i in range(ends)])  6.74 us
    pallas_call x1, Pallas kernels, decode(): pl.pallas_call(decode_kernel, out_shape=jax.ShapeDtypeStruct((8, 8, 24, O...  6.69 us
    ppermute x1, waiting for transfers between devices, shifted(): return lax.ppermute(block, axis, route)  5.14 us
  transfers between devices with their start and end apart: 9, of which 7 were waited for; matrix products, arithmetic and copies ran while one was open for 3% of the time, Pallas kernels for 4%

profile of v2, /device:TPU:16, one launch (start us, length us, event | category | flops | bytes accessed | tf_op | source)
XLA Modules:
  0.0 100.2 jit_solution(15201833657555488762)
XLA Ops:
  0.6 0.0 copy-start.6
  0.6 0.0 copy-start.2
  0.6 1.2 %reshape.31.query_ref = bf16[48,4096]{1,0:T(8,128)(2,1)S(1)} reshape(bf16[1,4,6,2,4096]{4,3,2,1,0:T(2,128)(2,1)} %bitcast.30) | data formatting | bytes 786432 | tf_op jit(solution)/shard_map/reshape | solution.py:66
  1.9 1.1 %reshape.32.key_ref = bf16[48,4096]{1,0:T(8,128)(2,1)S(1)} reshape(bf16[1,4,6,2,4096]{4,3,2,1,0:T(2,128)(2,1)} %bitcast.31) | data formatting | bytes 786432 | tf_op jit(solution)/shard_map/reshape | solution.py:66
  3.0 0.0 copy-done.6
  3.0 0.1 reshape.33.value_ref
  3.2 0.0 copy-done.2
  3.2 0.0 copy-start.7
  3.2 2.4 %shard_map.131 = bf16[32,120,128]{2,1,0:T(8,128)(2,1)} custom-call(bf16[48,4096]{1,0:T(8,128)(2,1)S(1)} %reshape.31.query_ref, bf16[48,4096]{1,0:T(8,128)(2,1)S(1)} %reshape.32.key_ref, bf16[48,4096]{1,0:T(8,128)(2,1)S(1)} %reshape.33.value_ref, bf16[64,4096]{1,0:T(8,128)(2,1)S(1)} %bitcast.25), custom_call_target="tpu_custom_call" | custom-call | tf_op jit(solution)/shard_map/pallas_call | solution.py:72
  5.6 11.4 %all-to-all-start = ((bf16[32,120,128]{2,1,0:T(8,128)(2,1)}), bf16[32,120,128]{2,1,0:T(8,128)(2,1)S(1)}, u32[]{:S(2)}, u32[]{:S(2)}) async-start(bf16[32,120,128]{2,1,0:T(8,128)(2,1)} %shard_map.131), calls=%async_computation | async-start | bytes 1966080 | tf_op jit(solution)/shard_map/all_to_all | solution.py:529
  17.0 0.0 copy-done.7
  17.1 3.7 %collective-permute-start = (f32[4,2,1,64]{3,1,2,0:T(2,128)S(1)}, f32[4,2,1,64]{3,1,2,0:T(2,128)S(1)}, u32[]{:S(2)}, u32[]{:S(2)}) collective-permute-start(f32[4,2,1,64]{3,1,2,0:T(2,128)S(1)} %get-tuple-element.22), channel_id=1, source_target_pairs={{0,4},{4,8},{8,12},{1,5},{5,9},{9,13},{2,6},{6,10},{10,14},{3,7},{... | collective-permute-start | bytes 6152 | tf_op jit(solution)/shard_map/ppermute | solution.py:491
  20.8 1.3 %collective-permute-start.1 = (f32[4,2,1,64]{3,1,2,0:T(2,128)S(1)}, f32[4,2,1,64]{3,1,2,0:T(2,128)S(1)}, u32[]{:S(2)}, u32[]{:S(2)}) collective-permute-start(f32[4,2,1,64]{3,1,2,0:T(2,128)S(1)} %get-tuple-element.23), channel_id=1, source_target_pairs={{4,0},{8,4},{12,8},{5,1},{9,5},{13,9},{6,2},{10,6},{14,10},{7,3},{... | collective-permute-start | bytes 6152 | tf_op jit(solution)/shard_map/ppermute | solution.py:493
  22.1 0.0 collective-permute-done
  22.1 4.1 %collective-permute-done.1 = f32[4,2,1,64]{3,1,2,0:T(2,128)S(1)} collective-permute-done((f32[4,2,1,64]{3,1,2,0:T(2,128)S(1)}, f32[4,2,1,64]{3,1,2,0:T(2,128)S(1)}, u32[]{:S(2)}, u32[]{:S(2)}) %collective-permute-start.1) | collective-permute-done | bytes 2080 | tf_op jit(solution)/shard_map/ppermute | solution.py:493
  26.3 1.3 %collective-permute-start.2 = (f32[4,1,8,64]{3,1,2,0:T(1,128)S(1)}, f32[4,1,8,64]{3,1,2,0:T(1,128)S(1)}, u32[]{:S(2)}, u32[]{:S(2)}) collective-permute-start(f32[4,1,8,64]{3,1,2,0:T(1,128)S(1)} %get-tuple-element.20), channel_id=1, source_target_pairs={{0,1},{1,2},{2,3},{4,5},{5,6},{6,7},{8,9},{9,10},{10,11},{12,13},{... | collective-permute-start | bytes 24584 | tf_op jit(solution)/shard_map/ppermute | solution.py:491
  27.6 1.3 %collective-permute-start.3 = (f32[4,1,8,64]{3,1,2,0:T(1,128)S(1)}, f32[4,1,8,64]{3,1,2,0:T(1,128)S(1)}, u32[]{:S(2)}, u32[]{:S(2)}) collective-permute-start(f32[4,1,8,64]{3,1,2,0:T(1,128)S(1)} %get-tuple-element.21), channel_id=1, source_target_pairs={{1,0},{2,1},{3,2},{5,4},{6,5},{7,6},{9,8},{10,9},{11,10},{13,12},{... | collective-permute-start | bytes 24584 | tf_op jit(solution)/shard_map/ppermute | solution.py:493
  28.9 0.1 pad_add_fusion.place_ref
  29.0 0.0 copy-done.5
  29.0 2.2 %copy.15.spatial_ref = bf16[3,3,384,192]{3,2,1,0:T(8,128)(2,1)} copy(bf16[3,3,384,192]{2,3,1,0:T(8,128)(2,1)S(1)} %copy-done.5) | data formatting | bytes 2654208 | tf_op jit(solution)/shard_map/optimization_barrier | solution.py:523
  31.3 1.5 %copy-done.1 = bf16[3,3,384,192]{3,2,1,0:T(8,128)(2,1)S(1)} copy-done((bf16[3,3,384,192]{3,2,1,0:T(8,128)(2,1)S(1)}, bf16[3,3,384,192]{3,2,1,0:T(8,128)(2,1)}, u32[]{:S(2)}) %copy-start.1) | copy-done | bytes 1327128
  32.7 1.0 shard_map.132.rest_1_.window_hbm
  33.7 0.0 copy-start
  33.7 0.0 collective-permute-done.2
  33.7 2.6 %collective-permute-done.3 = f32[4,1,8,64]{3,1,2,0:T(1,128)S(1)} collective-permute-done((f32[4,1,8,64]{3,1,2,0:T(1,128)S(1)}, f32[4,1,8,64]{3,1,2,0:T(1,128)S(1)}, u32[]{:S(2)}, u32[]{:S(2)}) %collective-permute-start.3) | collective-permute-done | bytes 8224 | tf_op jit(solution)/shard_map/ppermute | solution.py:493
  36.3 0.1 pad_maximum_fusion
  36.4 0.1 copy.18
  36.4 0.1 reshape.35.rest_0_
  36.5 9.8 %all-to-all-done.recv_ref = bf16[32,120,128]{2,1,0:T(8,128)(2,1)S(1)} async-done(((bf16[32,120,128]{2,1,0:T(8,128)(2,1)}), bf16[32,120,128]{2,1,0:T(8,128)(2,1)S(1)}, u32[]{:S(2)}, u32[]{:S(2)}) %all-to-all-start) | async-done | bytes 983072 | tf_op jit(solution)/shard_map/all_to_all | solution.py:529
  46.3 0.6 shard_map.133
  46.9 0.0 copy-done
  46.9 1.9 %collective-permute-start.4 = (bf16[16,72,128]{2,1,0:T(8,128)(2,1)S(1)}, bf16[16,72,128]{2,1,0:T(8,128)(2,1)S(1)}, u32[]{:S(2)}, u32[]{:S(2)}) collective-permute-start(bf16[16,72,128]{2,1,0:T(8,128)(2,1)S(1)} %shard_map.133), channel_id=1, source_target_pairs={{0,50},{1,51},{2,48},{3,49},{4,54},{5,55},{6,52},{7,53},{8,58},{9,... | collective-permute-start | bytes 884744 | tf_op jit(solution)/shard_map/ppermute | solution.py:531
  48.8 3.0 %shard_map.134 = (f32[16,24,128]{2,1,0:T(8,128)S(1)}, f32[768,128]{1,0:T(8,128)S(1)}, f32[768,128]{1,0:T(8,128)S(1)}) custom-call(s32[4]{0:T(128)S(1)} %pad_add_fusion.place_ref, bf16[32,120,128]{2,1,0:T(8,128)(2,1)S(1)} %all-to-all-done.recv_ref), custom_call_target="tpu_custom_call" | custom-call | flops 905969664 | bytes 4194304 | tf_op jit(solution)/shard_map/pallas_call | solution.py:168
  51.8 8.0 %collective-permute-done.4.prior_ref = bf16[16,72,128]{2,1,0:T(8,128)(2,1)S(1)} collective-permute-done((bf16[16,72,128]{2,1,0:T(8,128)(2,1)S(1)}, bf16[16,72,128]{2,1,0:T(8,128)(2,1)S(1)}, u32[]{:S(2)}, u32[]{:S(2)}) %collective-permute-start.4) | collective-permute-done | bytes 294944 | tf_op jit(solution)/shard_map/ppermute | solution.py:531
  59.8 3.1 %shard_map.135 = bf16[16,128,128]{2,1,0:T(8,128)(2,1)} custom-call(s32[4]{0:T(128)S(1)} %pad_add_fusion.place_ref, bf16[32,120,128]{2,1,0:T(8,128)(2,1)S(1)} %all-to-all-done.recv_ref, bf16[16,72,128]{2,1,0:T(8,128)(2,1)S(1)} %collective-permute-done.4.prior_ref, f32[16,24,128]{2,1,0:T(8,128)S(1)} %get-tuple-element.13.late_ref, ...), custom_call_target="tpu_custom_call" | custom-call | tf_op jit(solution)/shard_map/pallas_call | solution.py:249
  62.9 3.6 %all-to-all-start.1 = ((bf16[16,128,128]{2,1,0:T(8,128)(2,1)}), bf16[16,128,128]{2,1,0:T(8,128)(2,1)S(1)}, u32[]{:S(2)}, u32[]{:S(2)}) async-start(bf16[16,128,128]{2,1,0:T(8,128)(2,1)} %shard_map.135), calls=%async_computation.1 | async-start | bytes 1048576 | tf_op jit(solution)/shard_map/all_to_all | solution.py:534
  66.5 10.8 %all-to-all-done.1.back_ref = bf16[16,128,128]{2,1,0:T(8,128)(2,1)S(1)} async-done(((bf16[16,128,128]{2,1,0:T(8,128)(2,1)}), bf16[16,128,128]{2,1,0:T(8,128)(2,1)S(1)}, u32[]{:S(2)}, u32[]{:S(2)}) %all-to-all-start.1) | async-done | bytes 524320 | tf_op jit(solution)/shard_map/all_to_all | solution.py:534
  77.3 0.1 shard_map.136
  77.4 0.1 collective-permute-start.5
  77.5 0.1 pad_add_fusion.1.place_ref
  78.2 0.0 copy-done.8
  78.3 6.9 %collective-permute-done.5 = bf16[64,128]{1,0:T(8,128)(2,1)S(1)} collective-permute-done((bf16[64,128]{1,0:T(8,128)(2,1)S(1)}, bf16[64,128]{1,0:T(8,128)(2,1)S(1)}, u32[]{:S(2)}, u32[]{:S(2)}) %collective-permute-start.5) | collective-permute-done | bytes 16416 | tf_op jit(solution)/shard_map/ppermute | solution.py:536
  85.2 2.4 %collective-permute-start.6 = (bf16[64,128]{1,0:T(8,128)(2,1)S(1)}, bf16[64,128]{1,0:T(8,128)(2,1)S(1)}, u32[]{:S(2)}, u32[]{:S(2)}) collective-permute-start(bf16[64,128]{1,0:T(8,128)(2,1)S(1)} %get-tuple-element.18.now_ref), channel_id=1, source_target_pairs={{0,16},{16,32},{32,48},{48,64},{64,80},{80,96},{96,112},{112,128},... | collective-permute-start | bytes 49160 | tf_op jit(solution)/shard_map/ppermute | solution.py:480
  87.6 0.1 reshape.36
  87.7 0.6 copy.16
  88.4 5.1 %collective-permute-done.6.before_ref = bf16[64,128]{1,0:T(8,128)(2,1)S(1)} collective-permute-done((bf16[64,128]{1,0:T(8,128)(2,1)S(1)}, bf16[64,128]{1,0:T(8,128)(2,1)S(1)}, u32[]{:S(2)}, u32[]{:S(2)}) %collective-permute-start.6) | collective-permute-done | bytes 16416 | tf_op jit(solution)/shard_map/ppermute | solution.py:480
  93.5 0.0 copy-done.4
  93.5 6.7 %shard_map.137 = bf16[8,8,24,192]{3,2,1,0:T(8,128)(2,1)} custom-call(s32[3]{0:T(128)S(1)} %pad_add_fusion.1.place_ref, bf16[64,128]{1,0:T(8,128)(2,1)S(1)} %collective-permute-done.6.before_ref, bf16[64,128]{1,0:T(8,128)(2,1)S(1)} %get-tuple-element.18.now_ref, bf16[432,384]{1,0:T(8,128)(2,1)S(1)} %bitcast.26, f32[1,384]{1,0:T(1,128)S(1)} %broadcast_in_dim.12.inlet_bias_ref, ...), custom_call_target="tpu_custom_call" | custom-call | tf_op jit(solution)/shard_map/pallas_call | solution.py:454
  (15 shorter events, 0.1 us)
Async XLA Ops:
  0.6 2.4 %copy-start.6 = (bf16[1,4,2,6,4096]{4,2,3,1,0:T(2,128)(2,1)S(1)}, bf16[1,4,2,6,4096]{4,2,3,1,0:T(2,128)(2,1)}, u32[]{:S(2)}) copy-start(bf16[1,4,2,6,4096]{4,2,3,1,0:T(2,128)(2,1)} %param.14) | copy-start | bytes 1179652
  0.6 2.6 %copy-start.2 = (bf16[4096,64]{0,1:T(8,128)(2,1)S(1)}, bf16[4096,64]{0,1:T(8,128)(2,1)}, u32[]{:S(2)}) copy-start(bf16[4096,64]{0,1:T(8,128)(2,1)} %param.17) | copy-start | bytes 1572868
  3.2 13.8 %copy-start.7 = (f32[1,4,2,6,64]{4,2,3,1,0:T(2,128)S(1)}, f32[1,4,2,6,64]{4,2,3,1,0:T(2,128)}, u32[]{:S(2)}) copy-start(f32[1,4,2,6,64]{4,2,3,1,0:T(2,128)} %param.15) | copy-start | bytes 36868
  5.6 23.4 %copy-start.5 = (bf16[3,3,384,192]{2,3,1,0:T(8,128)(2,1)S(1)}, bf16[3,3,384,192]{2,3,1,0:T(8,128)(2,1)}, u32[]{:S(2)}) copy-start(bf16[3,3,384,192]{2,3,1,0:T(8,128)(2,1)} %param.22) | copy-start | bytes 3981316
  5.6 40.8 %all-to-all-start = ((bf16[32,120,128]{2,1,0:T(8,128)(2,1)}), bf16[32,120,128]{2,1,0:T(8,128)(2,1)S(1)}, u32[]{:S(2)}, u32[]{:S(2)}) async-start(bf16[32,120,128]{2,1,0:T(8,128)(2,1)} %shard_map.131), calls=%async_computation | async-start | bytes 1966080 | tf_op jit(solution)/shard_map/all_to_all | solution.py:529
  17.1 5.0 %collective-permute-start = (f32[4,2,1,64]{3,1,2,0:T(2,128)S(1)}, f32[4,2,1,64]{3,1,2,0:T(2,128)S(1)}, u32[]{:S(2)}, u32[]{:S(2)}) collective-permute-start(f32[4,2,1,64]{3,1,2,0:T(2,128)S(1)} %get-tuple-element.22), channel_id=1, source_target_pairs={{0,4},{4,8},{8,12},{1,5},{5,9},{9,13},{2,6},{6,10},{10,14},{3,7},{... | collective-permute-start | bytes 6152 | tf_op jit(solution)/shard_map/ppermute | solution.py:491
  20.8 5.5 %collective-permute-start.1 = (f32[4,2,1,64]{3,1,2,0:T(2,128)S(1)}, f32[4,2,1,64]{3,1,2,0:T(2,128)S(1)}, u32[]{:S(2)}, u32[]{:S(2)}) collective-permute-start(f32[4,2,1,64]{3,1,2,0:T(2,128)S(1)} %get-tuple-element.23), channel_id=1, source_target_pairs={{4,0},{8,4},{12,8},{5,1},{9,5},{13,9},{6,2},{10,6},{14,10},{7,3},{... | collective-permute-start | bytes 6152 | tf_op jit(solution)/shard_map/ppermute | solution.py:493
  26.3 7.4 %collective-permute-start.2 = (f32[4,1,8,64]{3,1,2,0:T(1,128)S(1)}, f32[4,1,8,64]{3,1,2,0:T(1,128)S(1)}, u32[]{:S(2)}, u32[]{:S(2)}) collective-permute-start(f32[4,1,8,64]{3,1,2,0:T(1,128)S(1)} %get-tuple-element.20), channel_id=1, source_target_pairs={{0,1},{1,2},{2,3},{4,5},{5,6},{6,7},{8,9},{9,10},{10,11},{12,13},{... | collective-permute-start | bytes 24584 | tf_op jit(solution)/shard_map/ppermute | solution.py:491
  27.6 8.7 %collective-permute-start.3 = (f32[4,1,8,64]{3,1,2,0:T(1,128)S(1)}, f32[4,1,8,64]{3,1,2,0:T(1,128)S(1)}, u32[]{:S(2)}, u32[]{:S(2)}) collective-permute-start(f32[4,1,8,64]{3,1,2,0:T(1,128)S(1)} %get-tuple-element.21), channel_id=1, source_target_pairs={{1,0},{2,1},{3,2},{5,4},{6,5},{7,6},{9,8},{10,9},{11,10},{13,12},{... | collective-permute-start | bytes 24584 | tf_op jit(solution)/shard_map/ppermute | solution.py:493
  31.3 1.5 %copy-start.1 = (bf16[3,3,384,192]{3,2,1,0:T(8,128)(2,1)S(1)}, bf16[3,3,384,192]{3,2,1,0:T(8,128)(2,1)}, u32[]{:S(2)}) copy-start(bf16[3,3,384,192]{3,2,1,0:T(8,128)(2,1)} %copy.15.spatial_ref) | copy-start | bytes 3981316
  33.7 13.2 %copy-start = (bf16[1536,768]{1,0:T(8,128)(2,1)}, bf16[1536,768]{1,0:T(8,128)(2,1)S(1)}, u32[]{:S(2)}) copy-start(bf16[1536,768]{1,0:T(8,128)(2,1)S(1)} %shard_map.132.rest_1_.window_hbm) | copy-start | bytes 7077892
  46.9 12.9 %collective-permute-start.4 = (bf16[16,72,128]{2,1,0:T(8,128)(2,1)S(1)}, bf16[16,72,128]{2,1,0:T(8,128)(2,1)S(1)}, u32[]{:S(2)}, u32[]{:S(2)}) collective-permute-start(bf16[16,72,128]{2,1,0:T(8,128)(2,1)S(1)} %shard_map.133), channel_id=1, source_target_pairs={{0,50},{1,51},{2,48},{3,49},{4,54},{5,55},{6,52},{7,53},{8,58},{9,... | collective-permute-start | bytes 884744 | tf_op jit(solution)/shard_map/ppermute | solution.py:531
  59.8 18.5 %copy-start.8 = (f32[768]{0:T(1024)S(1)}, f32[768]{0:T(1024)}, u32[]{:S(2)}) copy-start(f32[768]{0:T(1024)} %param.21) | copy-start | bytes 9220
  59.8 18.5 %copy-start.9 = (f32[384]{0:T(512)S(1)}, f32[384]{0:T(512)}, u32[]{:S(2)}) copy-start(f32[384]{0:T(512)} %param.19) | copy-start | bytes 4612
  59.8 33.7 %copy-start.3 = (bf16[3,3,3,16,384]{4,3,2,1,0:T(8,128)(2,1)S(1)}, bf16[3,3,3,16,384]{4,3,2,1,0:T(8,128)(2,1)}, u32[]{:S(2)}) copy-start(bf16[3,3,3,16,384]{4,3,2,1,0:T(8,128)(2,1)} %param.18) | copy-start | bytes 995332
  59.8 33.7 %copy-start.4 = (f32[192]{0:T(256)S(1)}, f32[192]{0:T(256)}, u32[]{:S(2)}) copy-start(f32[192]{0:T(256)} %param.23) | copy-start | bytes 2308
  62.9 14.4 %all-to-all-start.1 = ((bf16[16,128,128]{2,1,0:T(8,128)(2,1)}), bf16[16,128,128]{2,1,0:T(8,128)(2,1)S(1)}, u32[]{:S(2)}, u32[]{:S(2)}) async-start(bf16[16,128,128]{2,1,0:T(8,128)(2,1)} %shard_map.135), calls=%async_computation.1 | async-start | bytes 1048576 | tf_op jit(solution)/shard_map/all_to_all | solution.py:534
  77.4 7.7 %collective-permute-start.5 = (bf16[64,128]{1,0:T(8,128)(2,1)S(1)}, bf16[64,128]{1,0:T(8,128)(2,1)S(1)}, u32[]{:S(2)}, u32[]{:S(2)}) collective-permute-start(bf16[64,128]{1,0:T(8,128)(2,1)S(1)} %get-tuple-element.17), channel_id=1, source_target_pairs={{0,2},{1,3},{2,0},{3,1},{4,6},{5,7},{6,4},{7,5},{8,10},{9,11},{10,... | collective-permute-start | bytes 49160 | tf_op jit(solution)/shard_map/ppermute | solution.py:536
  85.2 8.3 %collective-permute-start.6 = (bf16[64,128]{1,0:T(8,128)(2,1)S(1)}, bf16[64,128]{1,0:T(8,128)(2,1)S(1)}, u32[]{:S(2)}, u32[]{:S(2)}) collective-permute-start(bf16[64,128]{1,0:T(8,128)(2,1)S(1)} %get-tuple-element.18.now_ref), channel_id=1, source_target_pairs={{0,16},{16,32},{32,48},{48,64},{64,80},{80,96},{96,112},{112,128},... | collective-permute-start | bytes 49160 | tf_op jit(solution)/shard_map/ppermute | solution.py:480

commit v3 on v2

--- a/solution.py
+++ b/solution.py
@@ -45,30 +45,34 @@
     return [(groups[g][k], groups[g + 1][k]) for g in range(len(groups) - 1) for k in range(HEADS)]
 
 
-PREP_STEPS = 4
+PREP_STEPS = 2
 PREP_HEADS = HEADS // PREP_STEPS
 
 
 def prep_kernel(query_ref, key_ref, value_ref, weight_ref, out_ref):
     dims = (((1,), (1,)), ((), ()))
+    width = PREP_HEADS * HD
+    query = query_ref[0].reshape(OWN, width)
+    key = key_ref[0].reshape(OWN, width)
+    value = value_ref[0].reshape(OWN, width)
     for h in range(PREP_HEADS):
         lanes = slice(h * HD, (h + 1) * HD)
-        out_ref[h, 0:OWN, :] = query_ref[:, lanes]
-        out_ref[h, OWN : 2 * OWN, :] = key_ref[:, lanes]
+        out_ref[h, 0:OWN, :] = query[:, lanes]
+        out_ref[h, OWN : 2 * OWN, :] = key[:, lanes]
         folded = lax.dot_general(
-            value_ref[:, lanes], weight_ref[:, lanes], dims, preferred_element_type=jnp.float32
+            value[:, lanes], weight_ref[:, lanes], dims, preferred_element_type=jnp.float32
         )
         packed = jnp.concatenate([folded[: OWN // 2], folded[OWN // 2 :]], axis=1)
         out_ref[h, 2 * OWN : ROWS, :] = packed.astype(jnp.bfloat16)
 
 
-def token_rows(states):
-    return states.transpose(0, 1, 3, 2, 4).reshape(OWN, states.shape[-1])
+def own_order(states):
+    return pltpu.with_memory_space_constraint(states.transpose(0, 1, 3, 2, 4), pltpu.HBM)
 
 
 def prep(query, key, value, weight):
     width = PREP_HEADS * HD
-    tile = pl.BlockSpec((OWN, width), lambda i: (0, i))
+    tile = pl.BlockSpec((1, 4, 6, 2, width), lambda i: (0, 0, 0, 0, i))
     return pl.pallas_call(
         prep_kernel,
         grid=(PREP_STEPS,),
@@ -76,7 +80,7 @@
         in_specs=[tile, tile, tile, pl.BlockSpec((LAT, width), lambda i: (0, i))],
         out_specs=pl.BlockSpec((PREP_HEADS, ROWS, HD), lambda i: (i, 0, 0)),
         compiler_params=pltpu.CompilerParams(vmem_limit_bytes=16 * 1024 * 1024),
-    )(token_rows(query), token_rows(key), token_rows(value), weight.T)
+    )(own_order(query), own_order(key), own_order(value), pltpu.with_memory_space_constraint(weight.T, pltpu.HBM))
 
 
 def spread_values(packed, target):
@@ -123,7 +127,9 @@
     )(place, recv, *ready)
 
 
-def attend_here_kernel(place_ref, recv_ref, out_ref, max_ref, mix_ref, early_v, late_v):
+def attend_here_kernel(
+    place_ref, recv_ref, out_hbm, max_ref, mix_ref, early_v, late_v, packed_ref, grid_ref, out_ref, sem
+):
     early = place_ref[0]
     late = 16 - early
     spread_values(recv_ref[pl.ds(early, 16), 2 * OWN :, :], early_v)
@@ -143,10 +149,14 @@
         before = jnp.exp2(before - top).astype(jnp.bfloat16)
         mixed = jnp.dot(here, late_v[...], preferred_element_type=jnp.float32)
         mixed += jnp.dot(before, early_v[...], preferred_element_type=jnp.float32)
-        pack_result(mixed, out_ref, i * QB, QB)
+        pack_result(mixed, packed_ref, i * QB, QB)
         return carry
 
     lax.fori_loop(0, 16 // QB, late_block, 0)
+    pair = place_ref[2]
+    scatter_halo(packed_ref, grid_ref, out_ref, place_ref[3], pair)
+    copy = pltpu.make_async_copy(out_ref, out_hbm.at[pl.ds(8 - 8 * pair, 8)], sem)
+    copy.start()
 
     def early_block(i, carry):
         query = recv_ref[pl.ds(early + i * QB, QB), :OWN, :].reshape(QB * OWN, HD)
@@ -160,6 +170,16 @@
         return carry
 
     lax.fori_loop(0, 16 // QB, early_block, 0)
+    copy.wait()
+
+
+def halo_scratch():
+    return [
+        pltpu.VMEM((16, OWN // 2, HD), jnp.float32),
+        pltpu.VMEM((4, 2, 10, 8, HD), jnp.float32),
+        pltpu.VMEM((8, 128, HD), jnp.bfloat16),
+        pltpu.SemaphoreType.DMA,
+    ]
 
 
 def attend_here(place, recv):
@@ -168,13 +188,13 @@
     return pl.pallas_call(
         attend_here_kernel,
         out_shape=(
-            jax.ShapeDtypeStruct((16, OWN // 2, HD), jnp.float32),
+            pltpu.HBM((16, 128, HD), jnp.bfloat16),
             jax.ShapeDtypeStruct((tokens, HD), jnp.float32),
             jax.ShapeDtypeStruct((tokens, HD), jnp.float32),
         ),
         in_specs=[pl.BlockSpec(memory_space=pltpu.SMEM), vmem],
-        out_specs=(vmem, vmem, vmem),
-        scratch_shapes=[pltpu.VMEM((tokens, HD), jnp.bfloat16)] * 2,
+        out_specs=(pl.BlockSpec(memory_space=pltpu.HBM), vmem, vmem),
+        scratch_shapes=[pltpu.VMEM((tokens, HD), jnp.bfloat16)] * 2 + halo_scratch(),
         compiler_params=pltpu.CompilerParams(vmem_limit_bytes=VMEM_BYTES),
         cost_estimate=pl.CostEstimate(
             flops=4 * 3 * tokens * tokens * HD, bytes_accessed=4 << 20, transcendentals=3 * tokens * tokens
@@ -183,16 +203,14 @@
 
 
 def attend_prior_kernel(
-    place_ref, recv_ref, prior_ref, late_ref, max_ref, mix_ref, out_hbm, prior_v, packed_ref, grid_ref,
+    place_ref, recv_ref, prior_ref, max_ref, mix_ref, late_hbm, out_hbm, prior_v, packed_ref, grid_ref,
     out_ref, sem,
 ):
     early = place_ref[0]
-    late = 16 - early
     penalty = jnp.where(place_ref[1] > 0, 0.0, -1e30).astype(jnp.float32)
     spread_values(prior_ref[:, OWN:, :], prior_v)
     prior_k = prior_ref[:, :OWN, :].reshape(16 * OWN, HD)
     scale = fold_scale()
-    packed_ref[pl.ds(late, 16)] = late_ref[...]
 
     def block(i, carry):
         rows = pl.ds(i * PB * OWN, PB * OWN)
@@ -203,63 +221,53 @@
         before = jnp.exp2(before - top).astype(jnp.bfloat16)
         mixed = jnp.dot(before, prior_v[...], preferred_element_type=jnp.float32)
         mixed += mix_ref[rows, :] * jnp.exp2(old - top)
-        pack_result(mixed, packed_ref, early + i * PB, PB)
+        pack_result(mixed, packed_ref, i * PB, PB)
         return carry
 
     lax.fori_loop(0, 16 // PB, block, 0, unroll=True)
-    scatter_halo(place_ref, packed_ref, grid_ref, out_ref)
-    copy = pltpu.make_async_copy(out_ref, out_hbm, sem)
+    scatter_halo(packed_ref, grid_ref, out_ref, place_ref[3], 0)
+    copy = pltpu.make_async_copy(out_ref, out_hbm.at[pl.ds(8 * place_ref[2], 8)], sem)
     copy.start()
     copy.wait()
 
 
-def scatter_halo(place_ref, packed_ref, grid_ref, out_ref):
-    flip = place_ref[2]
-    high = place_ref[3]
+def scatter_halo(packed_ref, grid_ref, out_ref, high, flip):
     grid_ref[...] = jnp.zeros_like(grid_ref)
-    for a in range(2):
-        for b in range(2):
-            tile_high = b if a == 1 else jnp.where(flip > 0, 1 - b, b)
-            for core in range(2):
-                row = 2 * (2 * tile_high + core) + 1
-                for x in range(4):
-                    block = a * 16 + x * 4 + b * 2 + core
-                    for frame in range(2):
-                        for sub in range(2):
-                            line = packed_ref[block, pl.ds(frame * 12 + sub, 6, stride=2), :]
-                            grid_ref[a, x, frame, row + sub, 1:7, :] = line
-                            if x < 3:
-                                grid_ref[a, x + 1, frame, row + sub, 0:1, :] = line[5:6]
-                            if x > 0:
-                                grid_ref[a, x - 1, frame, row + sub, 7:8, :] = line[0:1]
-    for a in range(2):
-        for x in range(4):
-            for core in range(2):
-                for part in range(2):
-                    row = 2 * (2 * (high if part == 0 else 1 - high) + core)
-                    tile = grid_ref[a, x, :, pl.ds(row, 4), :, :].reshape(64, HD)
-                    out_ref[a * 8 + x * 2 + core, part * 64 : (part + 1) * 64, :] = tile.astype(
-                        jnp.bfloat16
-                    )
-
-
-def attend_prior(place, recv, prior, late, top, mix):
+    for b in range(2):
+        tile_high = b + flip * (1 - 2 * b)
+        for core in range(2):
+            row = 2 * (2 * tile_high + core) + 1
+            for x in range(4):
+                block = x * 4 + b * 2 + core
+                for frame in range(2):
+                    for sub in range(2):
+                        line = packed_ref[block, pl.ds(frame * 12 + sub, 6, stride=2), :]
+                        grid_ref[x, frame, row + sub, 1:7, :] = line
+                        if x < 3:
+                            grid_ref[x + 1, frame, row + sub, 0:1, :] = line[5:6]
+                        if x > 0:
+                            grid_ref[x - 1, frame, row + sub, 7:8, :] = line[0:1]
+    for x in range(4):
+        for core in range(2):
+            for part in range(2):
+                row = 2 * (2 * (high if part == 0 else 1 - high) + core)
+                tile = grid_ref[x, :, pl.ds(row, 4), :, :].reshape(64, HD)
+                out_ref[x * 2 + core, part * 64 : (part + 1) * 64, :] = tile.astype(jnp.bfloat16)
+
+
+def attend_prior(place, recv, prior, top, mix, sent):
     vmem = pl.BlockSpec(memory_space=pltpu.VMEM)
+    hbm = pl.BlockSpec(memory_space=pltpu.HBM)
     tokens = 16 * OWN
     return pl.pallas_call(
         attend_prior_kernel,
         out_shape=pltpu.HBM((16, 128, HD), jnp.bfloat16),
-        in_specs=[pl.BlockSpec(memory_space=pltpu.SMEM)] + [vmem] * 5,
-        out_specs=pl.BlockSpec(memory_space=pltpu.HBM),
-        scratch_shapes=[
-            pltpu.VMEM((tokens, HD), jnp.bfloat16),
-            pltpu.VMEM((HEADS, OWN // 2, HD), jnp.float32),
-            pltpu.VMEM((2, 4, 2, 10, 8, HD), jnp.float32),
-            pltpu.VMEM((16, 128, HD), jnp.bfloat16),
-            pltpu.SemaphoreType.DMA,
-        ],
+        in_specs=[pl.BlockSpec(memory_space=pltpu.SMEM)] + [vmem] * 4 + [hbm],
+        out_specs=hbm,
+        input_output_aliases={5: 0},
+        scratch_shapes=[pltpu.VMEM((tokens, HD), jnp.bfloat16)] + halo_scratch(),
         compiler_params=pltpu.CompilerParams(vmem_limit_bytes=VMEM_BYTES),
-    )(place, recv, prior, late, top, mix)
+    )(place, recv, prior, top, mix, sent)
 
 
 def sum_kernel(back_ref, own_ref, other_ref):
@@ -290,17 +298,18 @@
 
 
 def spread_inlet(inlet_ref, wide_ref):
-    wide_ref[...] = jnp.zeros_like(wide_ref)
+    blank = jnp.zeros((ZC, CH), jnp.bfloat16)
     for frame in range(3):
-        for b in range(3):
-            for e in range(3):
-                tap = inlet_ref[((frame * 3 + b) * 3 + e) * ZC : ((frame * 3 + b) * 3 + e + 1) * ZC, :]
-                for down in range(2):
-                    for right in range(2):
-                        u, v = b + down, e + right
-                        row = frame * 256 + (u // 2 * 2 + v // 2) * LAT + (u % 2 * 2 + v % 2) * ZC
-                        sub = 2 * down + right
-                        wide_ref[row : row + ZC, sub * CH : (sub + 1) * CH] = tap
+        for u in range(4):
+            for v in range(4):
+                row = frame * 256 + (u // 2 * 2 + v // 2) * LAT + (u % 2 * 2 + v % 2) * ZC
+                for sub in range(4):
+                    b, e = u - sub // 2, v - sub % 2
+                    tap = blank
+                    if 0 <= b < 3 and 0 <= e < 3:
+                        first = ((frame * 3 + b) * 3 + e) * ZC
+                        tap = inlet_ref[first : first + ZC, :]
+                    wide_ref[row : row + ZC, sub * CH : (sub + 1) * CH] = tap
 
 
 def window_kernel(spatial_ref, window_ref):
@@ -335,13 +344,14 @@
     )(spatial_weight)
 
 
+SPACE_START = (0, 96, 192, 256)
 WIN = 24
 
 
 def decode_kernel(
     place_ref, before_ref, now_ref, inlet_ref, inlet_bias_ref, time_hbm, time_bias_ref, window_hbm,
-    space_bias_ref, out_ref, patch_ref, feature_ref, time_in_ref, double_ref, shift_ref, space_in_ref,
-    low_ref, rest_ref, wide_ref, time_ref, window_ref, sems,
+    space_bias_ref, out_hbm, patch_ref, feature_ref, time_in_ref, double_ref, shift_ref, space_in_ref,
+    low_ref, rest_ref, wide_ref, time_ref, window_ref, out_ref, sems,
 ):
     time_copy = pltpu.make_async_copy(time_hbm, time_ref, sems.at[0])
     time_copy.start()
@@ -391,58 +401,71 @@
         if sub % 2 == 0:
             shift_ref[sub // 2, :103, :] = double_ref[sub, 1:104, :]
             shift_ref[sub // 2, 103:, :] = jnp.zeros((9, 2 * CH), jnp.float32)
-    for py in range(2):
-        for px in range(2):
-            for wy in range(2):
-                for wx in range(2):
-                    down, right = (py + wy) // 2, (px + wx) // 2
-                    alpha, beta = (py + wy) % 2, (px + wx) % 2
-                    for u in range(2):
-                        lanes = slice(u * CH, (u + 1) * CH)
-                        rows = slice(down * 8, down * 8 + 96)
-                        if right:
-                            value = shift_ref[alpha, rows, lanes]
-                        else:
-                            value = double_ref[2 * alpha + beta, rows, lanes]
-                        start = ((2 * py + px) * 2 + u) * 96
-                        piece = (2 * wy + wx) * CH
-                        space_in_ref[start : start + 96, piece : piece + CH] = value.astype(
-                            jnp.bfloat16
-                        )
-    window_copy.wait()
-    for py in range(2):
-        for px in range(2):
-            start = (2 * py + px) * 192
-            mixed = jnp.dot(
-                space_in_ref[start : start + 192, :], window_ref[...], preferred_element_type=jnp.float32
-            )
-            for oy in range(2):
-                for ox in range(2):
-                    column = 8 - 1 + 2 * px + ox
-                    out = 2 * oy + ox
-                    for ri in range(3):
-                        high = 4 * ri - 1 + 2 * py + oy
-                        if not 0 <= high < 8:
-                            continue
-                        for u in range(2):
-                            for t in range(4):
-                                row = u * 96 + t * WIN + ri * 8
-                                low = mixed[row : row + 8, out * 128 : (out + 1) * 128]
-                                rest = mixed[row : row + 8, (4 + oy) * 128 : (5 + oy) * 128]
-                                if ox:
-                                    rest = pltpu.roll(rest, 64, 1)
-                                spot = pl.ds(column, 8, stride=4)
-                                low_ref[(2 * t + u) * 8 + high, spot, :] = low
-                                rest_ref[(2 * t + u) * 8 + high, spot, :] = rest
     low_bias = space_bias_ref[:, :128]
     rest_bias = space_bias_ref[:, 128:]
-    for frame in range(8):
-        for high in range(8):
-            line = frame * 8 + high
-            out_ref[frame, high, :, :128] = (low_ref[line, 8:32, :] + low_bias).astype(jnp.bfloat16)
-            out_ref[frame, high, :, 128:] = (rest_ref[line, 8:32, :LAT] + rest_bias).astype(
-                jnp.bfloat16
-            )
+    copies = []
+    for half in range(2):
+        for py in range(2):
+            for px in range(2):
+                start = SPACE_START[2 * py + px]
+                for wy in range(2):
+                    for wx in range(2):
+                        alpha, beta = (py + wy) % 2, (px + wx) % 2
+                        ref = shift_ref.at[alpha] if px + wx == 2 else double_ref.at[2 * alpha + beta]
+                        piece = slice((2 * wy + wx) * CH, (2 * wy + wx + 1) * CH)
+                        for u in range(2):
+                            lanes = slice(u * CH, (u + 1) * CH)
+                            if py == 0:
+                                spans = [(half * 2 * WIN, start + u * 2 * WIN, 2 * WIN)]
+                            else:
+                                spans = [
+                                    ((half * 2 + t) * WIN + wy * 8, start + (u * 2 + t) * 16, 16)
+                                    for t in range(2)
+                                ]
+                            for source, target, rows in spans:
+                                space_in_ref[half, target : target + rows, piece] = ref[
+                                    source : source + rows, lanes
+                                ].astype(jnp.bfloat16)
+        if half == 0:
+            window_copy.wait()
+        mixed = jnp.dot(space_in_ref[half], window_ref[...], preferred_element_type=jnp.float32)
+        for py in range(2):
+            for px in range(2):
+                for oy in range(2):
+                    for ox in range(2):
+                        column = 8 - 1 + 2 * px + ox
+                        out = 2 * oy + ox
+                        for ri in range(3 - py):
+                            high = 4 * ri - 1 + 2 * py + oy
+                            if not 0 <= high < 8:
+                                continue
+                            for u in range(2):
+                                for t in range(2):
+                                    row = SPACE_START[2 * py + px] + ri * 8
+                                    row += (u * 2 + t) * (WIN if py == 0 else 16)
+                                    low = mixed[row : row + 8, out * 128 : (out + 1) * 128]
+                                    rest = mixed[row : row + 8, (4 + oy) * 128 : (5 + oy) * 128]
+                                    if ox:
+                                        rest = pltpu.roll(rest, 64, 1)
+                                    spot = pl.ds(column, 8, stride=4)
+                                    line = (2 * (half * 2 + t) + u) * 8 + high
+                                    low_ref[line, spot, :] = low
+                                    rest_ref[line, spot, :] = rest
+        for frame in range(half * 4, half * 4 + 4):
+            for high in range(8):
+                line = frame * 8 + high
+                out_ref[frame, high, :, :128] = (low_ref[line, 8:32, :] + low_bias).astype(
+                    jnp.bfloat16
+                )
+                out_ref[frame, high, :, 128:] = (rest_ref[line, 8:32, :LAT] + rest_bias).astype(
+                    jnp.bfloat16
+                )
+        frames = pl.ds(half * 4, 4)
+        copy = pltpu.make_async_copy(out_ref.at[frames], out_hbm.at[frames], sems.at[2 + half])
+        copy.start()
+        copies.append(copy)
+    for copy in copies:
+        copy.wait()
 
 
 def decode(place, before, now, inlet, inlet_bias, time_weight, time_bias, window, space_bias):
@@ -453,22 +476,23 @@
     window = pltpu.with_memory_space_constraint(window, pltpu.HBM)
     return pl.pallas_call(
         decode_kernel,
-        out_shape=jax.ShapeDtypeStruct((8, 8, 24, OC), bf16),
+        out_shape=pltpu.HBM((8, 8, 24, OC), bf16),
         in_specs=[pl.BlockSpec(memory_space=pltpu.SMEM)] + [vmem] * 4 + [hbm, vmem, hbm, vmem],
-        out_specs=vmem,
+        out_specs=hbm,
         scratch_shapes=[
             pltpu.VMEM((8 * WIN, 256), f32),
             pltpu.VMEM((6 * WIN, 4 * CH), f32),
             pltpu.VMEM((384, 3 * CH), bf16),
             pltpu.VMEM((4, 112, 2 * CH), f32),
             pltpu.VMEM((2, 112, 2 * CH), f32),
-            pltpu.VMEM((768, 4 * CH), bf16),
+            pltpu.VMEM((2, 320, 4 * CH), bf16),
             pltpu.VMEM((64, 40, 128), f32),
             pltpu.VMEM((64, 40, 128), f32),
             pltpu.VMEM((768, 4 * CH), bf16),
             pltpu.VMEM((3 * CH, 2 * CH), bf16),
             pltpu.VMEM((4 * CH, 4 * OC), bf16),
-            pltpu.SemaphoreType.DMA((2,)),
+            pltpu.VMEM((8, 8, 24, OC), bf16),
+            pltpu.SemaphoreType.DMA((4,)),
         ],
         compiler_params=pltpu.CompilerParams(vmem_limit_bytes=VMEM_BYTES),
     )(place, before, now, inlet, inlet_bias, time_weight, time_bias, window, space_bias)
@@ -529,8 +553,8 @@
     recv = lax.all_to_all(sent, AXES, 0, 0, tiled=True, axis_index_groups=groups)
     late_kv = late_part(place, recv, (halo_noisy, window))
     prior = lax.ppermute(late_kv, AXES, prior_route(groups))
-    late, top, mix = attend_here(place, recv)
-    partial = attend_prior(place, recv, prior, late, top, mix)
+    partial, top, mix = attend_here(place, recv)
+    partial = attend_prior(place, recv, prior, top, mix, partial)
     back = lax.all_to_all(partial, AXES, 0, 0, tiled=True, axis_index_groups=half_groups(groups))
     own, other = sum_heads(back)
     other = lax.ppermute(other, "tile", [(0, 2), (1, 3), (2, 0), (3, 1)])

time: 101 us -> 98 us (0.970)
  local copies, waits for them, and re-layouts: 7.2 us -> 4.65 us
    reshape x3 -> x0, local copies, waits for them, and re-layouts: 2.52 us -> none  [token_rows(): return states.transpose(0, 1, 3, 2, 4).reshape(OWN, states.shape[-1])]
  transfers between devices with their start and end apart: 9 -> 9, of which waited for: 7 -> 7; matrix products, arithmetic and copies ran while one was open for 3% -> 3% of each run, Pallas kernels for 4% -> 5%
where the time goes in v3:
time: 98 us; the launch traced here: 97.5 us
  waiting for transfers between devices  46.6 us (48%)
  starting transfers between devices  27.1 us (28%)
  Pallas kernels  17.3 us (18%)
  local copies, waits for them, and re-layouts  4.65 us (5%)
  between operations  1.58 us (2%)
    all_to_all x1, starting transfers between devices, shards(): lax.all_to_all(sent, AXES, 0, 0, tiled=True, axis_index_groups=groups)  11.5 us
    all_to_all x1, waiting for transfers between devices, shards(): lax.all_to_all(partial, AXES, 0, 0, tiled=True, axis_index_groups=half_gr...  10.8 us
    all_to_all x1, waiting for transfers between devices, shards(): lax.all_to_all(sent, AXES, 0, 0, tiled=True, axis_index_groups=groups)  9.79 us
    ppermute x1, waiting for transfers between devices, shards(): prior = lax.ppermute(late_kv, AXES, prior_route(groups))  7.22 us
    ppermute x1, waiting for transfers between devices, shards(): other = lax.ppermute(other, 'tile', [(0, 2), (1, 3), (2, 0), (3, 1)])  6.86 us
    ppermute x2, waiting for transfers between devices, with_halo(): lax.ppermute(head, axis, [((i + 1) % count, i) for i in range(ends)])  6.76 us
    pallas_call x1, Pallas kernels, decode(): pl.pallas_call(decode_kernel, out_shape=pltpu.HBM((8, 8, 24, OC), bf16),...  6 us
    ppermute x1, waiting for transfers between devices, shifted(): return lax.ppermute(block, axis, route)  5.14 us
  transfers between devices with their start and end apart: 9, of which 7 were waited for; matrix products, arithmetic and copies ran while one was open for 3% of the time, Pallas kernels for 5%

profile of v3, /device:TPU:16, one launch (start us, length us, event | category | flops | bytes accessed | tf_op | source)
XLA Modules:
  0.0 97.5 jit_solution(11609076978021692646)
XLA Ops:
  0.6 0.0 copy-start.5
  0.6 3.1 %shard_map.131 = bf16[32,120,128]{2,1,0:T(8,128)(2,1)} custom-call(bf16[1,4,6,2,4096]{4,3,2,1,0:T(2,128)(2,1)} %bitcast.30, bf16[1,4,6,2,4096]{4,3,2,1,0:T(2,128)(2,1)} %bitcast.31, bf16[1,4,6,2,4096]{4,3,2,1,0:T(2,128)(2,1)} %bitcast.32, bf16[64,4096]{1,0:T(8,128)(2,1)} %bitcast.29), custom_call_target="tpu_custom_call" | custom-call | tf_op jit(solution)/shard_map/pallas_call | solution.py:76
  3.8 0.0 copy-start.4
  3.8 11.5 %all-to-all-start = ((bf16[32,120,128]{2,1,0:T(8,128)(2,1)}), bf16[32,120,128]{2,1,0:T(8,128)(2,1)S(1)}, u32[]{:S(2)}, u32[]{:S(2)}) async-start(bf16[32,120,128]{2,1,0:T(8,128)(2,1)} %shard_map.131), calls=%async_computation | async-start | bytes 1966080 | tf_op jit(solution)/shard_map/all_to_all | solution.py:553
  15.2 0.0 copy-done.5
  15.2 3.7 %collective-permute-start = (f32[4,2,1,64]{3,1,2,0:T(2,128)S(1)}, f32[4,2,1,64]{3,1,2,0:T(2,128)S(1)}, u32[]{:S(2)}, u32[]{:S(2)}) collective-permute-start(f32[4,2,1,64]{3,1,2,0:T(2,128)S(1)} %get-tuple-element.22), channel_id=1, source_target_pairs={{0,4},{4,8},{8,12},{1,5},{5,9},{9,13},{2,6},{6,10},{10,14},{3,7},{... | collective-permute-start | bytes 6152 | tf_op jit(solution)/shard_map/ppermute | solution.py:515
  18.9 1.3 %collective-permute-start.1 = (f32[4,2,1,64]{3,1,2,0:T(2,128)S(1)}, f32[4,2,1,64]{3,1,2,0:T(2,128)S(1)}, u32[]{:S(2)}, u32[]{:S(2)}) collective-permute-start(f32[4,2,1,64]{3,1,2,0:T(2,128)S(1)} %get-tuple-element.23), channel_id=1, source_target_pairs={{4,0},{8,4},{12,8},{5,1},{9,5},{13,9},{6,2},{10,6},{14,10},{7,3},{... | collective-permute-start | bytes 6152 | tf_op jit(solution)/shard_map/ppermute | solution.py:517
  20.3 0.0 collective-permute-done
  20.3 4.1 %collective-permute-done.1 = f32[4,2,1,64]{3,1,2,0:T(2,128)S(1)} collective-permute-done((f32[4,2,1,64]{3,1,2,0:T(2,128)S(1)}, f32[4,2,1,64]{3,1,2,0:T(2,128)S(1)}, u32[]{:S(2)}, u32[]{:S(2)}) %collective-permute-start.1) | collective-permute-done | bytes 2080 | tf_op jit(solution)/shard_map/ppermute | solution.py:517
  24.5 1.3 %collective-permute-start.2 = (f32[4,1,8,64]{3,1,2,0:T(1,128)S(1)}, f32[4,1,8,64]{3,1,2,0:T(1,128)S(1)}, u32[]{:S(2)}, u32[]{:S(2)}) collective-permute-start(f32[4,1,8,64]{3,1,2,0:T(1,128)S(1)} %get-tuple-element.20), channel_id=1, source_target_pairs={{0,1},{1,2},{2,3},{4,5},{5,6},{6,7},{8,9},{9,10},{10,11},{12,13},{... | collective-permute-start | bytes 24584 | tf_op jit(solution)/shard_map/ppermute | solution.py:515
  25.8 1.3 %collective-permute-start.3 = (f32[4,1,8,64]{3,1,2,0:T(1,128)S(1)}, f32[4,1,8,64]{3,1,2,0:T(1,128)S(1)}, u32[]{:S(2)}, u32[]{:S(2)}) collective-permute-start(f32[4,1,8,64]{3,1,2,0:T(1,128)S(1)} %get-tuple-element.21), channel_id=1, source_target_pairs={{1,0},{2,1},{3,2},{5,4},{6,5},{7,6},{9,8},{10,9},{11,10},{13,12},{... | collective-permute-start | bytes 24584 | tf_op jit(solution)/shard_map/ppermute | solution.py:517
  27.1 0.1 pad_add_fusion.place_ref
  27.2 0.0 copy-done.4
  27.2 2.2 %copy.16.spatial_ref = bf16[3,3,384,192]{3,2,1,0:T(8,128)(2,1)} copy(bf16[3,3,384,192]{2,3,1,0:T(8,128)(2,1)S(1)} %copy-done.4) | data formatting | bytes 2654208 | tf_op jit(solution)/shard_map/optimization_barrier | solution.py:547
  29.4 0.0 copy-start.1
  29.4 1.5 %copy-done.1 = bf16[3,3,384,192]{3,2,1,0:T(8,128)(2,1)S(1)} copy-done((bf16[3,3,384,192]{3,2,1,0:T(8,128)(2,1)S(1)}, bf16[3,3,384,192]{3,2,1,0:T(8,128)(2,1)}, u32[]{:S(2)}) %copy-start.1) | copy-done | bytes 1327128
  30.9 1.0 shard_map.132.rest_1_.window_hbm
  31.9 0.0 copy-start
  31.9 0.0 collective-permute-done.2
  31.9 2.6 %collective-permute-done.3 = f32[4,1,8,64]{3,1,2,0:T(1,128)S(1)} collective-permute-done((f32[4,1,8,64]{3,1,2,0:T(1,128)S(1)}, f32[4,1,8,64]{3,1,2,0:T(1,128)S(1)}, u32[]{:S(2)}, u32[]{:S(2)}) %collective-permute-start.3) | collective-permute-done | bytes 8224 | tf_op jit(solution)/shard_map/ppermute | solution.py:517
  34.5 0.1 pad_maximum_fusion
  34.5 0.1 copy.19
  34.6 0.1 reshape.23.rest_0_
  34.7 9.8 %all-to-all-done.recv_ref = bf16[32,120,128]{2,1,0:T(8,128)(2,1)S(1)} async-done(((bf16[32,120,128]{2,1,0:T(8,128)(2,1)}), bf16[32,120,128]{2,1,0:T(8,128)(2,1)S(1)}, u32[]{:S(2)}, u32[]{:S(2)}) %all-to-all-start) | async-done | bytes 983072 | tf_op jit(solution)/shard_map/all_to_all | solution.py:553
  44.5 0.6 shard_map.133
  45.1 0.0 copy-done
  45.1 1.9 %collective-permute-start.4 = (bf16[16,72,128]{2,1,0:T(8,128)(2,1)S(1)}, bf16[16,72,128]{2,1,0:T(8,128)(2,1)S(1)}, u32[]{:S(2)}, u32[]{:S(2)}) collective-permute-start(bf16[16,72,128]{2,1,0:T(8,128)(2,1)S(1)} %shard_map.133), channel_id=1, source_target_pairs={{0,50},{1,51},{2,48},{3,49},{4,54},{5,55},{6,52},{7,53},{8,58},{9,... | collective-permute-start | bytes 884744 | tf_op jit(solution)/shard_map/ppermute | solution.py:555
  47.0 3.7 %shard_map.134 = (bf16[16,128,128]{2,1,0:T(8,128)(2,1)}, f32[768,128]{1,0:T(8,128)S(1)}, f32[768,128]{1,0:T(8,128)S(1)}) custom-call(s32[4]{0:T(128)S(1)} %pad_add_fusion.place_ref, bf16[32,120,128]{2,1,0:T(8,128)(2,1)S(1)} %all-to-all-done.recv_ref), custom_call_target="tpu_custom_call" | custom-call | flops 905969664 | bytes 4194304 | tf_op jit(solution)/shard_map/pallas_call | solution.py:188
  50.7 7.2 %collective-permute-done.4.prior_ref = bf16[16,72,128]{2,1,0:T(8,128)(2,1)S(1)} collective-permute-done((bf16[16,72,128]{2,1,0:T(8,128)(2,1)S(1)}, bf16[16,72,128]{2,1,0:T(8,128)(2,1)S(1)}, u32[]{:S(2)}, u32[]{:S(2)}) %collective-permute-start.4) | collective-permute-done | bytes 294944 | tf_op jit(solution)/shard_map/ppermute | solution.py:555
  58.0 0.0 copy-start.6
  58.0 0.0 copy-start.7
  58.0 0.0 copy-start.2
  58.0 2.9 %shard_map.135 = bf16[16,128,128]{2,1,0:T(8,128)(2,1)} custom-call(s32[4]{0:T(128)S(1)} %pad_add_fusion.place_ref, bf16[32,120,128]{2,1,0:T(8,128)(2,1)S(1)} %all-to-all-done.recv_ref, bf16[16,72,128]{2,1,0:T(8,128)(2,1)S(1)} %collective-permute-done.4.prior_ref, f32[768,128]{1,0:T(8,128)S(1)} %get-tuple-element.13.max_ref, ...), custom_call_target="tpu_custom_call", output_to_operand_aliasing={{}: (5, {})} | custom-call | tf_op jit(solution)/shard_map/pallas_call | solution.py:262
  60.9 3.6 %all-to-all-start.1 = ((bf16[16,128,128]{2,1,0:T(8,128)(2,1)}), bf16[16,128,128]{2,1,0:T(8,128)(2,1)S(1)}, u32[]{:S(2)}, u32[]{:S(2)}) async-start(bf16[16,128,128]{2,1,0:T(8,128)(2,1)} %shard_map.135), calls=%async_computation.1 | async-start | bytes 1048576 | tf_op jit(solution)/shard_map/all_to_all | solution.py:558
  64.5 10.8 %all-to-all-done.1.back_ref = bf16[16,128,128]{2,1,0:T(8,128)(2,1)S(1)} async-done(((bf16[16,128,128]{2,1,0:T(8,128)(2,1)}), bf16[16,128,128]{2,1,0:T(8,128)(2,1)S(1)}, u32[]{:S(2)}, u32[]{:S(2)}) %all-to-all-start.1) | async-done | bytes 524320 | tf_op jit(solution)/shard_map/all_to_all | solution.py:558
  75.3 0.1 shard_map.136
  75.4 0.1 collective-permute-start.5
  75.5 0.1 pad_add_fusion.1.place_ref
  76.2 0.0 copy-done.6
  76.3 0.0 copy-done.7
  76.3 6.9 %collective-permute-done.5 = bf16[64,128]{1,0:T(8,128)(2,1)S(1)} collective-permute-done((bf16[64,128]{1,0:T(8,128)(2,1)S(1)}, bf16[64,128]{1,0:T(8,128)(2,1)S(1)}, u32[]{:S(2)}, u32[]{:S(2)}) %collective-permute-start.5) | collective-permute-done | bytes 16416 | tf_op jit(solution)/shard_map/ppermute | solution.py:560
  83.1 2.4 %collective-permute-start.6 = (bf16[64,128]{1,0:T(8,128)(2,1)S(1)}, bf16[64,128]{1,0:T(8,128)(2,1)S(1)}, u32[]{:S(2)}, u32[]{:S(2)}) collective-permute-start(bf16[64,128]{1,0:T(8,128)(2,1)S(1)} %get-tuple-element.18.now_ref), channel_id=1, source_target_pairs={{0,16},{16,32},{32,48},{48,64},{64,80},{80,96},{96,112},{112,128},... | collective-permute-start | bytes 49160 | tf_op jit(solution)/shard_map/ppermute | solution.py:504
  85.6 0.1 reshape.24
  85.7 0.6 copy.17
  86.3 5.1 %collective-permute-done.6.before_ref = bf16[64,128]{1,0:T(8,128)(2,1)S(1)} collective-permute-done((bf16[64,128]{1,0:T(8,128)(2,1)S(1)}, bf16[64,128]{1,0:T(8,128)(2,1)S(1)}, u32[]{:S(2)}, u32[]{:S(2)}) %collective-permute-start.6) | collective-permute-done | bytes 16416 | tf_op jit(solution)/shard_map/ppermute | solution.py:504
  91.5 0.0 copy-done.2
  91.5 0.0 copy-done.3
  91.5 6.0 %shard_map.137 = bf16[8,8,24,192]{3,2,1,0:T(8,128)(2,1)} custom-call(s32[3]{0:T(128)S(1)} %pad_add_fusion.1.place_ref, bf16[64,128]{1,0:T(8,128)(2,1)S(1)} %collective-permute-done.6.before_ref, bf16[64,128]{1,0:T(8,128)(2,1)S(1)} %get-tuple-element.18.now_ref, bf16[432,384]{1,0:T(8,128)(2,1)S(1)} %bitcast.25, f32[1,384]{1,0:T(1,128)S(1)} %broadcast_in_dim.12.inlet_bias_ref, ...), custom_call_target="tpu_custom_call" | custom-call | tf_op jit(solution)/shard_map/pallas_call | solution.py:477
  (8 shorter events, 0.1 us)
Async XLA Ops:
  0.6 14.6 %copy-start.5 = (f32[1,4,2,6,64]{4,2,3,1,0:T(2,128)S(1)}, f32[1,4,2,6,64]{4,2,3,1,0:T(2,128)}, u32[]{:S(2)}) copy-start(f32[1,4,2,6,64]{4,2,3,1,0:T(2,128)} %param.15) | copy-start | bytes 36868
  3.8 23.4 %copy-start.4 = (bf16[3,3,384,192]{2,3,1,0:T(8,128)(2,1)S(1)}, bf16[3,3,384,192]{2,3,1,0:T(8,128)(2,1)}, u32[]{:S(2)}) copy-start(bf16[3,3,384,192]{2,3,1,0:T(8,128)(2,1)} %param.22) | copy-start | bytes 3981316
  3.8 40.8 %all-to-all-start = ((bf16[32,120,128]{2,1,0:T(8,128)(2,1)}), bf16[32,120,128]{2,1,0:T(8,128)(2,1)S(1)}, u32[]{:S(2)}, u32[]{:S(2)}) async-start(bf16[32,120,128]{2,1,0:T(8,128)(2,1)} %shard_map.131), calls=%async_computation | async-start | bytes 1966080 | tf_op jit(solution)/shard_map/all_to_all | solution.py:553
  15.2 5.0 %collective-permute-start = (f32[4,2,1,64]{3,1,2,0:T(2,128)S(1)}, f32[4,2,1,64]{3,1,2,0:T(2,128)S(1)}, u32[]{:S(2)}, u32[]{:S(2)}) collective-permute-start(f32[4,2,1,64]{3,1,2,0:T(2,128)S(1)} %get-tuple-element.22), channel_id=1, source_target_pairs={{0,4},{4,8},{8,12},{1,5},{5,9},{9,13},{2,6},{6,10},{10,14},{3,7},{... | collective-permute-start | bytes 6152 | tf_op jit(solution)/shard_map/ppermute | solution.py:515
  18.9 5.5 %collective-permute-start.1 = (f32[4,2,1,64]{3,1,2,0:T(2,128)S(1)}, f32[4,2,1,64]{3,1,2,0:T(2,128)S(1)}, u32[]{:S(2)}, u32[]{:S(2)}) collective-permute-start(f32[4,2,1,64]{3,1,2,0:T(2,128)S(1)} %get-tuple-element.23), channel_id=1, source_target_pairs={{4,0},{8,4},{12,8},{5,1},{9,5},{13,9},{6,2},{10,6},{14,10},{7,3},{... | collective-permute-start | bytes 6152 | tf_op jit(solution)/shard_map/ppermute | solution.py:517
  24.5 7.4 %collective-permute-start.2 = (f32[4,1,8,64]{3,1,2,0:T(1,128)S(1)}, f32[4,1,8,64]{3,1,2,0:T(1,128)S(1)}, u32[]{:S(2)}, u32[]{:S(2)}) collective-permute-start(f32[4,1,8,64]{3,1,2,0:T(1,128)S(1)} %get-tuple-element.20), channel_id=1, source_target_pairs={{0,1},{1,2},{2,3},{4,5},{5,6},{6,7},{8,9},{9,10},{10,11},{12,13},{... | collective-permute-start | bytes 24584 | tf_op jit(solution)/shard_map/ppermute | solution.py:515
  25.8 8.7 %collective-permute-start.3 = (f32[4,1,8,64]{3,1,2,0:T(1,128)S(1)}, f32[4,1,8,64]{3,1,2,0:T(1,128)S(1)}, u32[]{:S(2)}, u32[]{:S(2)}) collective-permute-start(f32[4,1,8,64]{3,1,2,0:T(1,128)S(1)} %get-tuple-element.21), channel_id=1, source_target_pairs={{1,0},{2,1},{3,2},{5,4},{6,5},{7,6},{9,8},{10,9},{11,10},{13,12},{... | collective-permute-start | bytes 24584 | tf_op jit(solution)/shard_map/ppermute | solution.py:517
  29.4 1.5 %copy-start.1 = (bf16[3,3,384,192]{3,2,1,0:T(8,128)(2,1)S(1)}, bf16[3,3,384,192]{3,2,1,0:T(8,128)(2,1)}, u32[]{:S(2)}) copy-start(bf16[3,3,384,192]{3,2,1,0:T(8,128)(2,1)} %copy.16.spatial_ref) | copy-start | bytes 3981316
  31.9 13.2 %copy-start = (bf16[1536,768]{1,0:T(8,128)(2,1)}, bf16[1536,768]{1,0:T(8,128)(2,1)S(1)}, u32[]{:S(2)}) copy-start(bf16[1536,768]{1,0:T(8,128)(2,1)S(1)} %shard_map.132.rest_1_.window_hbm) | copy-start | bytes 7077892
  45.1 12.9 %collective-permute-start.4 = (bf16[16,72,128]{2,1,0:T(8,128)(2,1)S(1)}, bf16[16,72,128]{2,1,0:T(8,128)(2,1)S(1)}, u32[]{:S(2)}, u32[]{:S(2)}) collective-permute-start(bf16[16,72,128]{2,1,0:T(8,128)(2,1)S(1)} %shard_map.133), channel_id=1, source_target_pairs={{0,50},{1,51},{2,48},{3,49},{4,54},{5,55},{6,52},{7,53},{8,58},{9,... | collective-permute-start | bytes 884744 | tf_op jit(solution)/shard_map/ppermute | solution.py:555
  58.0 18.3 %copy-start.6 = (f32[768]{0:T(1024)S(1)}, f32[768]{0:T(1024)}, u32[]{:S(2)}) copy-start(f32[768]{0:T(1024)} %param.21) | copy-start | bytes 9220
  58.0 18.3 %copy-start.7 = (f32[384]{0:T(512)S(1)}, f32[384]{0:T(512)}, u32[]{:S(2)}) copy-start(f32[384]{0:T(512)} %param.19) | copy-start | bytes 4612
  58.0 33.5 %copy-start.2 = (bf16[3,3,3,16,384]{4,3,2,1,0:T(8,128)(2,1)S(1)}, bf16[3,3,3,16,384]{4,3,2,1,0:T(8,128)(2,1)}, u32[]{:S(2)}) copy-start(bf16[3,3,3,16,384]{4,3,2,1,0:T(8,128)(2,1)} %param.18) | copy-start | bytes 995332
  58.0 33.5 %copy-start.3 = (f32[192]{0:T(256)S(1)}, f32[192]{0:T(256)}, u32[]{:S(2)}) copy-start(f32[192]{0:T(256)} %param.23) | copy-start | bytes 2308
  60.9 14.4 %all-to-all-start.1 = ((bf16[16,128,128]{2,1,0:T(8,128)(2,1)}), bf16[16,128,128]{2,1,0:T(8,128)(2,1)S(1)}, u32[]{:S(2)}, u32[]{:S(2)}) async-start(bf16[16,128,128]{2,1,0:T(8,128)(2,1)} %shard_map.135), calls=%async_computation.1 | async-start | bytes 1048576 | tf_op jit(solution)/shard_map/all_to_all | solution.py:558
  75.4 7.7 %collective-permute-start.5 = (bf16[64,128]{1,0:T(8,128)(2,1)S(1)}, bf16[64,128]{1,0:T(8,128)(2,1)S(1)}, u32[]{:S(2)}, u32[]{:S(2)}) collective-permute-start(bf16[64,128]{1,0:T(8,128)(2,1)S(1)} %get-tuple-element.17), channel_id=1, source_target_pairs={{0,2},{1,3},{2,0},{3,1},{4,6},{5,7},{6,4},{7,5},{8,10},{9,11},{10,... | collective-permute-start | bytes 49160 | tf_op jit(solution)/shard_map/ppermute | solution.py:560
  83.1 8.3 %collective-permute-start.6 = (bf16[64,128]{1,0:T(8,128)(2,1)S(1)}, bf16[64,128]{1,0:T(8,128)(2,1)S(1)}, u32[]{:S(2)}, u32[]{:S(2)}) collective-permute-start(bf16[64,128]{1,0:T(8,128)(2,1)S(1)} %get-tuple-element.18.now_ref), channel_id=1, source_target_pairs={{0,16},{16,32},{32,48},{48,64},{64,80},{80,96},{96,112},{112,128},... | collective-permute-start | bytes 49160 | tf_op jit(solution)/shard_map/ppermute | solution.py:504

commit v4 on v3

--- a/solution.py
+++ b/solution.py
@@ -39,6 +39,18 @@
 
 def half_groups(groups):
     return [[d for d in group if d // 2 % 2 == high] for group in groups for high in range(2)]
+
+
+ACROSS = [(0, 2), (1, 3), (2, 0), (3, 1)]
+
+
+def span_route(turn):
+    return [
+        ((span * 4 + x) * 4 + tile, ((span + 1) * 4 + x) * 4 + (tile + turn) % 4)
+        for span in range(15)
+        for x in range(4)
+        for tile in range(4)
+    ]
 
 
 def prior_route(groups):
@@ -270,26 +282,29 @@
     )(place, recv, prior, top, mix, sent)
 
 
-def sum_kernel(back_ref, own_ref, other_ref):
+def sum_kernel(level_ref, back_ref, noisy_ref, own_ref, own_sent_ref, other_ref):
     total = back_ref[0].astype(jnp.float32)
     for k in range(1, 16):
         total += back_ref[k].astype(jnp.float32)
-    own_ref[...] = total[:64]
-    other_ref[...] = total[64:].astype(jnp.bfloat16)
-
-
-def sum_heads(back):
+    own = noisy_ref[...] - level_ref[0] * total[:64]
+    own_ref[...] = own
+    own_sent_ref[...] = own.astype(jnp.bfloat16)
+    other_ref[...] = (-level_ref[0] * total[64:]).astype(jnp.bfloat16)
+
+
+def sum_heads(level, back, noisy):
     vmem = pl.BlockSpec(memory_space=pltpu.VMEM)
     return pl.pallas_call(
         sum_kernel,
         out_shape=(
             jax.ShapeDtypeStruct((64, HD), jnp.float32),
             jax.ShapeDtypeStruct((64, HD), jnp.bfloat16),
+            jax.ShapeDtypeStruct((64, HD), jnp.bfloat16),
         ),
-        in_specs=[vmem],
-        out_specs=(vmem, vmem),
+        in_specs=[pl.BlockSpec(memory_space=pltpu.SMEM), vmem, vmem],
+        out_specs=(vmem, vmem, vmem),
         compiler_params=pltpu.CompilerParams(vmem_limit_bytes=4 * 1024 * 1024),
-    )(back)
+    )(level, back, noisy)
 
 
 CH = 384
@@ -310,6 +325,41 @@
                         first = ((frame * 3 + b) * 3 + e) * ZC
                         tap = inlet_ref[first : first + ZC, :]
                     wide_ref[row : row + ZC, sub * CH : (sub + 1) * CH] = tap
+
+
+def ready_kernel(inlet_ref, time_hbm, window_hbm, order_ref, wide_ref, time_ref, window_ref, sems):
+    copies = (
+        pltpu.make_async_copy(time_hbm, time_ref, sems.at[0]),
+        pltpu.make_async_copy(window_hbm, window_ref, sems.at[1]),
+    )
+    for copy in copies:
+        copy.start()
+    spread_inlet(inlet_ref, wide_ref)
+    for copy in copies:
+        copy.wait()
+
+
+def ready_weights(inlet, time_weight, window, order):
+    vmem = pl.BlockSpec(memory_space=pltpu.VMEM)
+    hbm = pl.BlockSpec(memory_space=pltpu.HBM)
+    return pl.pallas_call(
+        ready_kernel,
+        out_shape=(
+            pltpu.VMEM((768, 4 * CH), jnp.bfloat16),
+            pltpu.VMEM((3 * CH, 2 * CH), jnp.bfloat16),
+            pltpu.VMEM((4 * CH, 4 * OC), jnp.bfloat16),
+        ),
+        in_specs=[vmem, hbm, hbm, pl.BlockSpec(memory_space=pl.ANY)],
+        out_specs=(vmem, vmem, vmem),
+        scratch_shapes=[pltpu.SemaphoreType.DMA((2,))],
+        compiler_params=pltpu.CompilerParams(vmem_limit_bytes=12 * 1024 * 1024),
+        cost_estimate=pl.CostEstimate(flops=4 << 20, bytes_accessed=8 << 20, transcendentals=0),
+    )(
+        inlet,
+        pltpu.with_memory_space_constraint(time_weight, pltpu.HBM),
+        pltpu.with_memory_space_constraint(window, pltpu.HBM),
+        order,
+    )
 
 
 def window_kernel(spatial_ref, window_ref):
@@ -349,18 +399,14 @@
 
 
 def decode_kernel(
-    place_ref, before_ref, now_ref, inlet_ref, inlet_bias_ref, time_hbm, time_bias_ref, window_hbm,
+    place_ref, before_own_ref, before_other_ref, own_ref, other_ref, wide_ref, inlet_bias_ref, time_ref, time_bias_ref, window_ref,
     space_bias_ref, out_hbm, patch_ref, feature_ref, time_in_ref, double_ref, shift_ref, space_in_ref,
-    low_ref, rest_ref, wide_ref, time_ref, window_ref, out_ref, sems,
+    low_ref, rest_ref, out_ref, sems,
 ):
-    time_copy = pltpu.make_async_copy(time_hbm, time_ref, sems.at[0])
-    time_copy.start()
-    window_copy = pltpu.make_async_copy(window_hbm, window_ref, sems.at[1])
-    window_copy.start()
     has_prior, tile, head = place_ref[0], place_ref[1], place_ref[2]
-    spread_inlet(inlet_ref, wide_ref)
-    for half, ref in enumerate((before_ref, now_ref)):
-        cells = ref[...].astype(jnp.float32)
+    for half, (one_ref, two_ref) in enumerate(((before_own_ref, before_other_ref), (own_ref, other_ref))):
+        cells = one_ref[...].astype(jnp.float32) + two_ref[...].astype(jnp.float32)
+        cells = cells.astype(jnp.bfloat16).astype(jnp.float32)
         after = jnp.concatenate([cells[1:], cells[:1]], axis=0)
         for part in range(2):
             lanes = slice(part * LAT, (part + 1) * LAT)
@@ -384,7 +430,6 @@
             time_in_ref[sub * 96 : (sub + 1) * 96, a * CH : (a + 1) * CH] = feature_ref[
                 a * WIN : a * WIN + 96, sub * CH : (sub + 1) * CH
             ].astype(jnp.bfloat16)
-    time_copy.wait()
     doubled = jnp.dot(time_in_ref[...], time_ref[...], preferred_element_type=jnp.float32)
     place = lax.broadcasted_iota(jnp.int32, (96, 1), 0)
     window_row = lax.rem(place, WIN) // 8
@@ -426,8 +471,6 @@
                                 space_in_ref[half, target : target + rows, piece] = ref[
                                     source : source + rows, lanes
                                 ].astype(jnp.bfloat16)
-        if half == 0:
-            window_copy.wait()
         mixed = jnp.dot(space_in_ref[half], window_ref[...], preferred_element_type=jnp.float32)
         for py in range(2):
             for px in range(2):
@@ -461,23 +504,24 @@
                     jnp.bfloat16
                 )
         frames = pl.ds(half * 4, 4)
-        copy = pltpu.make_async_copy(out_ref.at[frames], out_hbm.at[frames], sems.at[2 + half])
+        copy = pltpu.make_async_copy(out_ref.at[frames], out_hbm.at[frames], sems.at[half])
         copy.start()
         copies.append(copy)
     for copy in copies:
         copy.wait()
 
 
-def decode(place, before, now, inlet, inlet_bias, time_weight, time_bias, window, space_bias):
+def decode(place, before_own, before_other, own, other, wide, inlet_bias, time_weight, time_bias, window, space_bias):
     vmem = pl.BlockSpec(memory_space=pltpu.VMEM)
     hbm = pl.BlockSpec(memory_space=pltpu.HBM)
     f32, bf16 = jnp.float32, jnp.bfloat16
-    time_weight = pltpu.with_memory_space_constraint(time_weight, pltpu.HBM)
-    window = pltpu.with_memory_space_constraint(window, pltpu.HBM)
+    wide, time_weight, window = (
+        pltpu.with_memory_space_constraint(weight, pltpu.VMEM) for weight in (wide, time_weight, window)
+    )
     return pl.pallas_call(
         decode_kernel,
         out_shape=pltpu.HBM((8, 8, 24, OC), bf16),
-        in_specs=[pl.BlockSpec(memory_space=pltpu.SMEM)] + [vmem] * 4 + [hbm, vmem, hbm, vmem],
+        in_specs=[pl.BlockSpec(memory_space=pltpu.SMEM)] + [vmem] * 10,
         out_specs=hbm,
         scratch_shapes=[
             pltpu.VMEM((8 * WIN, 256), f32),
@@ -488,20 +532,11 @@
             pltpu.VMEM((2, 320, 4 * CH), bf16),
             pltpu.VMEM((64, 40, 128), f32),
             pltpu.VMEM((64, 40, 128), f32),
-            pltpu.VMEM((768, 4 * CH), bf16),
-            pltpu.VMEM((3 * CH, 2 * CH), bf16),
-            pltpu.VMEM((4 * CH, 4 * OC), bf16),
             pltpu.VMEM((8, 8, 24, OC), bf16),
-            pltpu.SemaphoreType.DMA((4,)),
+            pltpu.SemaphoreType.DMA((2,)),
         ],
         compiler_params=pltpu.CompilerParams(vmem_limit_bytes=VMEM_BYTES),
-    )(place, before, now, inlet, inlet_bias, time_weight, time_bias, window, space_bias)
-
-
-def shifted(block, axis, distance):
-    devices = range(lax.axis_size(axis))
-    route = [(i - distance, i) for i in devices if i - distance in devices]
-    return lax.ppermute(block, axis, route)
+    )(place, before_own, before_other, own, other, wide, inlet_bias, time_weight, time_bias, window, space_bias)
 
 
 def with_halo(cells, sides, width):
@@ -556,22 +591,26 @@
     partial, top, mix = attend_here(place, recv)
     partial = attend_prior(place, recv, prior, top, mix, partial)
     back = lax.all_to_all(partial, AXES, 0, 0, tiled=True, axis_index_groups=half_groups(groups))
-    own, other = sum_heads(back)
-    other = lax.ppermute(other, "tile", [(0, 2), (1, 3), (2, 0), (3, 1)])
-    velocity = own + other.astype(jnp.float32)
-    clean = halo_noisy - noise_level[0] * velocity
-    latent = clean.astype(jnp.bfloat16)
-    before = shifted(latent, "grp", 1)
+    own, own_sent, other_sent = sum_heads(noise_level, back, halo_noisy)
+    across = lax.ppermute(other_sent, "tile", ACROSS)
+    before_other = lax.ppermute(other_sent, AXES, span_route(2))
+    before_own = lax.ppermute(own_sent, AXES, span_route(0))
+    clean = own + across.astype(jnp.float32)
     clean_latent = clean.reshape(2, 4, 8, 2, LAT)[:, 1:3, 1:7].transpose(3, 0, 1, 2, 4)
     clean_latent = clean_latent.reshape(noisy_latent.shape)
+    wide, time_ready, window = ready_weights(
+        inlet_weight.reshape(27 * ZC, CH), temporal_weight.reshape(3 * CH, 2 * CH), window, clean_latent
+    )
     where = jnp.stack([has_prior.astype(jnp.int32), lax.axis_index("tile"), lax.axis_index("head")])
     decoded = decode(
         where,
-        before,
-        latent,
-        inlet_weight.reshape(27 * ZC, CH),
+        before_own,
+        before_other,
+        own,
+        across,
+        wide,
         inlet_bias[None],
-        temporal_weight.reshape(3 * CH, 2 * CH),
+        time_ready,
         temporal_bias[None],
         window,
         spatial_bias[None],

time: 98 us -> 96 us (0.980)
  waiting for transfers between devices: 46.6 us -> 37.4 us
  starting transfers between devices: 27.1 us -> 33.6 us
    ppermute x2 -> x3, waiting for transfers between devices: 12 us -> 3.39 us  [the longest x1 3.38 us: shards(): before_own = lax.ppermute(own_sent, AXES, span_route(0))]
    ppermute x2 -> x3, starting transfers between devices: 2.54 us -> 8.92 us  [the longest x1 6.9 us: shards(): before_other = lax.ppermute(other_sent, AXES, span_route(2))]
    pallas_call x0 -> x1, Pallas kernels: none -> 2.23 us  [ready_weights(): pl.pallas_call(ready_kernel, out_shape=(pltpu.VMEM((768, 4 * CH), jnp.bfl...]
    pallas_call x1, Pallas kernels: 6 us -> 4.53 us  [decode(): pl.pallas_call(decode_kernel, out_shape=pltpu.HBM((8, 8, 24, OC), bf16),...]
    unnamed x16 -> x17, local copies, waits for them, and re-layouts: 1.5 us -> 2.13 us
  transfers between devices with their start and end apart: 9 -> 10, of which waited for: 7 -> 6; matrix products, arithmetic and copies ran while one was open for 3% -> 4% of each run, Pallas kernels for 5% -> 7%
where the time goes in v4:
time: 96 us; the launch traced here: 95.5 us
  waiting for transfers between devices  37.4 us (39%)
  starting transfers between devices  33.6 us (35%)
  Pallas kernels  18.1 us (19%)
  local copies, waits for them, and re-layouts  4.65 us (5%)
  between operations  1.6 us (2%)
    all_to_all x1, starting transfers between devices, shards(): lax.all_to_all(sent, AXES, 0, 0, tiled=True, axis_index_groups=groups)  11.5 us
    all_to_all x1, waiting for transfers between devices, shards(): lax.all_to_all(partial, AXES, 0, 0, tiled=True, axis_index_groups=half_gr...  10.2 us
    all_to_all x1, waiting for transfers between devices, shards(): lax.all_to_all(sent, AXES, 0, 0, tiled=True, axis_index_groups=groups)  9.79 us
    ppermute x1, waiting for transfers between devices, shards(): prior = lax.ppermute(late_kv, AXES, prior_route(groups))  7.24 us
    ppermute x1, starting transfers between devices, shards(): before_other = lax.ppermute(other_sent, AXES, span_route(2))  6.9 us
    ppermute x2, waiting for transfers between devices, with_halo(): lax.ppermute(head, axis, [((i + 1) % count, i) for i in range(ends)])  6.77 us
    ppermute x2, starting transfers between devices, with_halo(): lax.ppermute(tail, axis, [(i, (i + 1) % count) for i in range(ends)])  4.99 us
    pallas_call x1, Pallas kernels, decode(): pl.pallas_call(decode_kernel, out_shape=pltpu.HBM((8, 8, 24, OC), bf16),...  4.53 us
  transfers between devices with their start and end apart: 10, of which 6 were waited for; matrix products, arithmetic and copies ran while one was open for 4% of the time, Pallas kernels for 7%

profile of v4, /device:TPU:16, one launch (start us, length us, event | category | flops | bytes accessed | tf_op | source)
XLA Modules:
  0.0 95.5 jit_solution(810912881500049038)
XLA Ops:
  0.6 0.0 copy-start.5
  0.6 3.1 %shard_map.131 = bf16[32,120,128]{2,1,0:T(8,128)(2,1)} custom-call(bf16[1,4,6,2,4096]{4,3,2,1,0:T(2,128)(2,1)} %bitcast.30, bf16[1,4,6,2,4096]{4,3,2,1,0:T(2,128)(2,1)} %bitcast.31, bf16[1,4,6,2,4096]{4,3,2,1,0:T(2,128)(2,1)} %bitcast.32, bf16[64,4096]{1,0:T(8,128)(2,1)} %bitcast.29), custom_call_target="tpu_custom_call" | custom-call | tf_op jit(solution)/shard_map/pallas_call | solution.py:88
  3.7 0.0 copy-start.4
  3.8 11.5 %all-to-all-start = ((bf16[32,120,128]{2,1,0:T(8,128)(2,1)}), bf16[32,120,128]{2,1,0:T(8,128)(2,1)S(1)}, u32[]{:S(2)}, u32[]{:S(2)}) async-start(bf16[32,120,128]{2,1,0:T(8,128)(2,1)} %shard_map.131), calls=%async_computation | async-start | bytes 1966080 | tf_op jit(solution)/shard_map/all_to_all | solution.py:588
  15.2 0.0 copy-done.5
  15.2 3.7 %collective-permute-start = (f32[4,2,1,64]{3,1,2,0:T(2,128)S(1)}, f32[4,2,1,64]{3,1,2,0:T(2,128)S(1)}, u32[]{:S(2)}, u32[]{:S(2)}) collective-permute-start(f32[4,2,1,64]{3,1,2,0:T(2,128)S(1)} %get-tuple-element.30), channel_id=1, source_target_pairs={{0,4},{4,8},{8,12},{1,5},{5,9},{9,13},{2,6},{6,10},{10,14},{3,7},{... | collective-permute-start | bytes 6152 | tf_op jit(solution)/shard_map/ppermute | solution.py:550
  18.9 1.3 %collective-permute-start.1 = (f32[4,2,1,64]{3,1,2,0:T(2,128)S(1)}, f32[4,2,1,64]{3,1,2,0:T(2,128)S(1)}, u32[]{:S(2)}, u32[]{:S(2)}) collective-permute-start(f32[4,2,1,64]{3,1,2,0:T(2,128)S(1)} %get-tuple-element.31), channel_id=1, source_target_pairs={{4,0},{8,4},{12,8},{5,1},{9,5},{13,9},{6,2},{10,6},{14,10},{7,3},{... | collective-permute-start | bytes 6152 | tf_op jit(solution)/shard_map/ppermute | solution.py:552
  20.3 0.0 collective-permute-done
  20.3 4.1 %collective-permute-done.1 = f32[4,2,1,64]{3,1,2,0:T(2,128)S(1)} collective-permute-done((f32[4,2,1,64]{3,1,2,0:T(2,128)S(1)}, f32[4,2,1,64]{3,1,2,0:T(2,128)S(1)}, u32[]{:S(2)}, u32[]{:S(2)}) %collective-permute-start.1) | collective-permute-done | bytes 2080 | tf_op jit(solution)/shard_map/ppermute | solution.py:552
  24.5 1.3 %collective-permute-start.2 = (f32[4,1,8,64]{3,1,2,0:T(1,128)S(1)}, f32[4,1,8,64]{3,1,2,0:T(1,128)S(1)}, u32[]{:S(2)}, u32[]{:S(2)}) collective-permute-start(f32[4,1,8,64]{3,1,2,0:T(1,128)S(1)} %get-tuple-element.28), channel_id=1, source_target_pairs={{0,1},{1,2},{2,3},{4,5},{5,6},{6,7},{8,9},{9,10},{10,11},{12,13},{... | collective-permute-start | bytes 24584 | tf_op jit(solution)/shard_map/ppermute | solution.py:550
  25.8 1.3 %collective-permute-start.3 = (f32[4,1,8,64]{3,1,2,0:T(1,128)S(1)}, f32[4,1,8,64]{3,1,2,0:T(1,128)S(1)}, u32[]{:S(2)}, u32[]{:S(2)}) collective-permute-start(f32[4,1,8,64]{3,1,2,0:T(1,128)S(1)} %get-tuple-element.29), channel_id=1, source_target_pairs={{1,0},{2,1},{3,2},{5,4},{6,5},{7,6},{9,8},{10,9},{11,10},{13,12},{... | collective-permute-start | bytes 24584 | tf_op jit(solution)/shard_map/ppermute | solution.py:552
  27.1 0.1 pad_add_fusion.place_ref
  27.2 0.0 copy-done.4
  27.2 2.2 %copy.16.spatial_ref = bf16[3,3,384,192]{3,2,1,0:T(8,128)(2,1)} copy(bf16[3,3,384,192]{2,3,1,0:T(8,128)(2,1)S(1)} %copy-done.4) | data formatting | bytes 2654208 | tf_op jit(solution)/shard_map/optimization_barrier | solution.py:582
  29.4 1.5 %copy-done.1 = bf16[3,3,384,192]{3,2,1,0:T(8,128)(2,1)S(1)} copy-done((bf16[3,3,384,192]{3,2,1,0:T(8,128)(2,1)S(1)}, bf16[3,3,384,192]{3,2,1,0:T(8,128)(2,1)}, u32[]{:S(2)}) %copy-start.1) | copy-done | bytes 1327128
  30.9 1.0 %shard_map.132.rest_1_.window_hbm = bf16[1536,768]{1,0:T(8,128)(2,1)S(1)} custom-call(bf16[3,3,384,192]{3,2,1,0:T(8,128)(2,1)S(1)} %copy-done.1), custom_call_target="tpu_custom_call" | custom-call | flops 4194304 | bytes 4194304 | tf_op jit(solution)/shard_map/pallas_call | solution.py:387
  31.8 0.0 copy-start
  31.9 0.0 collective-permute-done.2
  31.9 2.6 %collective-permute-done.3 = f32[4,1,8,64]{3,1,2,0:T(1,128)S(1)} collective-permute-done((f32[4,1,8,64]{3,1,2,0:T(1,128)S(1)}, f32[4,1,8,64]{3,1,2,0:T(1,128)S(1)}, u32[]{:S(2)}, u32[]{:S(2)}) %collective-permute-start.3) | collective-permute-done | bytes 8224 | tf_op jit(solution)/shard_map/ppermute | solution.py:552
  34.5 0.1 pad_maximum_fusion
  34.5 0.1 copy.20
  34.6 0.1 reshape.23.rest_0_.noisy_ref
  34.7 9.8 %all-to-all-done.recv_ref = bf16[32,120,128]{2,1,0:T(8,128)(2,1)S(1)} async-done(((bf16[32,120,128]{2,1,0:T(8,128)(2,1)}), bf16[32,120,128]{2,1,0:T(8,128)(2,1)S(1)}, u32[]{:S(2)}, u32[]{:S(2)}) %all-to-all-start) | async-done | bytes 983072 | tf_op jit(solution)/shard_map/all_to_all | solution.py:588
  44.5 0.6 shard_map.133
  45.1 0.0 copy-done
  45.1 1.9 %collective-permute-start.4 = (bf16[16,72,128]{2,1,0:T(8,128)(2,1)S(1)}, bf16[16,72,128]{2,1,0:T(8,128)(2,1)S(1)}, u32[]{:S(2)}, u32[]{:S(2)}) collective-permute-start(bf16[16,72,128]{2,1,0:T(8,128)(2,1)S(1)} %shard_map.133), channel_id=1, source_target_pairs={{0,50},{1,51},{2,48},{3,49},{4,54},{5,55},{6,52},{7,53},{8,58},{9,... | collective-permute-start | bytes 884744 | tf_op jit(solution)/shard_map/ppermute | solution.py:590
  47.0 3.7 %shard_map.134 = (bf16[16,128,128]{2,1,0:T(8,128)(2,1)}, f32[768,128]{1,0:T(8,128)S(1)}, f32[768,128]{1,0:T(8,128)S(1)}) custom-call(s32[4]{0:T(128)S(1)} %pad_add_fusion.place_ref, bf16[32,120,128]{2,1,0:T(8,128)(2,1)S(1)} %all-to-all-done.recv_ref), custom_call_target="tpu_custom_call" | custom-call | flops 905969664 | bytes 4194304 | tf_op jit(solution)/shard_map/pallas_call | solution.py:200
  50.7 7.2 %collective-permute-done.4.prior_ref = bf16[16,72,128]{2,1,0:T(8,128)(2,1)S(1)} collective-permute-done((bf16[16,72,128]{2,1,0:T(8,128)(2,1)S(1)}, bf16[16,72,128]{2,1,0:T(8,128)(2,1)S(1)}, u32[]{:S(2)}, u32[]{:S(2)}) %collective-permute-start.4) | collective-permute-done | bytes 294944 | tf_op jit(solution)/shard_map/ppermute | solution.py:590
  58.0 2.9 %shard_map.135 = bf16[16,128,128]{2,1,0:T(8,128)(2,1)} custom-call(s32[4]{0:T(128)S(1)} %pad_add_fusion.place_ref, bf16[32,120,128]{2,1,0:T(8,128)(2,1)S(1)} %all-to-all-done.recv_ref, bf16[16,72,128]{2,1,0:T(8,128)(2,1)S(1)} %collective-permute-done.4.prior_ref, f32[768,128]{1,0:T(8,128)S(1)} %get-tuple-element.17.max_ref, ...), custom_call_target="tpu_custom_call", output_to_operand_aliasing={{}: (5, {})} | custom-call | tf_op jit(solution)/shard_map/pallas_call | solution.py:274
  60.9 0.0 copy-start.2
  60.9 3.7 %all-to-all-start.1 = ((bf16[16,128,128]{2,1,0:T(8,128)(2,1)}), bf16[16,128,128]{2,1,0:T(8,128)(2,1)S(1)}, u32[]{:S(2)}, u32[]{:S(2)}) async-start(bf16[16,128,128]{2,1,0:T(8,128)(2,1)} %shard_map.135), calls=%async_computation.1 | async-start | bytes 1048576 | tf_op jit(solution)/shard_map/all_to_all | solution.py:593
  65.3 10.2 %all-to-all-done.1.back_ref = bf16[16,128,128]{2,1,0:T(8,128)(2,1)S(1)} async-done(((bf16[16,128,128]{2,1,0:T(8,128)(2,1)}), bf16[16,128,128]{2,1,0:T(8,128)(2,1)S(1)}, u32[]{:S(2)}, u32[]{:S(2)}) %all-to-all-start.1) | async-done | bytes 524320 | tf_op jit(solution)/shard_map/all_to_all | solution.py:593
  75.4 0.1 shard_map.136
  75.5 0.1 collective-permute-start.5
  75.6 0.1 pad_add_fusion.1.place_ref
  75.7 0.0 copy-done.6
  75.7 0.0 copy-done.7
  75.7 6.9 %collective-permute-start.7 = (bf16[64,128]{1,0:T(8,128)(2,1)S(1)}, bf16[64,128]{1,0:T(8,128)(2,1)S(1)}, u32[]{:S(2)}, u32[]{:S(2)}) collective-permute-start(bf16[64,128]{1,0:T(8,128)(2,1)S(1)} %get-tuple-element.21), channel_id=1, source_target_pairs={{0,18},{1,19},{2,16},{3,17},{4,22},{5,23},{6,20},{7,21},{8,26},{9,... | collective-permute-start | bytes 49160 | tf_op jit(solution)/shard_map/ppermute | solution.py:596
  82.6 1.9 %collective-permute-start.6 = (bf16[64,128]{1,0:T(8,128)(2,1)S(1)}, bf16[64,128]{1,0:T(8,128)(2,1)S(1)}, u32[]{:S(2)}, u32[]{:S(2)}) collective-permute-start(bf16[64,128]{1,0:T(8,128)(2,1)S(1)} %get-tuple-element.22), channel_id=1, source_target_pairs={{0,16},{1,17},{2,18},{3,19},{4,20},{5,21},{6,22},{7,23},{8,24},{9,... | collective-permute-start | bytes 49160 | tf_op jit(solution)/shard_map/ppermute | solution.py:597
  84.6 0.0 collective-permute-done.5.other_ref
  84.6 0.1 reshape.24
  84.7 0.6 copy.18
  85.3 0.0 copy-done.2
  85.3 2.2 %shard_map.137 = (bf16[768,1536]{1,0:T(8,128)(2,1)S(1)}, bf16[1152,768]{1,0:T(8,128)(2,1)S(1)}, bf16[1536,768]{1,0:T(8,128)(2,1)S(1)}) custom-call(bf16[432,384]{1,0:T(8,128)(2,1)S(1)} %bitcast.23, bf16[1152,768]{1,0:T(8,128)(2,1)} %bitcast.27, bf16[1536,768]{1,0:T(8,128)(2,1)} %copy-done, f32[1,4,2,6,64]{4,3,2,1,0:T(8,128)S(1)} %bitcast.25), custom_call_target="tpu_custom_call" | custom-call | flops 4194304 | bytes 8388608 | tf_op jit(solution)/shard_map/pallas_call | solution.py:345
  87.6 3.4 %collective-permute-done.6.before_own_ref = bf16[64,128]{1,0:T(8,128)(2,1)S(1)} collective-permute-done((bf16[64,128]{1,0:T(8,128)(2,1)S(1)}, bf16[64,128]{1,0:T(8,128)(2,1)S(1)}, u32[]{:S(2)}, u32[]{:S(2)}) %collective-permute-start.6) | collective-permute-done | bytes 16416 | tf_op jit(solution)/shard_map/ppermute | solution.py:597
  91.0 0.0 collective-permute-done.7.before_other_ref
  91.0 0.0 copy-done.3
  91.0 4.5 %shard_map.138 = bf16[8,8,24,192]{3,2,1,0:T(8,128)(2,1)} custom-call(s32[3]{0:T(128)S(1)} %pad_add_fusion.1.place_ref, bf16[64,128]{1,0:T(8,128)(2,1)S(1)} %collective-permute-done.6.before_own_ref, bf16[64,128]{1,0:T(8,128)(2,1)S(1)} %collective-permute-done.7.before_other_ref, f32[64,128]{1,0:T(8,128)S(1)} %get-tuple-element.20.own_ref, ...), custom_call_target="tpu_custom_call" | custom-call | tf_op jit(solution)/shard_map/pallas_call | solution.py:521
  (12 shorter events, 0.1 us)
Async XLA Ops:
  0.6 14.6 %copy-start.5 = (f32[1,4,2,6,64]{4,2,3,1,0:T(2,128)S(1)}, f32[1,4,2,6,64]{4,2,3,1,0:T(2,128)}, u32[]{:S(2)}) copy-start(f32[1,4,2,6,64]{4,2,3,1,0:T(2,128)} %param.15) | copy-start | bytes 36868
  3.7 23.4 %copy-start.4 = (bf16[3,3,384,192]{2,3,1,0:T(8,128)(2,1)S(1)}, bf16[3,3,384,192]{2,3,1,0:T(8,128)(2,1)}, u32[]{:S(2)}) copy-start(bf16[3,3,384,192]{2,3,1,0:T(8,128)(2,1)} %param.22) | copy-start | bytes 3981316
  3.8 40.8 %all-to-all-start = ((bf16[32,120,128]{2,1,0:T(8,128)(2,1)}), bf16[32,120,128]{2,1,0:T(8,128)(2,1)S(1)}, u32[]{:S(2)}, u32[]{:S(2)}) async-start(bf16[32,120,128]{2,1,0:T(8,128)(2,1)} %shard_map.131), calls=%async_computation | async-start | bytes 1966080 | tf_op jit(solution)/shard_map/all_to_all | solution.py:588
  15.2 5.0 %collective-permute-start = (f32[4,2,1,64]{3,1,2,0:T(2,128)S(1)}, f32[4,2,1,64]{3,1,2,0:T(2,128)S(1)}, u32[]{:S(2)}, u32[]{:S(2)}) collective-permute-start(f32[4,2,1,64]{3,1,2,0:T(2,128)S(1)} %get-tuple-element.30), channel_id=1, source_target_pairs={{0,4},{4,8},{8,12},{1,5},{5,9},{9,13},{2,6},{6,10},{10,14},{3,7},{... | collective-permute-start | bytes 6152 | tf_op jit(solution)/shard_map/ppermute | solution.py:550
  18.9 5.5 %collective-permute-start.1 = (f32[4,2,1,64]{3,1,2,0:T(2,128)S(1)}, f32[4,2,1,64]{3,1,2,0:T(2,128)S(1)}, u32[]{:S(2)}, u32[]{:S(2)}) collective-permute-start(f32[4,2,1,64]{3,1,2,0:T(2,128)S(1)} %get-tuple-element.31), channel_id=1, source_target_pairs={{4,0},{8,4},{12,8},{5,1},{9,5},{13,9},{6,2},{10,6},{14,10},{7,3},{... | collective-permute-start | bytes 6152 | tf_op jit(solution)/shard_map/ppermute | solution.py:552
  24.5 7.4 %collective-permute-start.2 = (f32[4,1,8,64]{3,1,2,0:T(1,128)S(1)}, f32[4,1,8,64]{3,1,2,0:T(1,128)S(1)}, u32[]{:S(2)}, u32[]{:S(2)}) collective-permute-start(f32[4,1,8,64]{3,1,2,0:T(1,128)S(1)} %get-tuple-element.28), channel_id=1, source_target_pairs={{0,1},{1,2},{2,3},{4,5},{5,6},{6,7},{8,9},{9,10},{10,11},{12,13},{... | collective-permute-start | bytes 24584 | tf_op jit(solution)/shard_map/ppermute | solution.py:550
  25.8 8.7 %collective-permute-start.3 = (f32[4,1,8,64]{3,1,2,0:T(1,128)S(1)}, f32[4,1,8,64]{3,1,2,0:T(1,128)S(1)}, u32[]{:S(2)}, u32[]{:S(2)}) collective-permute-start(f32[4,1,8,64]{3,1,2,0:T(1,128)S(1)} %get-tuple-element.29), channel_id=1, source_target_pairs={{1,0},{2,1},{3,2},{5,4},{6,5},{7,6},{9,8},{10,9},{11,10},{13,12},{... | collective-permute-start | bytes 24584 | tf_op jit(solution)/shard_map/ppermute | solution.py:552
  29.4 1.5 %copy-start.1 = (bf16[3,3,384,192]{3,2,1,0:T(8,128)(2,1)S(1)}, bf16[3,3,384,192]{3,2,1,0:T(8,128)(2,1)}, u32[]{:S(2)}) copy-start(bf16[3,3,384,192]{3,2,1,0:T(8,128)(2,1)} %copy.16.spatial_ref) | copy-start | bytes 3981316
  31.8 13.2 %copy-start = (bf16[1536,768]{1,0:T(8,128)(2,1)}, bf16[1536,768]{1,0:T(8,128)(2,1)S(1)}, u32[]{:S(2)}) copy-start(bf16[1536,768]{1,0:T(8,128)(2,1)S(1)} %shard_map.132.rest_1_.window_hbm) | copy-start | bytes 7077892
  45.1 12.9 %collective-permute-start.4 = (bf16[16,72,128]{2,1,0:T(8,128)(2,1)S(1)}, bf16[16,72,128]{2,1,0:T(8,128)(2,1)S(1)}, u32[]{:S(2)}, u32[]{:S(2)}) collective-permute-start(bf16[16,72,128]{2,1,0:T(8,128)(2,1)S(1)} %shard_map.133), channel_id=1, source_target_pairs={{0,50},{1,51},{2,48},{3,49},{4,54},{5,55},{6,52},{7,53},{8,58},{9,... | collective-permute-start | bytes 884744 | tf_op jit(solution)/shard_map/ppermute | solution.py:590
  58.0 17.7 %copy-start.6 = (f32[768]{0:T(1024)S(1)}, f32[768]{0:T(1024)}, u32[]{:S(2)}) copy-start(f32[768]{0:T(1024)} %param.21) | copy-start | bytes 9220
  58.0 17.7 %copy-start.7 = (f32[384]{0:T(512)S(1)}, f32[384]{0:T(512)}, u32[]{:S(2)}) copy-start(f32[384]{0:T(512)} %param.19) | copy-start | bytes 4612
  60.9 24.5 %copy-start.2 = (bf16[3,3,3,16,384]{4,3,2,1,0:T(8,128)(2,1)S(1)}, bf16[3,3,3,16,384]{4,3,2,1,0:T(8,128)(2,1)}, u32[]{:S(2)}) copy-start(bf16[3,3,3,16,384]{4,3,2,1,0:T(8,128)(2,1)} %param.18) | copy-start | bytes 995332
  60.9 14.6 %all-to-all-start.1 = ((bf16[16,128,128]{2,1,0:T(8,128)(2,1)}), bf16[16,128,128]{2,1,0:T(8,128)(2,1)S(1)}, u32[]{:S(2)}, u32[]{:S(2)}) async-start(bf16[16,128,128]{2,1,0:T(8,128)(2,1)} %shard_map.135), calls=%async_computation.1 | async-start | bytes 1048576 | tf_op jit(solution)/shard_map/all_to_all | solution.py:593
  75.5 9.0 %collective-permute-start.5 = (bf16[64,128]{1,0:T(8,128)(2,1)S(1)}, bf16[64,128]{1,0:T(8,128)(2,1)S(1)}, u32[]{:S(2)}, u32[]{:S(2)}) collective-permute-start(bf16[64,128]{1,0:T(8,128)(2,1)S(1)} %get-tuple-element.21), channel_id=1, source_target_pairs={{0,2},{1,3},{2,0},{3,1},{4,6},{5,7},{6,4},{7,5},{8,10},{9,11},{10,... | collective-permute-start | bytes 49160 | tf_op jit(solution)/shard_map/ppermute | solution.py:595
  75.7 15.2 %collective-permute-start.7 = (bf16[64,128]{1,0:T(8,128)(2,1)S(1)}, bf16[64,128]{1,0:T(8,128)(2,1)S(1)}, u32[]{:S(2)}, u32[]{:S(2)}) collective-permute-start(bf16[64,128]{1,0:T(8,128)(2,1)S(1)} %get-tuple-element.21), channel_id=1, source_target_pairs={{0,18},{1,19},{2,16},{3,17},{4,22},{5,23},{6,20},{7,21},{8,26},{9,... | collective-permute-start | bytes 49160 | tf_op jit(solution)/shard_map/ppermute | solution.py:596
  82.6 8.3 %collective-permute-start.6 = (bf16[64,128]{1,0:T(8,128)(2,1)S(1)}, bf16[64,128]{1,0:T(8,128)(2,1)S(1)}, u32[]{:S(2)}, u32[]{:S(2)}) collective-permute-start(bf16[64,128]{1,0:T(8,128)(2,1)S(1)} %get-tuple-element.22), channel_id=1, source_target_pairs={{0,16},{1,17},{2,18},{3,19},{4,20},{5,21},{6,22},{7,23},{8,24},{9,... | collective-permute-start | bytes 49160 | tf_op jit(solution)/shard_map/ppermute | solution.py:597
  85.3 5.6 %copy-start.3 = (f32[192]{0:T(256)S(1)}, f32[192]{0:T(256)}, u32[]{:S(2)}) copy-start(f32[192]{0:T(256)} %param.23) | copy-start | bytes 2308

commit v5 on v4

--- a/solution.py
+++ b/solution.py
@@ -224,19 +224,19 @@
     prior_k = prior_ref[:, :OWN, :].reshape(16 * OWN, HD)
     scale = fold_scale()
 
-    def block(i, carry):
+    blocks = range(16 // PB)
+    scores = []
+    for i in blocks:
+        query = recv_ref[pl.ds(early + i * PB, PB), :OWN, :].reshape(PB * OWN, HD)
+        scores.append(scores_of(query, prior_k) * scale + penalty)
+    for i in blocks:
         rows = pl.ds(i * PB * OWN, PB * OWN)
-        query = recv_ref[pl.ds(early + i * PB, PB), :OWN, :].reshape(PB * OWN, HD)
-        before = scores_of(query, prior_k) * scale + penalty
         old = max_ref[rows, :]
-        top = jnp.maximum(old[:, :1], jnp.max(before, axis=1, keepdims=True))
-        before = jnp.exp2(before - top).astype(jnp.bfloat16)
+        top = jnp.maximum(old[:, :1], jnp.max(scores[i], axis=1, keepdims=True))
+        before = jnp.exp2(scores[i] - top).astype(jnp.bfloat16)
         mixed = jnp.dot(before, prior_v[...], preferred_element_type=jnp.float32)
         mixed += mix_ref[rows, :] * jnp.exp2(old - top)
         pack_result(mixed, packed_ref, i * PB, PB)
-        return carry
-
-    lax.fori_loop(0, 16 // PB, block, 0, unroll=True)
     scatter_halo(packed_ref, grid_ref, out_ref, place_ref[3], 0)
     copy = pltpu.make_async_copy(out_ref, out_hbm.at[pl.ds(8 * place_ref[2], 8)], sem)
     copy.start()
@@ -593,8 +593,8 @@
     back = lax.all_to_all(partial, AXES, 0, 0, tiled=True, axis_index_groups=half_groups(groups))
     own, own_sent, other_sent = sum_heads(noise_level, back, halo_noisy)
     across = lax.ppermute(other_sent, "tile", ACROSS)
+    before_own = lax.ppermute(own_sent, AXES, span_route(0))
     before_other = lax.ppermute(other_sent, AXES, span_route(2))
-    before_own = lax.ppermute(own_sent, AXES, span_route(0))
     clean = own + across.astype(jnp.float32)
     clean_latent = clean.reshape(2, 4, 8, 2, LAT)[:, 1:3, 1:7].transpose(3, 0, 1, 2, 4)
     clean_latent = clean_latent.reshape(noisy_latent.shape)

time: 96 us -> 95.8 us (level)
  no operation moved by 1% of the time
where the time goes in v5:
time: 95.8 us; the launch traced here: 95.2 us
  waiting for transfers between devices  37.4 us (39%)
  starting transfers between devices  33.6 us (35%)
  Pallas kernels  17.8 us (19%)
  local copies, waits for them, and re-layouts  4.65 us (5%)
  between operations  1.6 us (2%)
    all_to_all x1, starting transfers between devices, shards(): lax.all_to_all(sent, AXES, 0, 0, tiled=True, axis_index_groups=groups)  11.5 us
    all_to_all x1, waiting for transfers between devices, shards(): lax.all_to_all(partial, AXES, 0, 0, tiled=True, axis_index_groups=half_gr...  10.2 us
    all_to_all x1, waiting for transfers between devices, shards(): lax.all_to_all(sent, AXES, 0, 0, tiled=True, axis_index_groups=groups)  9.79 us
    ppermute x1, waiting for transfers between devices, shards(): prior = lax.ppermute(late_kv, AXES, prior_route(groups))  7.24 us
    ppermute x1, starting transfers between devices, shards(): before_other = lax.ppermute(other_sent, AXES, span_route(2))  6.9 us
    ppermute x2, waiting for transfers between devices, with_halo(): lax.ppermute(head, axis, [((i + 1) % count, i) for i in range(ends)])  6.77 us
    ppermute x2, starting transfers between devices, with_halo(): lax.ppermute(tail, axis, [(i, (i + 1) % count) for i in range(ends)])  4.99 us
    pallas_call x1, Pallas kernels, decode(): pl.pallas_call(decode_kernel, out_shape=pltpu.HBM((8, 8, 24, OC), bf16),...  4.53 us
  transfers between devices with their start and end apart: 10, of which 6 were waited for; matrix products, arithmetic and copies ran while one was open for 4% of the time, Pallas kernels for 7%

profile of v5, /device:TPU:16, one launch (start us, length us, event | category | flops | bytes accessed | tf_op | source)
XLA Modules:
  0.0 95.2 jit_solution(3517950602826890844)
XLA Ops:
  0.6 0.0 copy-start.5
  0.6 3.1 %shard_map.131 = bf16[32,120,128]{2,1,0:T(8,128)(2,1)} custom-call(bf16[1,4,6,2,4096]{4,3,2,1,0:T(2,128)(2,1)} %bitcast.30, bf16[1,4,6,2,4096]{4,3,2,1,0:T(2,128)(2,1)} %bitcast.31, bf16[1,4,6,2,4096]{4,3,2,1,0:T(2,128)(2,1)} %bitcast.32, bf16[64,4096]{1,0:T(8,128)(2,1)} %bitcast.29), custom_call_target="tpu_custom_call" | custom-call | tf_op jit(solution)/shard_map/pallas_call | solution.py:88
  3.7 0.0 copy-start.4
  3.8 11.5 %all-to-all-start = ((bf16[32,120,128]{2,1,0:T(8,128)(2,1)}), bf16[32,120,128]{2,1,0:T(8,128)(2,1)S(1)}, u32[]{:S(2)}, u32[]{:S(2)}) async-start(bf16[32,120,128]{2,1,0:T(8,128)(2,1)} %shard_map.131), calls=%async_computation | async-start | bytes 1966080 | tf_op jit(solution)/shard_map/all_to_all | solution.py:588
  15.2 0.0 copy-done.5
  15.2 3.7 %collective-permute-start = (f32[4,2,1,64]{3,1,2,0:T(2,128)S(1)}, f32[4,2,1,64]{3,1,2,0:T(2,128)S(1)}, u32[]{:S(2)}, u32[]{:S(2)}) collective-permute-start(f32[4,2,1,64]{3,1,2,0:T(2,128)S(1)} %get-tuple-element.30), channel_id=1, source_target_pairs={{0,4},{4,8},{8,12},{1,5},{5,9},{9,13},{2,6},{6,10},{10,14},{3,7},{... | collective-permute-start | bytes 6152 | tf_op jit(solution)/shard_map/ppermute | solution.py:550
  18.9 1.3 %collective-permute-start.1 = (f32[4,2,1,64]{3,1,2,0:T(2,128)S(1)}, f32[4,2,1,64]{3,1,2,0:T(2,128)S(1)}, u32[]{:S(2)}, u32[]{:S(2)}) collective-permute-start(f32[4,2,1,64]{3,1,2,0:T(2,128)S(1)} %get-tuple-element.31), channel_id=1, source_target_pairs={{4,0},{8,4},{12,8},{5,1},{9,5},{13,9},{6,2},{10,6},{14,10},{7,3},{... | collective-permute-start | bytes 6152 | tf_op jit(solution)/shard_map/ppermute | solution.py:552
  20.3 0.0 collective-permute-done
  20.3 4.1 %collective-permute-done.1 = f32[4,2,1,64]{3,1,2,0:T(2,128)S(1)} collective-permute-done((f32[4,2,1,64]{3,1,2,0:T(2,128)S(1)}, f32[4,2,1,64]{3,1,2,0:T(2,128)S(1)}, u32[]{:S(2)}, u32[]{:S(2)}) %collective-permute-start.1) | collective-permute-done | bytes 2080 | tf_op jit(solution)/shard_map/ppermute | solution.py:552
  24.5 1.3 %collective-permute-start.2 = (f32[4,1,8,64]{3,1,2,0:T(1,128)S(1)}, f32[4,1,8,64]{3,1,2,0:T(1,128)S(1)}, u32[]{:S(2)}, u32[]{:S(2)}) collective-permute-start(f32[4,1,8,64]{3,1,2,0:T(1,128)S(1)} %get-tuple-element.28), channel_id=1, source_target_pairs={{0,1},{1,2},{2,3},{4,5},{5,6},{6,7},{8,9},{9,10},{10,11},{12,13},{... | collective-permute-start | bytes 24584 | tf_op jit(solution)/shard_map/ppermute | solution.py:550
  25.8 1.3 %collective-permute-start.3 = (f32[4,1,8,64]{3,1,2,0:T(1,128)S(1)}, f32[4,1,8,64]{3,1,2,0:T(1,128)S(1)}, u32[]{:S(2)}, u32[]{:S(2)}) collective-permute-start(f32[4,1,8,64]{3,1,2,0:T(1,128)S(1)} %get-tuple-element.29), channel_id=1, source_target_pairs={{1,0},{2,1},{3,2},{5,4},{6,5},{7,6},{9,8},{10,9},{11,10},{13,12},{... | collective-permute-start | bytes 24584 | tf_op jit(solution)/shard_map/ppermute | solution.py:552
  27.1 0.1 pad_add_fusion.place_ref
  27.2 0.0 copy-done.4
  27.2 2.2 %copy.16.spatial_ref = bf16[3,3,384,192]{3,2,1,0:T(8,128)(2,1)} copy(bf16[3,3,384,192]{2,3,1,0:T(8,128)(2,1)S(1)} %copy-done.4) | data formatting | bytes 2654208 | tf_op jit(solution)/shard_map/optimization_barrier | solution.py:582
  29.4 1.5 %copy-done.1 = bf16[3,3,384,192]{3,2,1,0:T(8,128)(2,1)S(1)} copy-done((bf16[3,3,384,192]{3,2,1,0:T(8,128)(2,1)S(1)}, bf16[3,3,384,192]{3,2,1,0:T(8,128)(2,1)}, u32[]{:S(2)}) %copy-start.1) | copy-done | bytes 1327128
  30.9 1.0 %shard_map.132.rest_1_.window_hbm = bf16[1536,768]{1,0:T(8,128)(2,1)S(1)} custom-call(bf16[3,3,384,192]{3,2,1,0:T(8,128)(2,1)S(1)} %copy-done.1), custom_call_target="tpu_custom_call" | custom-call | flops 4194304 | bytes 4194304 | tf_op jit(solution)/shard_map/pallas_call | solution.py:387
  31.8 0.0 copy-start
  31.9 0.0 collective-permute-done.2
  31.9 2.6 %collective-permute-done.3 = f32[4,1,8,64]{3,1,2,0:T(1,128)S(1)} collective-permute-done((f32[4,1,8,64]{3,1,2,0:T(1,128)S(1)}, f32[4,1,8,64]{3,1,2,0:T(1,128)S(1)}, u32[]{:S(2)}, u32[]{:S(2)}) %collective-permute-start.3) | collective-permute-done | bytes 8224 | tf_op jit(solution)/shard_map/ppermute | solution.py:552
  34.5 0.1 pad_maximum_fusion
  34.5 0.1 copy.20
  34.6 0.1 reshape.23.rest_0_.noisy_ref
  34.7 9.8 %all-to-all-done.recv_ref = bf16[32,120,128]{2,1,0:T(8,128)(2,1)S(1)} async-done(((bf16[32,120,128]{2,1,0:T(8,128)(2,1)}), bf16[32,120,128]{2,1,0:T(8,128)(2,1)S(1)}, u32[]{:S(2)}, u32[]{:S(2)}) %all-to-all-start) | async-done | bytes 983072 | tf_op jit(solution)/shard_map/all_to_all | solution.py:588
  44.5 0.6 shard_map.133
  45.1 0.0 copy-done
  45.1 1.9 %collective-permute-start.4 = (bf16[16,72,128]{2,1,0:T(8,128)(2,1)S(1)}, bf16[16,72,128]{2,1,0:T(8,128)(2,1)S(1)}, u32[]{:S(2)}, u32[]{:S(2)}) collective-permute-start(bf16[16,72,128]{2,1,0:T(8,128)(2,1)S(1)} %shard_map.133), channel_id=1, source_target_pairs={{0,50},{1,51},{2,48},{3,49},{4,54},{5,55},{6,52},{7,53},{8,58},{9,... | collective-permute-start | bytes 884744 | tf_op jit(solution)/shard_map/ppermute | solution.py:590
  47.0 3.7 %shard_map.134 = (bf16[16,128,128]{2,1,0:T(8,128)(2,1)}, f32[768,128]{1,0:T(8,128)S(1)}, f32[768,128]{1,0:T(8,128)S(1)}) custom-call(s32[4]{0:T(128)S(1)} %pad_add_fusion.place_ref, bf16[32,120,128]{2,1,0:T(8,128)(2,1)S(1)} %all-to-all-done.recv_ref), custom_call_target="tpu_custom_call" | custom-call | flops 905969664 | bytes 4194304 | tf_op jit(solution)/shard_map/pallas_call | solution.py:200
  50.7 7.2 %collective-permute-done.4.prior_ref = bf16[16,72,128]{2,1,0:T(8,128)(2,1)S(1)} collective-permute-done((bf16[16,72,128]{2,1,0:T(8,128)(2,1)S(1)}, bf16[16,72,128]{2,1,0:T(8,128)(2,1)S(1)}, u32[]{:S(2)}, u32[]{:S(2)}) %collective-permute-start.4) | collective-permute-done | bytes 294944 | tf_op jit(solution)/shard_map/ppermute | solution.py:590
  58.0 2.7 %shard_map.135 = bf16[16,128,128]{2,1,0:T(8,128)(2,1)} custom-call(s32[4]{0:T(128)S(1)} %pad_add_fusion.place_ref, bf16[32,120,128]{2,1,0:T(8,128)(2,1)S(1)} %all-to-all-done.recv_ref, bf16[16,72,128]{2,1,0:T(8,128)(2,1)S(1)} %collective-permute-done.4.prior_ref, f32[768,128]{1,0:T(8,128)S(1)} %get-tuple-element.17.max_ref, ...), custom_call_target="tpu_custom_call", output_to_operand_aliasing={{}: (5, {})} | custom-call | tf_op jit(solution)/shard_map/pallas_call | solution.py:274
  60.6 0.0 copy-start.2
  60.6 3.7 %all-to-all-start.1 = ((bf16[16,128,128]{2,1,0:T(8,128)(2,1)}), bf16[16,128,128]{2,1,0:T(8,128)(2,1)S(1)}, u32[]{:S(2)}, u32[]{:S(2)}) async-start(bf16[16,128,128]{2,1,0:T(8,128)(2,1)} %shard_map.135), calls=%async_computation.1 | async-start | bytes 1048576 | tf_op jit(solution)/shard_map/all_to_all | solution.py:593
  65.0 10.2 %all-to-all-done.1.back_ref = bf16[16,128,128]{2,1,0:T(8,128)(2,1)S(1)} async-done(((bf16[16,128,128]{2,1,0:T(8,128)(2,1)}), bf16[16,128,128]{2,1,0:T(8,128)(2,1)S(1)}, u32[]{:S(2)}, u32[]{:S(2)}) %all-to-all-start.1) | async-done | bytes 524320 | tf_op jit(solution)/shard_map/all_to_all | solution.py:593
  75.2 0.1 shard_map.136
  75.3 0.1 collective-permute-start.5
  75.4 0.1 pad_add_fusion.1.place_ref
  75.4 0.0 copy-done.6
  75.5 0.0 copy-done.7
  75.5 6.9 %collective-permute-start.7 = (bf16[64,128]{1,0:T(8,128)(2,1)S(1)}, bf16[64,128]{1,0:T(8,128)(2,1)S(1)}, u32[]{:S(2)}, u32[]{:S(2)}) collective-permute-start(bf16[64,128]{1,0:T(8,128)(2,1)S(1)} %get-tuple-element.21), channel_id=1, source_target_pairs={{0,18},{1,19},{2,16},{3,17},{4,22},{5,23},{6,20},{7,21},{8,26},{9,... | collective-permute-start | bytes 49160 | tf_op jit(solution)/shard_map/ppermute | solution.py:597
  82.4 1.9 %collective-permute-start.6 = (bf16[64,128]{1,0:T(8,128)(2,1)S(1)}, bf16[64,128]{1,0:T(8,128)(2,1)S(1)}, u32[]{:S(2)}, u32[]{:S(2)}) collective-permute-start(bf16[64,128]{1,0:T(8,128)(2,1)S(1)} %get-tuple-element.22), channel_id=1, source_target_pairs={{0,16},{1,17},{2,18},{3,19},{4,20},{5,21},{6,22},{7,23},{8,24},{9,... | collective-permute-start | bytes 49160 | tf_op jit(solution)/shard_map/ppermute | solution.py:596
  84.3 0.0 collective-permute-done.5.other_ref
  84.3 0.1 reshape.24
  84.5 0.6 copy.18
  85.1 0.0 copy-done.2
  85.1 2.2 %shard_map.137 = (bf16[768,1536]{1,0:T(8,128)(2,1)S(1)}, bf16[1152,768]{1,0:T(8,128)(2,1)S(1)}, bf16[1536,768]{1,0:T(8,128)(2,1)S(1)}) custom-call(bf16[432,384]{1,0:T(8,128)(2,1)S(1)} %bitcast.23, bf16[1152,768]{1,0:T(8,128)(2,1)} %bitcast.27, bf16[1536,768]{1,0:T(8,128)(2,1)} %copy-done, f32[1,4,2,6,64]{4,3,2,1,0:T(8,128)S(1)} %bitcast.25), custom_call_target="tpu_custom_call" | custom-call | flops 4194304 | bytes 8388608 | tf_op jit(solution)/shard_map/pallas_call | solution.py:345
  87.3 3.4 %collective-permute-done.6.before_own_ref = bf16[64,128]{1,0:T(8,128)(2,1)S(1)} collective-permute-done((bf16[64,128]{1,0:T(8,128)(2,1)S(1)}, bf16[64,128]{1,0:T(8,128)(2,1)S(1)}, u32[]{:S(2)}, u32[]{:S(2)}) %collective-permute-start.6) | collective-permute-done | bytes 16416 | tf_op jit(solution)/shard_map/ppermute | solution.py:596
  90.7 0.0 collective-permute-done.7.before_other_ref
  90.7 0.0 copy-done.3
  90.7 4.5 %shard_map.138 = bf16[8,8,24,192]{3,2,1,0:T(8,128)(2,1)} custom-call(s32[3]{0:T(128)S(1)} %pad_add_fusion.1.place_ref, bf16[64,128]{1,0:T(8,128)(2,1)S(1)} %collective-permute-done.6.before_own_ref, bf16[64,128]{1,0:T(8,128)(2,1)S(1)} %collective-permute-done.7.before_other_ref, f32[64,128]{1,0:T(8,128)S(1)} %get-tuple-element.20.own_ref, ...), custom_call_target="tpu_custom_call" | custom-call | tf_op jit(solution)/shard_map/pallas_call | solution.py:521
  (12 shorter events, 0.1 us)
Async XLA Ops:
  0.6 14.6 %copy-start.5 = (f32[1,4,2,6,64]{4,2,3,1,0:T(2,128)S(1)}, f32[1,4,2,6,64]{4,2,3,1,0:T(2,128)}, u32[]{:S(2)}) copy-start(f32[1,4,2,6,64]{4,2,3,1,0:T(2,128)} %param.15) | copy-start | bytes 36868
  3.7 23.4 %copy-start.4 = (bf16[3,3,384,192]{2,3,1,0:T(8,128)(2,1)S(1)}, bf16[3,3,384,192]{2,3,1,0:T(8,128)(2,1)}, u32[]{:S(2)}) copy-start(bf16[3,3,384,192]{2,3,1,0:T(8,128)(2,1)} %param.22) | copy-start | bytes 3981316
  3.8 40.8 %all-to-all-start = ((bf16[32,120,128]{2,1,0:T(8,128)(2,1)}), bf16[32,120,128]{2,1,0:T(8,128)(2,1)S(1)}, u32[]{:S(2)}, u32[]{:S(2)}) async-start(bf16[32,120,128]{2,1,0:T(8,128)(2,1)} %shard_map.131), calls=%async_computation | async-start | bytes 1966080 | tf_op jit(solution)/shard_map/all_to_all | solution.py:588
  15.2 5.0 %collective-permute-start = (f32[4,2,1,64]{3,1,2,0:T(2,128)S(1)}, f32[4,2,1,64]{3,1,2,0:T(2,128)S(1)}, u32[]{:S(2)}, u32[]{:S(2)}) collective-permute-start(f32[4,2,1,64]{3,1,2,0:T(2,128)S(1)} %get-tuple-element.30), channel_id=1, source_target_pairs={{0,4},{4,8},{8,12},{1,5},{5,9},{9,13},{2,6},{6,10},{10,14},{3,7},{... | collective-permute-start | bytes 6152 | tf_op jit(solution)/shard_map/ppermute | solution.py:550
  18.9 5.5 %collective-permute-start.1 = (f32[4,2,1,64]{3,1,2,0:T(2,128)S(1)}, f32[4,2,1,64]{3,1,2,0:T(2,128)S(1)}, u32[]{:S(2)}, u32[]{:S(2)}) collective-permute-start(f32[4,2,1,64]{3,1,2,0:T(2,128)S(1)} %get-tuple-element.31), channel_id=1, source_target_pairs={{4,0},{8,4},{12,8},{5,1},{9,5},{13,9},{6,2},{10,6},{14,10},{7,3},{... | collective-permute-start | bytes 6152 | tf_op jit(solution)/shard_map/ppermute | solution.py:552
  24.5 7.4 %collective-permute-start.2 = (f32[4,1,8,64]{3,1,2,0:T(1,128)S(1)}, f32[4,1,8,64]{3,1,2,0:T(1,128)S(1)}, u32[]{:S(2)}, u32[]{:S(2)}) collective-permute-start(f32[4,1,8,64]{3,1,2,0:T(1,128)S(1)} %get-tuple-element.28), channel_id=1, source_target_pairs={{0,1},{1,2},{2,3},{4,5},{5,6},{6,7},{8,9},{9,10},{10,11},{12,13},{... | collective-permute-start | bytes 24584 | tf_op jit(solution)/shard_map/ppermute | solution.py:550
  25.8 8.7 %collective-permute-start.3 = (f32[4,1,8,64]{3,1,2,0:T(1,128)S(1)}, f32[4,1,8,64]{3,1,2,0:T(1,128)S(1)}, u32[]{:S(2)}, u32[]{:S(2)}) collective-permute-start(f32[4,1,8,64]{3,1,2,0:T(1,128)S(1)} %get-tuple-element.29), channel_id=1, source_target_pairs={{1,0},{2,1},{3,2},{5,4},{6,5},{7,6},{9,8},{10,9},{11,10},{13,12},{... | collective-permute-start | bytes 24584 | tf_op jit(solution)/shard_map/ppermute | solution.py:552
  29.4 1.5 %copy-start.1 = (bf16[3,3,384,192]{3,2,1,0:T(8,128)(2,1)S(1)}, bf16[3,3,384,192]{3,2,1,0:T(8,128)(2,1)}, u32[]{:S(2)}) copy-start(bf16[3,3,384,192]{3,2,1,0:T(8,128)(2,1)} %copy.16.spatial_ref) | copy-start | bytes 3981316
  31.8 13.2 %copy-start = (bf16[1536,768]{1,0:T(8,128)(2,1)}, bf16[1536,768]{1,0:T(8,128)(2,1)S(1)}, u32[]{:S(2)}) copy-start(bf16[1536,768]{1,0:T(8,128)(2,1)S(1)} %shard_map.132.rest_1_.window_hbm) | copy-start | bytes 7077892
  45.1 12.9 %collective-permute-start.4 = (bf16[16,72,128]{2,1,0:T(8,128)(2,1)S(1)}, bf16[16,72,128]{2,1,0:T(8,128)(2,1)S(1)}, u32[]{:S(2)}, u32[]{:S(2)}) collective-permute-start(bf16[16,72,128]{2,1,0:T(8,128)(2,1)S(1)} %shard_map.133), channel_id=1, source_target_pairs={{0,50},{1,51},{2,48},{3,49},{4,54},{5,55},{6,52},{7,53},{8,58},{9,... | collective-permute-start | bytes 884744 | tf_op jit(solution)/shard_map/ppermute | solution.py:590
  58.0 17.5 %copy-start.6 = (f32[768]{0:T(1024)S(1)}, f32[768]{0:T(1024)}, u32[]{:S(2)}) copy-start(f32[768]{0:T(1024)} %param.21) | copy-start | bytes 9220
  58.0 17.5 %copy-start.7 = (f32[384]{0:T(512)S(1)}, f32[384]{0:T(512)}, u32[]{:S(2)}) copy-start(f32[384]{0:T(512)} %param.19) | copy-start | bytes 4612
  60.6 24.5 %copy-start.2 = (bf16[3,3,3,16,384]{4,3,2,1,0:T(8,128)(2,1)S(1)}, bf16[3,3,3,16,384]{4,3,2,1,0:T(8,128)(2,1)}, u32[]{:S(2)}) copy-start(bf16[3,3,3,16,384]{4,3,2,1,0:T(8,128)(2,1)} %param.18) | copy-start | bytes 995332
  60.6 14.6 %all-to-all-start.1 = ((bf16[16,128,128]{2,1,0:T(8,128)(2,1)}), bf16[16,128,128]{2,1,0:T(8,128)(2,1)S(1)}, u32[]{:S(2)}, u32[]{:S(2)}) async-start(bf16[16,128,128]{2,1,0:T(8,128)(2,1)} %shard_map.135), calls=%async_computation.1 | async-start | bytes 1048576 | tf_op jit(solution)/shard_map/all_to_all | solution.py:593
  75.3 9.0 %collective-permute-start.5 = (bf16[64,128]{1,0:T(8,128)(2,1)S(1)}, bf16[64,128]{1,0:T(8,128)(2,1)S(1)}, u32[]{:S(2)}, u32[]{:S(2)}) collective-permute-start(bf16[64,128]{1,0:T(8,128)(2,1)S(1)} %get-tuple-element.21), channel_id=1, source_target_pairs={{0,2},{1,3},{2,0},{3,1},{4,6},{5,7},{6,4},{7,5},{8,10},{9,11},{10,... | collective-permute-start | bytes 49160 | tf_op jit(solution)/shard_map/ppermute | solution.py:595
  75.5 15.2 %collective-permute-start.7 = (bf16[64,128]{1,0:T(8,128)(2,1)S(1)}, bf16[64,128]{1,0:T(8,128)(2,1)S(1)}, u32[]{:S(2)}, u32[]{:S(2)}) collective-permute-start(bf16[64,128]{1,0:T(8,128)(2,1)S(1)} %get-tuple-element.21), channel_id=1, source_target_pairs={{0,18},{1,19},{2,16},{3,17},{4,22},{5,23},{6,20},{7,21},{8,26},{9,... | collective-permute-start | bytes 49160 | tf_op jit(solution)/shard_map/ppermute | solution.py:597
  82.4 8.3 %collective-permute-start.6 = (bf16[64,128]{1,0:T(8,128)(2,1)S(1)}, bf16[64,128]{1,0:T(8,128)(2,1)S(1)}, u32[]{:S(2)}, u32[]{:S(2)}) collective-permute-start(bf16[64,128]{1,0:T(8,128)(2,1)S(1)} %get-tuple-element.22), channel_id=1, source_target_pairs={{0,16},{1,17},{2,18},{3,19},{4,20},{5,21},{6,22},{7,23},{8,24},{9,... | collective-permute-start | bytes 49160 | tf_op jit(solution)/shard_map/ppermute | solution.py:596
  85.1 5.6 %copy-start.3 = (f32[192]{0:T(256)S(1)}, f32[192]{0:T(256)}, u32[]{:S(2)}) copy-start(f32[192]{0:T(256)} %param.23) | copy-start | bytes 2308

commit v6 on v4

--- a/solution.py
+++ b/solution.py
@@ -503,10 +503,9 @@
                 out_ref[frame, high, :, 128:] = (rest_ref[line, 8:32, :LAT] + rest_bias).astype(
                     jnp.bfloat16
                 )
-        frames = pl.ds(half * 4, 4)
-        copy = pltpu.make_async_copy(out_ref.at[frames], out_hbm.at[frames], sems.at[half])
-        copy.start()
-        copies.append(copy)
+            copy = pltpu.make_async_copy(out_ref.at[frame], out_hbm.at[frame], sems.at[frame])
+            copy.start()
+            copies.append(copy)
     for copy in copies:
         copy.wait()
 
@@ -533,7 +532,7 @@
             pltpu.VMEM((64, 40, 128), f32),
             pltpu.VMEM((64, 40, 128), f32),
             pltpu.VMEM((8, 8, 24, OC), bf16),
-            pltpu.SemaphoreType.DMA((2,)),
+            pltpu.SemaphoreType.DMA((8,)),
         ],
         compiler_params=pltpu.CompilerParams(vmem_limit_bytes=VMEM_BYTES),
     )(place, before_own, before_other, own, other, wide, inlet_bias, time_weight, time_bias, window, space_bias)

time: 96 us -> 96.1 us (level)
  no operation moved by 1% of the time
where the time goes in v6:
time: 96.1 us; the launch traced here: 95.5 us
  waiting for transfers between devices  37.4 us (39%)
  starting transfers between devices  33.6 us (35%)
  Pallas kernels  18.1 us (19%)
  local copies, waits for them, and re-layouts  4.65 us (5%)
  between operations  1.6 us (2%)
    all_to_all x1, starting transfers between devices, shards(): lax.all_to_all(sent, AXES, 0, 0, tiled=True, axis_index_groups=groups)  11.5 us
    all_to_all x1, waiting for transfers between devices, shards(): lax.all_to_all(partial, AXES, 0, 0, tiled=True, axis_index_groups=half_gr...  10.2 us
    all_to_all x1, waiting for transfers between devices, shards(): lax.all_to_all(sent, AXES, 0, 0, tiled=True, axis_index_groups=groups)  9.79 us
    ppermute x1, waiting for transfers between devices, shards(): prior = lax.ppermute(late_kv, AXES, prior_route(groups))  7.24 us
    ppermute x1, starting transfers between devices, shards(): before_other = lax.ppermute(other_sent, AXES, span_route(2))  6.9 us
    ppermute x2, waiting for transfers between devices, with_halo(): lax.ppermute(head, axis, [((i + 1) % count, i) for i in range(ends)])  6.77 us
    ppermute x2, starting transfers between devices, with_halo(): lax.ppermute(tail, axis, [(i, (i + 1) % count) for i in range(ends)])  4.99 us
    pallas_call x1, Pallas kernels, decode(): pl.pallas_call(decode_kernel, out_shape=pltpu.HBM((8, 8, 24, OC), bf16),...  4.54 us
  transfers between devices with their start and end apart: 10, of which 6 were waited for; matrix products, arithmetic and copies ran while one was open for 4% of the time, Pallas kernels for 7%

profile of v6, /device:TPU:16, one launch (start us, length us, event | category | flops | bytes accessed | tf_op | source)
XLA Modules:
  0.0 95.5 jit_solution(6127767953282227453)
XLA Ops:
  0.6 0.0 copy-start.5
  0.6 3.1 %shard_map.131 = bf16[32,120,128]{2,1,0:T(8,128)(2,1)} custom-call(bf16[1,4,6,2,4096]{4,3,2,1,0:T(2,128)(2,1)} %bitcast.30, bf16[1,4,6,2,4096]{4,3,2,1,0:T(2,128)(2,1)} %bitcast.31, bf16[1,4,6,2,4096]{4,3,2,1,0:T(2,128)(2,1)} %bitcast.32, bf16[64,4096]{1,0:T(8,128)(2,1)} %bitcast.29), custom_call_target="tpu_custom_call" | custom-call | tf_op jit(solution)/shard_map/pallas_call | solution.py:88
  3.7 0.0 copy-start.4
  3.8 11.5 %all-to-all-start = ((bf16[32,120,128]{2,1,0:T(8,128)(2,1)}), bf16[32,120,128]{2,1,0:T(8,128)(2,1)S(1)}, u32[]{:S(2)}, u32[]{:S(2)}) async-start(bf16[32,120,128]{2,1,0:T(8,128)(2,1)} %shard_map.131), calls=%async_computation | async-start | bytes 1966080 | tf_op jit(solution)/shard_map/all_to_all | solution.py:587
  15.2 0.0 copy-done.5
  15.2 3.7 %collective-permute-start = (f32[4,2,1,64]{3,1,2,0:T(2,128)S(1)}, f32[4,2,1,64]{3,1,2,0:T(2,128)S(1)}, u32[]{:S(2)}, u32[]{:S(2)}) collective-permute-start(f32[4,2,1,64]{3,1,2,0:T(2,128)S(1)} %get-tuple-element.30), channel_id=1, source_target_pairs={{0,4},{4,8},{8,12},{1,5},{5,9},{9,13},{2,6},{6,10},{10,14},{3,7},{... | collective-permute-start | bytes 6152 | tf_op jit(solution)/shard_map/ppermute | solution.py:549
  18.9 1.3 %collective-permute-start.1 = (f32[4,2,1,64]{3,1,2,0:T(2,128)S(1)}, f32[4,2,1,64]{3,1,2,0:T(2,128)S(1)}, u32[]{:S(2)}, u32[]{:S(2)}) collective-permute-start(f32[4,2,1,64]{3,1,2,0:T(2,128)S(1)} %get-tuple-element.31), channel_id=1, source_target_pairs={{4,0},{8,4},{12,8},{5,1},{9,5},{13,9},{6,2},{10,6},{14,10},{7,3},{... | collective-permute-start | bytes 6152 | tf_op jit(solution)/shard_map/ppermute | solution.py:551
  20.3 0.0 collective-permute-done
  20.3 4.1 %collective-permute-done.1 = f32[4,2,1,64]{3,1,2,0:T(2,128)S(1)} collective-permute-done((f32[4,2,1,64]{3,1,2,0:T(2,128)S(1)}, f32[4,2,1,64]{3,1,2,0:T(2,128)S(1)}, u32[]{:S(2)}, u32[]{:S(2)}) %collective-permute-start.1) | collective-permute-done | bytes 2080 | tf_op jit(solution)/shard_map/ppermute | solution.py:551
  24.5 1.3 %collective-permute-start.2 = (f32[4,1,8,64]{3,1,2,0:T(1,128)S(1)}, f32[4,1,8,64]{3,1,2,0:T(1,128)S(1)}, u32[]{:S(2)}, u32[]{:S(2)}) collective-permute-start(f32[4,1,8,64]{3,1,2,0:T(1,128)S(1)} %get-tuple-element.28), channel_id=1, source_target_pairs={{0,1},{1,2},{2,3},{4,5},{5,6},{6,7},{8,9},{9,10},{10,11},{12,13},{... | collective-permute-start | bytes 24584 | tf_op jit(solution)/shard_map/ppermute | solution.py:549
  25.8 1.3 %collective-permute-start.3 = (f32[4,1,8,64]{3,1,2,0:T(1,128)S(1)}, f32[4,1,8,64]{3,1,2,0:T(1,128)S(1)}, u32[]{:S(2)}, u32[]{:S(2)}) collective-permute-start(f32[4,1,8,64]{3,1,2,0:T(1,128)S(1)} %get-tuple-element.29), channel_id=1, source_target_pairs={{1,0},{2,1},{3,2},{5,4},{6,5},{7,6},{9,8},{10,9},{11,10},{13,12},{... | collective-permute-start | bytes 24584 | tf_op jit(solution)/shard_map/ppermute | solution.py:551
  27.1 0.1 pad_add_fusion.place_ref
  27.2 0.0 copy-done.4
  27.2 2.2 %copy.16.spatial_ref = bf16[3,3,384,192]{3,2,1,0:T(8,128)(2,1)} copy(bf16[3,3,384,192]{2,3,1,0:T(8,128)(2,1)S(1)} %copy-done.4) | data formatting | bytes 2654208 | tf_op jit(solution)/shard_map/optimization_barrier | solution.py:581
  29.4 1.5 %copy-done.1 = bf16[3,3,384,192]{3,2,1,0:T(8,128)(2,1)S(1)} copy-done((bf16[3,3,384,192]{3,2,1,0:T(8,128)(2,1)S(1)}, bf16[3,3,384,192]{3,2,1,0:T(8,128)(2,1)}, u32[]{:S(2)}) %copy-start.1) | copy-done | bytes 1327128
  30.9 1.0 %shard_map.132.rest_1_.window_hbm = bf16[1536,768]{1,0:T(8,128)(2,1)S(1)} custom-call(bf16[3,3,384,192]{3,2,1,0:T(8,128)(2,1)S(1)} %copy-done.1), custom_call_target="tpu_custom_call" | custom-call | flops 4194304 | bytes 4194304 | tf_op jit(solution)/shard_map/pallas_call | solution.py:387
  31.8 0.0 copy-start
  31.9 0.0 collective-permute-done.2
  31.9 2.6 %collective-permute-done.3 = f32[4,1,8,64]{3,1,2,0:T(1,128)S(1)} collective-permute-done((f32[4,1,8,64]{3,1,2,0:T(1,128)S(1)}, f32[4,1,8,64]{3,1,2,0:T(1,128)S(1)}, u32[]{:S(2)}, u32[]{:S(2)}) %collective-permute-start.3) | collective-permute-done | bytes 8224 | tf_op jit(solution)/shard_map/ppermute | solution.py:551
  34.5 0.1 pad_maximum_fusion
  34.5 0.1 copy.20
  34.6 0.1 reshape.23.rest_0_.noisy_ref
  34.7 9.8 %all-to-all-done.recv_ref = bf16[32,120,128]{2,1,0:T(8,128)(2,1)S(1)} async-done(((bf16[32,120,128]{2,1,0:T(8,128)(2,1)}), bf16[32,120,128]{2,1,0:T(8,128)(2,1)S(1)}, u32[]{:S(2)}, u32[]{:S(2)}) %all-to-all-start) | async-done | bytes 983072 | tf_op jit(solution)/shard_map/all_to_all | solution.py:587
  44.5 0.6 shard_map.133
  45.1 0.0 copy-done
  45.1 1.9 %collective-permute-start.4 = (bf16[16,72,128]{2,1,0:T(8,128)(2,1)S(1)}, bf16[16,72,128]{2,1,0:T(8,128)(2,1)S(1)}, u32[]{:S(2)}, u32[]{:S(2)}) collective-permute-start(bf16[16,72,128]{2,1,0:T(8,128)(2,1)S(1)} %shard_map.133), channel_id=1, source_target_pairs={{0,50},{1,51},{2,48},{3,49},{4,54},{5,55},{6,52},{7,53},{8,58},{9,... | collective-permute-start | bytes 884744 | tf_op jit(solution)/shard_map/ppermute | solution.py:589
  47.0 3.7 %shard_map.134 = (bf16[16,128,128]{2,1,0:T(8,128)(2,1)}, f32[768,128]{1,0:T(8,128)S(1)}, f32[768,128]{1,0:T(8,128)S(1)}) custom-call(s32[4]{0:T(128)S(1)} %pad_add_fusion.place_ref, bf16[32,120,128]{2,1,0:T(8,128)(2,1)S(1)} %all-to-all-done.recv_ref), custom_call_target="tpu_custom_call" | custom-call | flops 905969664 | bytes 4194304 | tf_op jit(solution)/shard_map/pallas_call | solution.py:200
  50.7 7.2 %collective-permute-done.4.prior_ref = bf16[16,72,128]{2,1,0:T(8,128)(2,1)S(1)} collective-permute-done((bf16[16,72,128]{2,1,0:T(8,128)(2,1)S(1)}, bf16[16,72,128]{2,1,0:T(8,128)(2,1)S(1)}, u32[]{:S(2)}, u32[]{:S(2)}) %collective-permute-start.4) | collective-permute-done | bytes 294944 | tf_op jit(solution)/shard_map/ppermute | solution.py:589
  58.0 2.9 %shard_map.135 = bf16[16,128,128]{2,1,0:T(8,128)(2,1)} custom-call(s32[4]{0:T(128)S(1)} %pad_add_fusion.place_ref, bf16[32,120,128]{2,1,0:T(8,128)(2,1)S(1)} %all-to-all-done.recv_ref, bf16[16,72,128]{2,1,0:T(8,128)(2,1)S(1)} %collective-permute-done.4.prior_ref, f32[768,128]{1,0:T(8,128)S(1)} %get-tuple-element.17.max_ref, ...), custom_call_target="tpu_custom_call", output_to_operand_aliasing={{}: (5, {})} | custom-call | tf_op jit(solution)/shard_map/pallas_call | solution.py:274
  60.9 0.0 copy-start.2
  60.9 3.7 %all-to-all-start.1 = ((bf16[16,128,128]{2,1,0:T(8,128)(2,1)}), bf16[16,128,128]{2,1,0:T(8,128)(2,1)S(1)}, u32[]{:S(2)}, u32[]{:S(2)}) async-start(bf16[16,128,128]{2,1,0:T(8,128)(2,1)} %shard_map.135), calls=%async_computation.1 | async-start | bytes 1048576 | tf_op jit(solution)/shard_map/all_to_all | solution.py:592
  65.3 10.2 %all-to-all-done.1.back_ref = bf16[16,128,128]{2,1,0:T(8,128)(2,1)S(1)} async-done(((bf16[16,128,128]{2,1,0:T(8,128)(2,1)}), bf16[16,128,128]{2,1,0:T(8,128)(2,1)S(1)}, u32[]{:S(2)}, u32[]{:S(2)}) %all-to-all-start.1) | async-done | bytes 524320 | tf_op jit(solution)/shard_map/all_to_all | solution.py:592
  75.4 0.1 shard_map.136
  75.5 0.1 collective-permute-start.5
  75.6 0.1 pad_add_fusion.1.place_ref
  75.7 0.0 copy-done.6
  75.7 0.0 copy-done.7
  75.7 6.9 %collective-permute-start.7 = (bf16[64,128]{1,0:T(8,128)(2,1)S(1)}, bf16[64,128]{1,0:T(8,128)(2,1)S(1)}, u32[]{:S(2)}, u32[]{:S(2)}) collective-permute-start(bf16[64,128]{1,0:T(8,128)(2,1)S(1)} %get-tuple-element.21), channel_id=1, source_target_pairs={{0,18},{1,19},{2,16},{3,17},{4,22},{5,23},{6,20},{7,21},{8,26},{9,... | collective-permute-start | bytes 49160 | tf_op jit(solution)/shard_map/ppermute | solution.py:595
  82.6 1.9 %collective-permute-start.6 = (bf16[64,128]{1,0:T(8,128)(2,1)S(1)}, bf16[64,128]{1,0:T(8,128)(2,1)S(1)}, u32[]{:S(2)}, u32[]{:S(2)}) collective-permute-start(bf16[64,128]{1,0:T(8,128)(2,1)S(1)} %get-tuple-element.22), channel_id=1, source_target_pairs={{0,16},{1,17},{2,18},{3,19},{4,20},{5,21},{6,22},{7,23},{8,24},{9,... | collective-permute-start | bytes 49160 | tf_op jit(solution)/shard_map/ppermute | solution.py:596
  84.6 0.0 collective-permute-done.5.other_ref
  84.6 0.1 reshape.24
  84.7 0.6 copy.18
  85.3 0.0 copy-done.2
  85.3 2.2 %shard_map.137 = (bf16[768,1536]{1,0:T(8,128)(2,1)S(1)}, bf16[1152,768]{1,0:T(8,128)(2,1)S(1)}, bf16[1536,768]{1,0:T(8,128)(2,1)S(1)}) custom-call(bf16[432,384]{1,0:T(8,128)(2,1)S(1)} %bitcast.23, bf16[1152,768]{1,0:T(8,128)(2,1)} %bitcast.27, bf16[1536,768]{1,0:T(8,128)(2,1)} %copy-done, f32[1,4,2,6,64]{4,3,2,1,0:T(8,128)S(1)} %bitcast.25), custom_call_target="tpu_custom_call" | custom-call | flops 4194304 | bytes 8388608 | tf_op jit(solution)/shard_map/pallas_call | solution.py:345
  87.6 3.4 %collective-permute-done.6.before_own_ref = bf16[64,128]{1,0:T(8,128)(2,1)S(1)} collective-permute-done((bf16[64,128]{1,0:T(8,128)(2,1)S(1)}, bf16[64,128]{1,0:T(8,128)(2,1)S(1)}, u32[]{:S(2)}, u32[]{:S(2)}) %collective-permute-start.6) | collective-permute-done | bytes 16416 | tf_op jit(solution)/shard_map/ppermute | solution.py:596
  91.0 0.0 collective-permute-done.7.before_other_ref
  91.0 0.0 copy-done.3
  91.0 4.5 %shard_map.138 = bf16[8,8,24,192]{3,2,1,0:T(8,128)(2,1)} custom-call(s32[3]{0:T(128)S(1)} %pad_add_fusion.1.place_ref, bf16[64,128]{1,0:T(8,128)(2,1)S(1)} %collective-permute-done.6.before_own_ref, bf16[64,128]{1,0:T(8,128)(2,1)S(1)} %collective-permute-done.7.before_other_ref, f32[64,128]{1,0:T(8,128)S(1)} %get-tuple-element.20.own_ref, ...), custom_call_target="tpu_custom_call" | custom-call | tf_op jit(solution)/shard_map/pallas_call | solution.py:520
  (12 shorter events, 0.1 us)
Async XLA Ops:
  0.6 14.6 %copy-start.5 = (f32[1,4,2,6,64]{4,2,3,1,0:T(2,128)S(1)}, f32[1,4,2,6,64]{4,2,3,1,0:T(2,128)}, u32[]{:S(2)}) copy-start(f32[1,4,2,6,64]{4,2,3,1,0:T(2,128)} %param.15) | copy-start | bytes 36868
  3.7 23.4 %copy-start.4 = (bf16[3,3,384,192]{2,3,1,0:T(8,128)(2,1)S(1)}, bf16[3,3,384,192]{2,3,1,0:T(8,128)(2,1)}, u32[]{:S(2)}) copy-start(bf16[3,3,384,192]{2,3,1,0:T(8,128)(2,1)} %param.22) | copy-start | bytes 3981316
  3.8 40.8 %all-to-all-start = ((bf16[32,120,128]{2,1,0:T(8,128)(2,1)}), bf16[32,120,128]{2,1,0:T(8,128)(2,1)S(1)}, u32[]{:S(2)}, u32[]{:S(2)}) async-start(bf16[32,120,128]{2,1,0:T(8,128)(2,1)} %shard_map.131), calls=%async_computation | async-start | bytes 1966080 | tf_op jit(solution)/shard_map/all_to_all | solution.py:587
  15.2 5.0 %collective-permute-start = (f32[4,2,1,64]{3,1,2,0:T(2,128)S(1)}, f32[4,2,1,64]{3,1,2,0:T(2,128)S(1)}, u32[]{:S(2)}, u32[]{:S(2)}) collective-permute-start(f32[4,2,1,64]{3,1,2,0:T(2,128)S(1)} %get-tuple-element.30), channel_id=1, source_target_pairs={{0,4},{4,8},{8,12},{1,5},{5,9},{9,13},{2,6},{6,10},{10,14},{3,7},{... | collective-permute-start | bytes 6152 | tf_op jit(solution)/shard_map/ppermute | solution.py:549
  18.9 5.5 %collective-permute-start.1 = (f32[4,2,1,64]{3,1,2,0:T(2,128)S(1)}, f32[4,2,1,64]{3,1,2,0:T(2,128)S(1)}, u32[]{:S(2)}, u32[]{:S(2)}) collective-permute-start(f32[4,2,1,64]{3,1,2,0:T(2,128)S(1)} %get-tuple-element.31), channel_id=1, source_target_pairs={{4,0},{8,4},{12,8},{5,1},{9,5},{13,9},{6,2},{10,6},{14,10},{7,3},{... | collective-permute-start | bytes 6152 | tf_op jit(solution)/shard_map/ppermute | solution.py:551
  24.5 7.4 %collective-permute-start.2 = (f32[4,1,8,64]{3,1,2,0:T(1,128)S(1)}, f32[4,1,8,64]{3,1,2,0:T(1,128)S(1)}, u32[]{:S(2)}, u32[]{:S(2)}) collective-permute-start(f32[4,1,8,64]{3,1,2,0:T(1,128)S(1)} %get-tuple-element.28), channel_id=1, source_target_pairs={{0,1},{1,2},{2,3},{4,5},{5,6},{6,7},{8,9},{9,10},{10,11},{12,13},{... | collective-permute-start | bytes 24584 | tf_op jit(solution)/shard_map/ppermute | solution.py:549
  25.8 8.7 %collective-permute-start.3 = (f32[4,1,8,64]{3,1,2,0:T(1,128)S(1)}, f32[4,1,8,64]{3,1,2,0:T(1,128)S(1)}, u32[]{:S(2)}, u32[]{:S(2)}) collective-permute-start(f32[4,1,8,64]{3,1,2,0:T(1,128)S(1)} %get-tuple-element.29), channel_id=1, source_target_pairs={{1,0},{2,1},{3,2},{5,4},{6,5},{7,6},{9,8},{10,9},{11,10},{13,12},{... | collective-permute-start | bytes 24584 | tf_op jit(solution)/shard_map/ppermute | solution.py:551
  29.4 1.5 %copy-start.1 = (bf16[3,3,384,192]{3,2,1,0:T(8,128)(2,1)S(1)}, bf16[3,3,384,192]{3,2,1,0:T(8,128)(2,1)}, u32[]{:S(2)}) copy-start(bf16[3,3,384,192]{3,2,1,0:T(8,128)(2,1)} %copy.16.spatial_ref) | copy-start | bytes 3981316
  31.8 13.2 %copy-start = (bf16[1536,768]{1,0:T(8,128)(2,1)}, bf16[1536,768]{1,0:T(8,128)(2,1)S(1)}, u32[]{:S(2)}) copy-start(bf16[1536,768]{1,0:T(8,128)(2,1)S(1)} %shard_map.132.rest_1_.window_hbm) | copy-start | bytes 7077892
  45.1 12.9 %collective-permute-start.4 = (bf16[16,72,128]{2,1,0:T(8,128)(2,1)S(1)}, bf16[16,72,128]{2,1,0:T(8,128)(2,1)S(1)}, u32[]{:S(2)}, u32[]{:S(2)}) collective-permute-start(bf16[16,72,128]{2,1,0:T(8,128)(2,1)S(1)} %shard_map.133), channel_id=1, source_target_pairs={{0,50},{1,51},{2,48},{3,49},{4,54},{5,55},{6,52},{7,53},{8,58},{9,... | collective-permute-start | bytes 884744 | tf_op jit(solution)/shard_map/ppermute | solution.py:589
  58.0 17.7 %copy-start.6 = (f32[768]{0:T(1024)S(1)}, f32[768]{0:T(1024)}, u32[]{:S(2)}) copy-start(f32[768]{0:T(1024)} %param.21) | copy-start | bytes 9220
  58.0 17.7 %copy-start.7 = (f32[384]{0:T(512)S(1)}, f32[384]{0:T(512)}, u32[]{:S(2)}) copy-start(f32[384]{0:T(512)} %param.19) | copy-start | bytes 4612
  60.9 24.5 %copy-start.2 = (bf16[3,3,3,16,384]{4,3,2,1,0:T(8,128)(2,1)S(1)}, bf16[3,3,3,16,384]{4,3,2,1,0:T(8,128)(2,1)}, u32[]{:S(2)}) copy-start(bf16[3,3,3,16,384]{4,3,2,1,0:T(8,128)(2,1)} %param.18) | copy-start | bytes 995332
  60.9 14.6 %all-to-all-start.1 = ((bf16[16,128,128]{2,1,0:T(8,128)(2,1)}), bf16[16,128,128]{2,1,0:T(8,128)(2,1)S(1)}, u32[]{:S(2)}, u32[]{:S(2)}) async-start(bf16[16,128,128]{2,1,0:T(8,128)(2,1)} %shard_map.135), calls=%async_computation.1 | async-start | bytes 1048576 | tf_op jit(solution)/shard_map/all_to_all | solution.py:592
  75.5 9.0 %collective-permute-start.5 = (bf16[64,128]{1,0:T(8,128)(2,1)S(1)}, bf16[64,128]{1,0:T(8,128)(2,1)S(1)}, u32[]{:S(2)}, u32[]{:S(2)}) collective-permute-start(bf16[64,128]{1,0:T(8,128)(2,1)S(1)} %get-tuple-element.21), channel_id=1, source_target_pairs={{0,2},{1,3},{2,0},{3,1},{4,6},{5,7},{6,4},{7,5},{8,10},{9,11},{10,... | collective-permute-start | bytes 49160 | tf_op jit(solution)/shard_map/ppermute | solution.py:594
  75.7 15.2 %collective-permute-start.7 = (bf16[64,128]{1,0:T(8,128)(2,1)S(1)}, bf16[64,128]{1,0:T(8,128)(2,1)S(1)}, u32[]{:S(2)}, u32[]{:S(2)}) collective-permute-start(bf16[64,128]{1,0:T(8,128)(2,1)S(1)} %get-tuple-element.21), channel_id=1, source_target_pairs={{0,18},{1,19},{2,16},{3,17},{4,22},{5,23},{6,20},{7,21},{8,26},{9,... | collective-permute-start | bytes 49160 | tf_op jit(solution)/shard_map/ppermute | solution.py:595
  82.6 8.3 %collective-permute-start.6 = (bf16[64,128]{1,0:T(8,128)(2,1)S(1)}, bf16[64,128]{1,0:T(8,128)(2,1)S(1)}, u32[]{:S(2)}, u32[]{:S(2)}) collective-permute-start(bf16[64,128]{1,0:T(8,128)(2,1)S(1)} %get-tuple-element.22), channel_id=1, source_target_pairs={{0,16},{1,17},{2,18},{3,19},{4,20},{5,21},{6,22},{7,23},{8,24},{9,... | collective-permute-start | bytes 49160 | tf_op jit(solution)/shard_map/ppermute | solution.py:596
  85.3 5.6 %copy-start.3 = (f32[192]{0:T(256)S(1)}, f32[192]{0:T(256)}, u32[]{:S(2)}) copy-start(f32[192]{0:T(256)} %param.23) | copy-start | bytes 2308
